TPU v7x, 32 devices: a whole 2x2x4 slice. The times are simulated.
32 devices in a mesh: groups: 2 (over x), fsdp: 8 (over z, y), tp: 2 (over core).
Axes of the slice: x: 2, y: 2, z: 4, core: 2. Of those that a mesh axis runs over, the one named last changes fastest.
Arguments:
- queries: bfloat16 [64, 4, 128, 128], P(('groups', 'fsdp'), None, 'tp'), parts along dimension 0, may hold values from -128 to 128
- cache_keys: bfloat16 [64, 512, 8, 128], P(('groups', 'fsdp'), None, 'tp'), parts along dimension 0, may hold values from -6 to 6
- cache_values: bfloat16 [64, 512, 8, 128], P(('groups', 'fsdp'), None, 'tp'), parts along dimension 0, may hold values from -6 to 6
- new_keys: bfloat16 [64, 4, 8, 128], P(('groups', 'fsdp'), None, 'tp'), parts along dimension 0, may hold values from -12 to 12
- new_values: bfloat16 [64, 4, 8, 128], P(('groups', 'fsdp'), None, 'tp'), parts along dimension 0, may hold values from -6 to 6
- cache_lengths: int32 [64], P(('groups', 'fsdp')), parts along dimension 0, may hold values from 1 to 512, as said below
- base_weight: bfloat16 [16384, 16384], P('tp', 'fsdp'), may hold values from -0.046875 to 0.046875
- factor_in: bfloat16 [32768, 128], P(('groups', 'fsdp'), 'tp'), parts along dimension 0, may hold values from -0.046875 to 0.046875
- adapter_output_factor: bfloat16 [256, 16384], P(('groups', 'tp'), 'fsdp'), parts along dimension 0, may hold values from -0.5 to 0.5
Outputs:
- projected: bfloat16 [64, 4, 16384], P(('groups', 'fsdp'), None, 'tp'), parts along dimension 0
There are 2 independent parts, one for each index of `groups`. A program takes and returns all parts, laid end to end along the dimension named above; an argument that names none is the same for every part. Nothing has to cross between parts.
Inputs may be any that keep to these rules, and one draw needn't show every extreme that they name: The first cache_lengths[r] slots of sequence r are valid; some sequence has all 512.
All inputs are finite; a program needn't handle non-finite values.
Results may differ from a plain program's by a relative error of at most 0.0059.
Values may be sent and summed in bfloat16 or wider, within the bound.
No kernel may reach another device: no remote copies, remote signals or barrier semaphores. Data moves between devices by JAX's collectives and lax.ppermute only.
A program may use at most 128 MiB of HBM per device.

v0:
```python
import math

import jax
import jax.numpy as jnp
from jax import lax
from jax.sharding import PartitionSpec as P

adapter_scale = 2.0


def attend(
    queries, cache_keys, cache_values, new_keys, new_values, cache_lengths, start_step, stop_step
):
    row_count, step_count, head_count, head_width = queries.shape
    key_heads = cache_keys.shape[2]
    slot_count = cache_keys.shape[1]
    taken = stop_step - start_step
    query_now = queries.reshape(row_count, taken, key_heads, head_count // key_heads, head_width)
    score_scale = 1.0 / math.sqrt(head_width)
    old_scores = (
        jnp.einsum("rsgqd,rlgd->rgsql", query_now, cache_keys, preferred_element_type=jnp.float32)
        * score_scale
    )
    visible = jnp.arange(slot_count, dtype=jnp.int32)[None, :] < cache_lengths[:, None]
    old_scores = jnp.where(visible[:, None, None, None, :], old_scores, -jnp.inf)
    new_scores = (
        jnp.einsum("rsgqd,rtgd->rgsqt", query_now, new_keys, preferred_element_type=jnp.float32)
        * score_scale
    )
    causal = jnp.arange(stop_step)[None, :] <= (start_step + jnp.arange(taken))[:, None]
    new_scores = jnp.where(causal[None, None, :, None, :], new_scores, -jnp.inf)
    highest = jnp.maximum(old_scores.max(-1), new_scores.max(-1))
    old_weights = jnp.exp(old_scores - highest[..., None])
    new_weights = jnp.exp(new_scores - highest[..., None])
    totals = old_weights.sum(-1) + new_weights.sum(-1)
    weighted = jnp.einsum(
        "rgsql,rlgd->rsgqd",
        old_weights.astype(jnp.bfloat16),
        cache_values,
        preferred_element_type=jnp.float32,
    )
    weighted = weighted + jnp.einsum(
        "rgsqt,rtgd->rsgqd",
        new_weights.astype(jnp.bfloat16),
        new_values,
        preferred_element_type=jnp.float32,
    )
    attended = weighted / jnp.transpose(totals, (0, 2, 1, 3))[..., None]
    return attended.astype(jnp.bfloat16).reshape(row_count * taken, head_count * head_width)


def shards(
    queries,
    cache_keys,
    cache_values,
    new_keys,
    new_values,
    cache_lengths,
    base_weight,
    factor_in,
    adapter_output_factor,
):
    adapter_column_count = lax.all_gather(adapter_output_factor, "tp", axis=0, tiled=True)
    rank_all = lax.all_gather(factor_in, "tp", axis=1, tiled=True)
    every_row = lax.all_gather(rank_all, "fsdp", axis=0, tiled=True)
    half_size = base_weight.shape[0]
    midpoint_rows = lax.dynamic_slice_in_dim(
        every_row, lax.axis_index("tp") * half_size, half_size, 0
    )
    combined_weight = (
        base_weight
        + adapter_scale
        * jnp.dot(midpoint_rows, adapter_column_count, preferred_element_type=jnp.float32)
    ).astype(jnp.bfloat16)
    step_count = queries.shape[1]
    local_rows = attend(
        queries, cache_keys, cache_values, new_keys, new_values, cache_lengths, 0, step_count
    )
    partial_value = jnp.dot(
        lax.all_gather(local_rows, "fsdp", axis=0, tiled=True),
        combined_weight,
        preferred_element_type=jnp.float32,
    )
    spread = lax.all_to_all(partial_value, "fsdp", split_axis=0, concat_axis=1, tiled=True)
    summed = lax.psum_scatter(spread, "tp", scatter_dimension=1, tiled=True)
    return summed.astype(jnp.bfloat16).reshape(cache_lengths.shape[0], step_count, -1)


def solution(mesh):
    return jax.shard_map(
        shards,
        mesh=mesh,
        in_specs=(
            P(("groups", "fsdp"), None, "tp", None),
            P(("groups", "fsdp"), None, "tp", None),
            P(("groups", "fsdp"), None, "tp", None),
            P(("groups", "fsdp"), None, "tp", None),
            P(("groups", "fsdp"), None, "tp", None),
            P(("groups", "fsdp")),
            P("tp", "fsdp"),
            P(("groups", "fsdp"), "tp"),
            P(("groups", "tp"), "fsdp"),
        ),
        out_specs=P(("groups", "fsdp"), None, "tp"),
        check_vma=False,
    )
```

profile of v0, /device:TPU:1, one launch (start us, length us, event | category | flops | bytes accessed | tf_op | source)
XLA Modules:
  0.0 204.9 jit_solution(2427732599482783222)
XLA Ops:
  6.5 0.0 copy-start
  6.5 0.0 all-gather.3.cloned.1.call-start
  6.5 0.9 iota_compare_fusion
  7.4 1.7 fusion.42
  9.1 0.0 copy-done
  9.1 1.9 fusion.7
  11.0 0.0 copy-start.3
  11.1 0.0 copy-start.4
  11.1 0.1 fusion.30
  11.2 0.6 fusion.8
  11.9 0.0 copy-done.3
  11.9 0.3 fusion.32
  12.2 0.5 copy-done.4
  12.7 0.0 copy-start.1
  12.7 1.0 fusion.19
  13.6 0.0 copy-start.2
  13.7 0.8 reshape.48
  14.5 0.0 all-gather.3.cloned.1.call-update
  14.5 0.0 all-gather.5.cloned.1.call-start
  14.5 0.0 copy-done.1
  14.6 2.3 %all_gather.13 = bf16[2048,128]{0,1:T(8,128)(2,1)} all-gather(bf16[2048,64]{0,1:T(8,128)(2,1)S(1)} %copy-done.1), channel_id=1, replica_groups=mesh['groups'=2,'fsdp'=8,'tp'=2] {'tp'}, dimensions={1}, use_global_device_ids=true | all-gather | bytes 786432 | tf_op jit(solution)/shard_map/all_gather | solution.py:64
  16.9 0.0 all-gather.5.cloned.1.call-update
  16.9 0.0 reduce-scatter.2.cloned.1.call-start
  17.0 0.0 copy-done.2
  17.0 2.3 %all_gather.15 = bf16[128,2048]{1,0:T(8,128)(2,1)} all-gather(bf16[64,2048]{1,0:T(8,128)(2,1)S(1)} %copy-done.2), channel_id=1, replica_groups=mesh['groups'=2,'fsdp'=8,'tp'=2] {'tp'}, dimensions={0}, use_global_device_ids=true | all-gather | bytes 786432 | tf_op jit(solution)/shard_map/all_gather | solution.py:63
  19.3 45.6 %all-gather.3.cloned.1.call-done = bf16[128,8192]{1,0:T(8,128)(2,1)} async-done(((bf16[16,8192]{1,0:T(8,128)(2,1)}), bf16[128,8192]{1,0:T(8,128)(2,1)}) %all-gather.3.cloned.1.call-update) | async-done | bytes 2097168 | tf_op jit(solution)/shard_map/all_gather | solution.py:80
  64.9 74.0 %all-gather.5.cloned.1.call-done = bf16[16384,128]{0,1:T(8,128)(2,1)} async-done(((bf16[2048,128]{0,1:T(8,128)(2,1)}), bf16[16384,128]{0,1:T(8,128)(2,1)}) %all-gather.5.cloned.1.call-update) | async-done | bytes 4194320 | tf_op jit(solution)/shard_map/all_gather | solution.py:65
  138.9 18.6 %fusion = f32[128,2048]{1,0:T(8,128)S(1)} fusion(bf16[128,8192]{1,0:T(8,128)(2,1)} %all-gather.3.cloned.1.call-done, bf16[8192,2048]{1,0:T(8,128)(2,1)} %param.15, bf16[128,2048]{1,0:T(8,128)(2,1)} %all_gather.15, bf16[16384,128]{0,1:T(8,128)(2,1)} %all-gather.5.cloned.1.call-done, s32[]{:T(128)S(6)} %select_n.13), kind=kOutput, calls=%fused_computation.1 | convolution fusion | flops 8657043456 | bytes 39321604 | tf_op jit(solution)/shard_map/dot_general | solution.py:79
  157.6 28.5 %all_to_all.19 = f32[8,16,2048]{2,1,0:T(8,128)S(1)} all-to-all(f32[8,16,2048]{2,1,0:T(8,128)S(1)} %bitcast.24), channel_id=1, replica_groups=mesh['groups'=2,'fsdp'=8,'tp'=2] {'fsdp'}, dimensions={0} | all-to-all | bytes 2097152 | tf_op jit(solution)/shard_map/all_to_all | solution.py:84
  186.1 1.1 copy.44
  187.2 0.0 reduce-scatter.2.cloned.1.call-update
  187.2 9.3 %reduce-scatter.2.cloned.1.call-done = f32[16,8192]{1,0:T(8,128)} async-done(((f32[16,16384]{1,0:T(8,128)}), f32[16,8192]{1,0:T(8,128)}) %reduce-scatter.2.cloned.1.call-update) | async-done | bytes 524304 | tf_op jit(solution)/shard_map/reduce_scatter | solution.py:85
  196.5 1.1 convert_element_type.23
  197.6 0.8 reshape.49
  (4 shorter events, 0.1 us)
Async XLA Ops:
  6.5 2.6 %copy-start = (bf16[4,512,4,128]{3,2,1,0:T(4,128)(2,1)S(1)}, bf16[4,512,4,128]{3,2,1,0:T(4,128)(2,1)}, u32[]{:S(2)}) copy-start(bf16[4,512,4,128]{3,2,1,0:T(4,128)(2,1)} %param.10) | copy-start | bytes 6291460
  6.5 58.4 %all-gather.3.cloned.1.call-start = ((), (), s32[]{:S(2)}) async-start(), calls=%async_computation.2 | async-start | bytes 2359296 | tf_op jit(solution)/shard_map/all_gather | solution.py:80
  11.0 0.8 copy-start.3
  11.1 1.6 copy-start.4
  12.7 1.9 copy-start.1
  13.6 3.3 %copy-start.2 = (bf16[64,2048]{1,0:T(8,128)(2,1)S(1)}, bf16[64,2048]{1,0:T(8,128)(2,1)}, u32[]{:S(2)}) copy-start(bf16[64,2048]{1,0:T(8,128)(2,1)} %param.17) | copy-start | bytes 786436
  14.5 124.4 %all-gather.5.cloned.1.call-start = ((), (), s32[]{:S(2)}) async-start(), calls=%async_computation.3 | async-start | bytes 4718592 | tf_op jit(solution)/shard_map/all_gather | solution.py:65
  16.9 179.6 %reduce-scatter.2.cloned.1.call-start = ((), (), s32[]{:S(2)}) async-start(), calls=%async_computation.4 | async-start | bytes 1572864 | tf_op jit(solution)/shard_map/reduce_scatter | solution.py:85
Sparse Core Ops, SparseCore 0:
  14.6 50.2 all-gather.2
  67.1 71.7 all-gather.4
  187.3 9.1 reduce-scatter.1
where the time goes:
time: 205 us
  waiting for transfers between devices  129 us (63%)
  blocking collectives  33.1 us (16%)
  matrix products  23.5 us (11%)
  between operations  13.2 us (6%)
  local copies, waits for them, and re-layouts  3.21 us (2%)
  other arithmetic  2.76 us (1%)
    all_gather x1, waiting for transfers between devices, shards(): every_row = lax.all_gather(rank_all, 'fsdp', axis=0, tiled=True)  74 us
    all_gather x1, waiting for transfers between devices, shards(): lax.all_gather(local_rows, 'fsdp', axis=0, tiled=True)  45.6 us
    all_to_all x1, blocking collectives, shards(): lax.all_to_all(partial_value, 'fsdp', split_axis=0, concat_axis=1, tiled=...  28.5 us
    dot_general x1, matrix products, shards(): jnp.dot(lax.all_gather(local_rows, 'fsdp', axis=0, tiled=True), combined_...  18.6 us
    reduce_scatter x1, waiting for transfers between devices, shards(): summed = lax.psum_scatter(spread, 'tp', scatter_dimension=1, tiled=True)  9.3 us
  transfers between devices with their start and end apart: 3, of which 3 were waited for; matrix products, arithmetic and copies ran while one was open for 0% of the time, Pallas kernels for 0%

commit v1 on v0

v1 whole, which is shorter than its diff:
```python
import functools
import math

import jax
import jax.numpy as jnp
from jax import lax
from jax.experimental import pallas as pl
from jax.experimental.pallas import tpu as pltpu
from jax.sharding import PartitionSpec as P

adapter_scale = 2.0
chunk_count = 2


def attend(queries, cache_keys, cache_values, new_keys, new_values, cache_lengths):
    row_count, step_count, head_count, head_width = queries.shape
    key_heads = cache_keys.shape[2]
    slot_count = cache_keys.shape[1]
    query_now = queries.reshape(
        row_count, step_count, key_heads, head_count // key_heads, head_width
    )
    score_scale = 1.0 / math.sqrt(head_width)
    old_scores = (
        jnp.einsum("rsgqd,rlgd->rgsql", query_now, cache_keys, preferred_element_type=jnp.float32)
        * score_scale
    )
    visible = jnp.arange(slot_count, dtype=jnp.int32)[None, :] < cache_lengths[:, None]
    old_scores = jnp.where(visible[:, None, None, None, :], old_scores, -jnp.inf)
    new_scores = (
        jnp.einsum("rsgqd,rtgd->rgsqt", query_now, new_keys, preferred_element_type=jnp.float32)
        * score_scale
    )
    steps = jnp.arange(step_count)
    causal = steps[None, :] <= steps[:, None]
    new_scores = jnp.where(causal[None, None, :, None, :], new_scores, -jnp.inf)
    highest = jnp.maximum(old_scores.max(-1), new_scores.max(-1))
    old_weights = jnp.exp(old_scores - highest[..., None])
    new_weights = jnp.exp(new_scores - highest[..., None])
    totals = old_weights.sum(-1) + new_weights.sum(-1)
    weighted = jnp.einsum(
        "rgsql,rlgd->rsgqd",
        old_weights.astype(jnp.bfloat16),
        cache_values,
        preferred_element_type=jnp.float32,
    )
    weighted = weighted + jnp.einsum(
        "rgsqt,rtgd->rsgqd",
        new_weights.astype(jnp.bfloat16),
        new_values,
        preferred_element_type=jnp.float32,
    )
    attended = weighted / jnp.transpose(totals, (0, 2, 1, 3))[..., None]
    return attended.astype(jnp.bfloat16).reshape(row_count * step_count, head_count * head_width)


def ring_order(count):
    inner = max(d for d in range(1, count + 1) if count % d == 0 and d * d <= count)
    outer = count // inner
    if inner == 1:
        return list(range(count))
    order = [z * inner for z in range(outer)]
    for turn, z in enumerate(reversed(range(outer))):
        columns = list(range(1, inner))
        if turn % 2:
            columns.reverse()
        order += [z * inner + c for c in columns]
    return order


def ring_gather(block, order):
    count = len(order)
    up = [(order[i], order[(i + 1) % count]) for i in range(count)]
    down = [(b, a) for a, b in up]
    blocks = {0: block}
    rising = falling = block
    for step in range(1, count // 2):
        rising = lax.ppermute(rising, "fsdp", up)
        falling = lax.ppermute(falling, "fsdp", down)
        blocks[count - step] = rising
        blocks[step] = falling
    half = block.shape[1] // 2
    far_left = lax.ppermute(rising[:, :half], "fsdp", up)
    far_right = lax.ppermute(falling[:, half:], "fsdp", down)
    near = [blocks[i] for i in range(count) if i != count // 2]
    return near, (far_left, far_right)


def project_kernel(count, per_tile, with_previous, *refs):
    places, flags = refs[:2]
    near = refs[2 : count + 1]
    far_left, far_right, weight, own_in, other_in = refs[count + 1 : count + 6]
    rest = refs[count + 6 :]
    if with_previous:
        previous, previous_rank = rest[:2]
        rest = rest[2:]
    partial, ranked, attended, factor = rest
    step = pl.program_id(0)
    half = far_left.shape[1]
    block_rows = far_left.shape[0]
    rank_half, own_width = own_in.shape

    @pl.when(step == 0)
    def _():
        for place, ref in enumerate(near):
            place = place if place < count // 2 else place + 1
            attended[places[place]] = ref[...]
        far = places[count // 2]
        attended[far, :, :half] = far_left[...]
        attended[far, :, half:] = far_right[...]
        if with_previous:
            partial[...] = previous[...]
            ranked[...] = previous_rank[...]
        else:
            partial[...] = jnp.zeros_like(partial)
            ranked[...] = jnp.zeros_like(ranked)

        @pl.when(flags[0] == 1)
        def _():
            core = flags[2]
            factor[pl.ds(pl.multiple_of(core * rank_half, rank_half), rank_half), :] = own_in[...]
            factor[pl.ds(pl.multiple_of((1 - core) * rank_half, rank_half), rank_half), :] = (
                other_in[...]
            )
            columns = pl.ds(pl.multiple_of(flags[1], 128), own_width)
            rows = attended[:, :, columns].reshape(count * block_rows, own_width)
            ranked[...] += lax.dot_general(
                rows, factor[...], (((1,), (1,)), ((), ())), preferred_element_type=jnp.float32
            )

    columns = pl.ds(pl.multiple_of(step * per_tile, per_tile), per_tile)
    rows = attended[:, :, columns].reshape(count * block_rows, per_tile)
    partial[...] += jnp.dot(rows, weight[...], preferred_element_type=jnp.float32)


def project(chunk, places, flags, near, far, base_weight, own_in, other_in, previous):
    count = len(near) + 1
    block_rows, width = near[0].shape
    columns = base_weight.shape[1]
    per_tile = min(width, 1024)
    tiles = width // per_tile
    rows = count * block_rows
    rank = 2 * own_in.shape[0]

    def whole(shape):
        return pl.BlockSpec(shape, lambda *_: (0,) * len(shape))

    operands = [*near, *far, base_weight, own_in, other_in]
    specs = [whole(x.shape) for x in operands]
    specs[len(near) + 2] = pl.BlockSpec(
        (per_tile, columns), lambda k, *_: (chunk * tiles + k, 0)
    )
    if previous is not None:
        operands += list(previous)
        specs += [whole(x.shape) for x in previous]
    return pl.pallas_call(
        functools.partial(project_kernel, count, per_tile, previous is not None),
        grid_spec=pltpu.PrefetchScalarGridSpec(
            num_scalar_prefetch=2,
            grid=(tiles,),
            in_specs=specs,
            out_specs=[whole((rows, columns)), whole((rows, rank))],
            scratch_shapes=[
                pltpu.VMEM((count, block_rows, width), jnp.bfloat16),
                pltpu.VMEM((rank, own_in.shape[1]), jnp.bfloat16),
            ],
        ),
        out_shape=[
            jax.ShapeDtypeStruct((rows, columns), jnp.float32),
            jax.ShapeDtypeStruct((rows, rank), jnp.float32),
        ],
        compiler_params=pltpu.CompilerParams(vmem_limit_bytes=40 * 1024 * 1024),
        cost_estimate=pl.CostEstimate(
            flops=4 * rows * width * columns,
            bytes_accessed=2 * width * columns,
            transcendentals=0,
        ),
        name=f"project_{chunk}",
    )(places, flags, *operands)


def adapter_kernel(flags, partial, ranked, own_out, other_out, keep, send, factor):
    core, kept = flags[2], flags[3]
    rank_half = own_out.shape[0]
    rank = 2 * rank_half
    for part in range(2):
        base = part * rank
        factor[pl.ds(pl.multiple_of(base + core * rank_half, rank_half), rank_half), :] = own_out[...]
        factor[pl.ds(pl.multiple_of(base + (1 - core) * rank_half, rank_half), rank_half), :] = (
            other_out[...]
        )
    scaled = adapter_scale * ranked[...]
    high = scaled.astype(jnp.bfloat16)
    low = (scaled - high.astype(jnp.float32)).astype(jnp.bfloat16)
    added = jnp.dot(
        jnp.concatenate([high, low], axis=1), factor[...], preferred_element_type=jnp.float32
    )
    total = partial[...] + added
    rows = keep.shape[0]
    first, second = total[:rows], total[rows:]
    keep[...] = jnp.where(kept == 0, first, second)
    send[...] = jnp.where(kept == 0, second, first)


def add_adapter(flags, partial, ranked, own_out, other_out):
    rows, columns = partial.shape
    half = jax.ShapeDtypeStruct((rows // 2, columns), jnp.float32)
    vmem = pl.BlockSpec(memory_space=pltpu.VMEM)
    return pl.pallas_call(
        adapter_kernel,
        in_specs=[pl.BlockSpec(memory_space=pltpu.SMEM)] + [vmem] * 4,
        out_specs=[vmem] * 2,
        out_shape=[half, half],
        scratch_shapes=[pltpu.VMEM((4 * own_out.shape[0], columns), jnp.bfloat16)],
        compiler_params=pltpu.CompilerParams(vmem_limit_bytes=40 * 1024 * 1024),
        name="add_adapter",
    )(flags, partial, ranked, own_out, other_out)


def round_kernel(flags, keep, received, *outs):
    mine = flags[4]
    for offset, out in enumerate(outs):
        total = keep[mine ^ offset] + received[mine ^ offset]
        out[...] = total.astype(jnp.bfloat16).reshape(out.shape)


def round_and_split(flags, keep, received, row_count, step_count):
    rows, columns = keep.shape
    block = row_count * step_count
    pieces = rows // block
    vmem = pl.BlockSpec(memory_space=pltpu.VMEM)
    return pl.pallas_call(
        round_kernel,
        in_specs=[pl.BlockSpec(memory_space=pltpu.SMEM)] + [vmem] * 2,
        out_specs=[vmem] * pieces,
        out_shape=[jax.ShapeDtypeStruct((row_count, step_count, columns), jnp.bfloat16)] * pieces,
        compiler_params=pltpu.CompilerParams(vmem_limit_bytes=40 * 1024 * 1024),
        name="round_and_split",
    )(flags, keep.reshape(pieces, block, columns), received.reshape(pieces, block, columns))


def place_kernel(flags, *refs):
    out = refs[-1]
    mine = flags[4]
    for offset, ref in enumerate(refs[:-1]):
        width = ref.shape[2]
        out[:, :, pl.ds(pl.multiple_of((mine ^ offset) * width, width), width)] = ref[...]


def place(flags, pieces):
    row_count, step_count, width = pieces[0].shape
    vmem = pl.BlockSpec(memory_space=pltpu.VMEM)
    return pl.pallas_call(
        place_kernel,
        in_specs=[pl.BlockSpec(memory_space=pltpu.SMEM)] + [vmem] * len(pieces),
        out_specs=vmem,
        out_shape=jax.ShapeDtypeStruct(
            (row_count, step_count, width * len(pieces)), jnp.bfloat16
        ),
        name="place",
    )(flags, *pieces)


def shards(
    count,
    queries,
    cache_keys,
    cache_values,
    new_keys,
    new_values,
    cache_lengths,
    base_weight,
    factor_in,
    adapter_output_factor,
):
    order = ring_order(count)
    position = {f: i for i, f in enumerate(order)}
    half_count = count // 2
    both = ("fsdp", "tp")
    chip = lax.axis_index("fsdp").astype(jnp.int32)
    core = lax.axis_index("tp").astype(jnp.int32)
    side = chip // half_count
    mine = chip % half_count
    table = jnp.array(
        [[order[(position[f] + i) % count] for i in range(count)] for f in range(count)], jnp.int32
    )
    places = lax.dynamic_index_in_dim(table, chip, 0, keepdims=False)
    row_count, step_count = queries.shape[:2]

    factors = jnp.concatenate([factor_in.T, adapter_output_factor], axis=0)
    other = lax.ppermute(factors, "tp", [(0, 1), (1, 0)])
    rank_half = factor_in.shape[1]
    own_in, other_in = factor_in.T, other[:rank_half]
    own_out, other_out = adapter_output_factor, other[rank_half:]

    attended = attend(queries, cache_keys, cache_values, new_keys, new_values, cache_lengths)
    width = attended.shape[1] // chunk_count
    own_width = factor_in.shape[0]
    gathered = [
        ring_gather(attended[:, c * width : (c + 1) * width], order) for c in range(chunk_count)
    ]
    state = None
    for c, (near, far) in enumerate(gathered):
        start = mine * own_width - c * width
        owns = (core == side) & (start >= 0) & (start < width)
        flags = jnp.stack(
            [owns.astype(jnp.int32), jnp.clip(start, 0, width - own_width), core, core ^ side, mine]
        )
        state = project(c, places, flags, near, far, base_weight, own_in, other_in, state)
    partial, ranked = state

    bit = 1
    while bit < count:
        turn = 1 if bit == half_count else 0
        pairs = [
            (2 * f + t, 2 * (f ^ bit) + (t ^ turn)) for f in range(count) for t in range(2)
        ]
        ranked = ranked + lax.ppermute(ranked, both, pairs)
        bit *= 2

    keep, send = add_adapter(flags, partial, ranked, own_out, other_out)
    received = lax.ppermute(send, "tp", [(0, 1), (1, 0)])
    pieces = round_and_split(flags, keep, received, row_count, step_count)
    landed = []
    for offset, piece in enumerate(pieces):
        pairs = [
            (2 * f + t, 2 * (f ^ (t * half_count + offset)) + f // half_count)
            for f in range(count)
            for t in range(2)
        ]
        landed.append(lax.ppermute(piece, both, pairs))
    return place(flags, landed)


def solution(mesh):
    return jax.shard_map(
        functools.partial(shards, mesh.shape["fsdp"]),
        mesh=mesh,
        in_specs=(
            P(("groups", "fsdp"), None, "tp", None),
            P(("groups", "fsdp"), None, "tp", None),
            P(("groups", "fsdp"), None, "tp", None),
            P(("groups", "fsdp"), None, "tp", None),
            P(("groups", "fsdp"), None, "tp", None),
            P(("groups", "fsdp")),
            P("tp", "fsdp"),
            P(("groups", "fsdp"), "tp"),
            P(("groups", "tp"), "fsdp"),
        ),
        out_specs=P(("groups", "fsdp"), None, "tp"),
        check_vma=False,
    )
```

time: 205 us -> 85.4 us (0.42)
  waiting for transfers between devices: 129 us -> 20.2 us
  blocking collectives: 33.1 us -> 0 us
  starting transfers between devices: 0.09 us -> 31.9 us
  Pallas kernels: 0 us -> 19.4 us
  matrix products: 23.5 us -> 4.85 us
  between operations: 13.2 us -> 0.29 us
    all_gather x2 -> x0, waiting for transfers between devices: 120 us -> none  [the longest x1 74 us: shards(): every_row = lax.all_gather(rank_all, 'fsdp', axis=0, tiled=True)]
    ppermute x0 -> x25, starting transfers between devices: none -> 31.9 us  [the longest x3 11.1 us: shards(): ranked = ranked + lax.ppermute(ranked, both, pairs)]
    all_to_all x1 -> x0, blocking collectives: 28.5 us -> none  [shards(): lax.all_to_all(partial_value, 'fsdp', split_axis=0, concat_axis=1, tiled=...]
    ppermute x0 -> x25, waiting for transfers between devices: none -> 20.2 us  [the longest x3 7.7 us: shards(): ranked = ranked + lax.ppermute(ranked, both, pairs)]
    pallas_call x0 -> x5, Pallas kernels: none -> 19.4 us  [the longest x2 16.1 us: project(): pl.pallas_call(functools.partial(project_kernel, count, per_tile, previou...]
    dot_general x1 -> x0, matrix products: 18.6 us -> none  [shards(): jnp.dot(lax.all_gather(local_rows, 'fsdp', axis=0, tiled=True), combined_...]
    reduce_scatter x1 -> x0, waiting for transfers between devices: 9.3 us -> none  [shards(): summed = lax.psum_scatter(spread, 'tp', scatter_dimension=1, tiled=True)]
    all_gather x2 -> x0, blocking collectives: 4.63 us -> none  [the longest x1 2.31 us: shards(): lax.all_gather(adapter_output_factor, 'tp', axis=0, tiled=True)]
  transfers between devices with their start and end apart: 3 -> 25, of which waited for: 3 -> 14; matrix products, arithmetic and copies ran while one was open for 0% -> 10% of each run, Pallas kernels for 0% -> 9%
where the time goes in v1:
time: 85.4 us; the launch traced here: 85 us
  starting transfers between devices  31.9 us (37%)
  waiting for transfers between devices  20.2 us (24%)
  Pallas kernels  19.4 us (23%)
  matrix products  4.85 us (6%)
  local copies, waits for them, and re-layouts  4.77 us (6%)
  other arithmetic  3.58 us (4%)
    pallas_call x2, Pallas kernels, project(): pl.pallas_call(functools.partial(project_kernel, count, per_tile, previou...  16.1 us
    ppermute x3, starting transfers between devices, shards(): ranked = ranked + lax.ppermute(ranked, both, pairs)  11.1 us
    ppermute x6, starting transfers between devices, ring_gather(): rising = lax.ppermute(rising, 'fsdp', up)  9.49 us
    ppermute x3, waiting for transfers between devices, shards(): ranked = ranked + lax.ppermute(ranked, both, pairs)  7.7 us
    ppermute x4, starting transfers between devices, shards(): landed.append(lax.ppermute(piece, both, pairs))  6.97 us
    ppermute x6, waiting for transfers between devices, ring_gather(): rising = lax.ppermute(rising, 'fsdp', up)  6.2 us
    ppermute x4, waiting for transfers between devices, shards(): landed.append(lax.ppermute(piece, both, pairs))  4.52 us
    ppermute x2, starting transfers between devices, ring_gather(): far_left = lax.ppermute(rising[:, :half], 'fsdp', up)  3.14 us
  transfers between devices with their start and end apart: 25, of which 14 were waited for; matrix products, arithmetic and copies ran while one was open for 10% of the time, Pallas kernels for 9%

profile of v1, /device:TPU:1, one launch (start us, length us, event | category | flops | bytes accessed | tf_op | source)
XLA Modules:
  0.0 85.0 jit_solution(17763236868710945809)
XLA Ops:
  0.0 2.0 %pad_maximum_fusion = bf16[128,2048]{1,0:T(8,128)(2,1)} fusion(bf16[64,2048]{1,0:T(8,128)(2,1)} %own_out.1, bf16[64,2048]{1,0:T(8,128)(2,1)} %bitcast.28), kind=kLoop, calls=%fused_computation.19 | loop fusion | flops 1048576 | bytes 1048576 | tf_op jit(solution)/shard_map/concatenate | solution.py:289
  2.0 0.1 collective-permute-start.8
  2.1 0.7 iota_compare_fusion
  2.8 1.7 %fusion.38 = (f32[4,4,4,16]{3,2,1,0:T(4,128)S(1)}, f32[4,4,4,16,4]{3,4,2,1,0:T(4,128)S(1)}) fusion(bf16[4,4,4,128,1]{3,2,1,0,4:T(4,128)(2,1)} %bitcast.37, bf16[4,4,4,16,128]{4,3,2,1,0:T(8,128)(2,1)} %bitcast.33, pred[4,4]{1,0:T(4,128)(4,1)S(1)} %iota_compare_fusion.1), kind=kOutput, calls=%fused_computation.37 | convolution fusion | flops 1059840 | bytes 299024 | tf_op jit(solution)/shard_map/rsgqd,rtgd->rgsqt/dot_general | solution.py:30
  4.5 1.9 %fusion.4 = (f32[4,4,4,16]{3,2,1,0:T(4,128)S(1)}, f32[4,4,4,16,512]{4,3,2,1,0:T(8,128)S(1)}) fusion(pred[4,512]{1,0:T(4,128)(4,1)S(1)} %iota_compare_fusion, bf16[4,512,4,128,1]{3,2,1,0,4:T(4,128)(2,1)S(1)} %bitcast.27, bf16[4,4,4,16,128]{4,3,2,1,0:T(8,128)(2,1)} %bitcast.34), kind=kOutput, calls=%fused_computation.6 | convolution fusion | flops 135789568 | bytes 4462592 | tf_op jit(solution)/shard_map/rsgqd,rlgd->rgsql/dot_general | solution.py:24
  6.4 0.0 copy-start.10
  6.4 0.0 copy-start.11
  6.5 0.1 fusion.27
  6.6 0.6 fusion.5
  7.3 0.3 fusion.29
  7.6 0.5 copy-done.11
  8.0 1.0 %fusion.16 = bf16[4,4,4,16,128]{4,3,1,2,0:T(8,128)(2,1)S(1)} fusion(f32[4,4,4,16,128]{4,3,2,1,0:T(8,128)S(1)} %fusion.29, bf16[4,512,4,128,1]{3,2,1,0,4:T(4,128)(2,1)S(1)} %bitcast.36, f32[4,4,4,16,512]{4,3,2,1,0:T(8,128)S(1)} %get-tuple-element.30, f32[4,4,4,16]{3,2,1,0:T(4,128)S(1)} %max.15, pred[4,512]{1,0:T(4,128)(4,1)S(1)} %iota_compare_fusion, ...), kind=kOutput, calls=%fused_computation.12 | convolution fusion | flops 136708096 | bytes 4990976 | tf_op jit(solution)/shard_map/rgsql,rlgd->rsgqd/dot_general | solution.py:40
  9.0 0.0 copy-start.1
  9.1 0.1 reshape.48
  9.2 2.8 %collective-permute-start.12 = (bf16[16,4096]{1,0:T(8,128)(2,1)S(1)}, bf16[16,4096]{1,0:T(8,128)(2,1)S(1)}, u32[]{:S(2)}, u32[]{:S(2)}) collective-permute-start(bf16[16,4096]{1,0:T(8,128)(2,1)S(1)} %get-tuple-element.27.refs_2_), channel_id=1, source_target_pairs={{0,4},{4,8},{8,12},{12,14},{14,10},{10,6},{6,2},{2,0},{1,5},{5,9},... | collective-permute-start | bytes 393224 | tf_op jit(solution)/shard_map/ppermute | solution.py:77
  12.0 0.0 collective-permute-start.9
  12.0 1.5 %collective-permute-start.3 = (bf16[16,4096]{1,0:T(8,128)(2,1)S(1)}, bf16[16,4096]{1,0:T(8,128)(2,1)S(1)}, u32[]{:S(2)}, u32[]{:S(2)}) collective-permute-start(bf16[16,4096]{1,0:T(8,128)(2,1)S(1)} %get-tuple-element.28.refs_2_), channel_id=1, source_target_pairs={{0,4},{4,8},{8,12},{12,14},{14,10},{10,6},{6,2},{2,0},{1,5},{5,9},... | collective-permute-start | bytes 393224 | tf_op jit(solution)/shard_map/ppermute | solution.py:77
  13.5 0.0 collective-permute-start
  13.5 2.3 %collective-permute-done.12.refs_8_ = bf16[16,4096]{1,0:T(8,128)(2,1)S(1)} collective-permute-done((bf16[16,4096]{1,0:T(8,128)(2,1)S(1)}, bf16[16,4096]{1,0:T(8,128)(2,1)S(1)}, u32[]{:S(2)}, u32[]{:S(2)}) %collective-permute-start.12) | collective-permute-done | bytes 131104 | tf_op jit(solution)/shard_map/ppermute | solution.py:77
  15.8 1.3 %collective-permute-start.13 = (bf16[16,4096]{1,0:T(8,128)(2,1)S(1)}, bf16[16,4096]{1,0:T(8,128)(2,1)}, u32[]{:S(2)}, u32[]{:S(2)}) collective-permute-start(bf16[16,4096]{1,0:T(8,128)(2,1)S(1)} %collective-permute-done.12.refs_8_), channel_id=1, source_target_pairs={{0,4},{4,8},{8,12},{12,14},{14,10},{10,6},{6,2},{2,0},{1,5},{5,9},... | collective-permute-start | bytes 393224 | tf_op jit(solution)/shard_map/ppermute | solution.py:77
  17.1 0.1 collective-permute-start.10
  17.3 0.7 copy-done.3
  17.9 0.7 collective-permute-done.3.refs_8_
  18.6 1.3 %collective-permute-start.4 = (bf16[16,4096]{1,0:T(8,128)(2,1)S(1)}, bf16[16,4096]{1,0:T(8,128)(2,1)}, u32[]{:S(2)}, u32[]{:S(2)}) collective-permute-start(bf16[16,4096]{1,0:T(8,128)(2,1)S(1)} %collective-permute-done.3.refs_8_), channel_id=1, source_target_pairs={{0,4},{4,8},{8,12},{12,14},{14,10},{10,6},{6,2},{2,0},{1,5},{5,9},... | collective-permute-start | bytes 393224 | tf_op jit(solution)/shard_map/ppermute | solution.py:77
  19.9 0.1 collective-permute-start.1
  20.1 0.6 collective-permute-done.13.refs_7_
  20.7 1.3 %collective-permute-start.14 = (bf16[16,4096]{1,0:T(8,128)(2,1)}, bf16[16,4096]{1,0:T(8,128)(2,1)S(1)}, u32[]{:S(2)}, u32[]{:S(2)}) collective-permute-start(bf16[16,4096]{1,0:T(8,128)(2,1)} %collective-permute-done.13.refs_7_), channel_id=1, source_target_pairs={{0,4},{4,8},{8,12},{12,14},{14,10},{10,6},{6,2},{2,0},{1,5},{5,9},... | collective-permute-start | bytes 393224 | tf_op jit(solution)/shard_map/ppermute | solution.py:77
  22.0 0.2 collective-permute-start.11
  22.2 1.4 %collective-permute-done.4.refs_7_ = bf16[16,4096]{1,0:T(8,128)(2,1)} collective-permute-done((bf16[16,4096]{1,0:T(8,128)(2,1)S(1)}, bf16[16,4096]{1,0:T(8,128)(2,1)}, u32[]{:S(2)}, u32[]{:S(2)}) %collective-permute-start.4) | collective-permute-done | bytes 131104 | tf_op jit(solution)/shard_map/ppermute | solution.py:77
  23.6 1.3 %collective-permute-start.5 = (bf16[16,4096]{1,0:T(8,128)(2,1)}, bf16[16,4096]{1,0:T(8,128)(2,1)S(1)}, u32[]{:S(2)}, u32[]{:S(2)}) collective-permute-start(bf16[16,4096]{1,0:T(8,128)(2,1)} %collective-permute-done.4.refs_7_), channel_id=1, source_target_pairs={{0,4},{4,8},{8,12},{12,14},{14,10},{10,6},{6,2},{2,0},{1,5},{5,9},... | collective-permute-start | bytes 393224 | tf_op jit(solution)/shard_map/ppermute | solution.py:77
  24.8 0.2 collective-permute-start.2
  25.0 0.1 stack.42.refs_1_.flags
  25.1 0.1 stack.46.refs_1_
  25.2 0.7 dynamic-slice_bitcast_fusion.refs_0_
  25.9 0.1 collective-permute-done.14.refs_6_
  26.0 1.5 %collective-permute-start.15 = (bf16[16,2048]{1,0:T(8,128)(2,1)S(1)}, bf16[16,2048]{1,0:T(8,128)(2,1)S(1)}, u32[]{:S(2)}, u32[]{:S(2)}) collective-permute-start(bf16[16,2048]{1,0:T(8,128)(2,1)S(1)} %slice.37), channel_id=1, source_target_pairs={{0,4},{4,8},{8,12},{12,14},{14,10},{10,6},{6,2},{2,0},{1,5},{5,9},... | collective-permute-start | bytes 196616 | tf_op jit(solution)/shard_map/ppermute | solution.py:82
  27.5 0.1 collective-permute-start.16
  27.5 1.1 %collective-permute-done.5.refs_6_ = bf16[16,4096]{1,0:T(8,128)(2,1)S(1)} collective-permute-done((bf16[16,4096]{1,0:T(8,128)(2,1)}, bf16[16,4096]{1,0:T(8,128)(2,1)S(1)}, u32[]{:S(2)}, u32[]{:S(2)}) %collective-permute-start.5) | collective-permute-done | bytes 131104 | tf_op jit(solution)/shard_map/ppermute | solution.py:77
  28.6 1.7 %collective-permute-start.6 = (bf16[16,2048]{1,0:T(8,128)(2,1)S(1)}, bf16[16,2048]{1,0:T(8,128)(2,1)S(1)}, u32[]{:S(2)}, u32[]{:S(2)}) collective-permute-start(bf16[16,2048]{1,0:T(8,128)(2,1)S(1)} %slice.33), channel_id=1, source_target_pairs={{0,4},{4,8},{8,12},{12,14},{14,10},{10,6},{6,2},{2,0},{1,5},{5,9},... | collective-permute-start | bytes 196616 | tf_op jit(solution)/shard_map/ppermute | solution.py:82
  30.3 0.3 collective-permute-done.2.refs_5_
  30.6 1.1 %fusion.36 = (bf16[64,2048]{1,0:T(8,128)(2,1)S(1)}, bf16[64,2048]{1,0:T(8,128)(2,1)S(1)}) fusion(bf16[128,2048]{1,0:T(8,128)(2,1)} %collective-permute-done.8), kind=kLoop, calls=%fused_computation.35 | loop fusion | bytes 1048576 | tf_op jit(solution)/shard_map/slice | solution.py:293
  31.7 0.9 %copy-done.4 = bf16[16,4096]{1,0:T(8,128)(2,1)S(1)} copy-done((bf16[16,4096]{1,0:T(8,128)(2,1)S(1)}, bf16[16,4096]{1,0:T(8,128)(2,1)}, u32[]{:S(2)}) %copy-start.4) | copy-done | bytes 131096
  32.6 8.1 %project_0.1 = (f32[128,2048]{1,0:T(8,128)S(1)}, f32[128,128]{1,0:T(8,128)S(1)}) custom-call(s32[8]{0:T(128)S(1)} %dynamic-slice_bitcast_fusion.refs_0_, s32[5]{0:T(128)S(1)} %stack.46.refs_1_, bf16[16,4096]{1,0:T(8,128)(2,1)S(1)} %get-tuple-element.27.refs_2_, bf16[16,4096]{1,0:T(8,128)(2,1)S(1)} %copy-done.4, ...), custom_call_target="tpu_custom_call" | custom-call | flops 4294967296 | bytes 16777216 | tf_op jit(solution)/shard_map/project_0/pallas_call | solution.py:155
  40.7 0.0 copy-start.2
  40.7 8.1 %project_1.1 = (f32[128,2048]{1,0:T(8,128)S(1)}, f32[128,128]{1,0:T(8,128)S(1)}) custom-call(s32[8]{0:T(128)S(1)} %dynamic-slice_bitcast_fusion.refs_0_, s32[5]{0:T(128)S(1)} %stack.42.refs_1_.flags, bf16[16,4096]{1,0:T(8,128)(2,1)S(1)} %get-tuple-element.28.refs_2_, bf16[16,4096]{1,0:T(8,128)(2,1)S(1)} %collective-permute-done.refs_3_, ...), custom_call_target="tpu_custom_call" | custom-call | flops 4294967296 | bytes 16777216 | tf_op jit(solution)/shard_map/project_1/pallas_call | solution.py:155
  48.8 1.5 %collective-permute-start.17 = (f32[128,128]{1,0:T(8,128)S(1)}, f32[128,128]{1,0:T(8,128)S(1)}, u32[]{:S(2)}, u32[]{:S(2)}) collective-permute-start(f32[128,128]{1,0:T(8,128)S(1)} %get-tuple-element.18), channel_id=1, source_target_pairs={{0,2},{1,3},{2,0},{3,1},{4,6},{5,7},{6,4},{7,5},{8,10},{9,11},{10,... | collective-permute-start | bytes 196616 | tf_op jit(solution)/shard_map/ppermute | solution.py:317
  50.2 1.7 %collective-permute-done.17 = f32[128,128]{1,0:T(8,128)S(1)} collective-permute-done((f32[128,128]{1,0:T(8,128)S(1)}, f32[128,128]{1,0:T(8,128)S(1)}, u32[]{:S(2)}, u32[]{:S(2)}) %collective-permute-start.17) | collective-permute-done | bytes 65568 | tf_op jit(solution)/shard_map/ppermute | solution.py:317
  52.0 1.5 %collective-permute-start.18 = (f32[128,128]{1,0:T(8,128)S(1)}, f32[128,128]{1,0:T(8,128)S(1)}, u32[]{:S(2)}, u32[]{:S(2)}) collective-permute-start(f32[128,128]{1,0:T(8,128)S(1)} %add.38), channel_id=1, source_target_pairs={{0,4},{1,5},{2,6},{3,7},{4,0},{5,1},{6,2},{7,3},{8,12},{9,13},{10,... | collective-permute-start | bytes 196616 | tf_op jit(solution)/shard_map/ppermute | solution.py:317
  53.5 1.7 %collective-permute-done.18 = f32[128,128]{1,0:T(8,128)S(1)} collective-permute-done((f32[128,128]{1,0:T(8,128)S(1)}, f32[128,128]{1,0:T(8,128)S(1)}, u32[]{:S(2)}, u32[]{:S(2)}) %collective-permute-start.18) | collective-permute-done | bytes 65568 | tf_op jit(solution)/shard_map/ppermute | solution.py:317
  55.2 8.1 %collective-permute-start.19 = (f32[128,128]{1,0:T(8,128)S(1)}, f32[128,128]{1,0:T(8,128)S(1)}, u32[]{:S(2)}, u32[]{:S(2)}) collective-permute-start(f32[128,128]{1,0:T(8,128)S(1)} %add.39), channel_id=1, source_target_pairs={{0,9},{1,8},{2,11},{3,10},{4,13},{5,12},{6,15},{7,14},{8,1},{9,0},... | collective-permute-start | bytes 196616 | tf_op jit(solution)/shard_map/ppermute | solution.py:317
  63.3 4.3 %collective-permute-done.19 = f32[128,128]{1,0:T(8,128)S(1)} collective-permute-done((f32[128,128]{1,0:T(8,128)S(1)}, f32[128,128]{1,0:T(8,128)S(1)}, u32[]{:S(2)}, u32[]{:S(2)}) %collective-permute-start.19) | collective-permute-done | bytes 65568 | tf_op jit(solution)/shard_map/ppermute | solution.py:317
  67.6 1.0 %add_adapter.1 = (f32[64,2048]{1,0:T(8,128)S(1)}, f32[64,2048]{1,0:T(8,128)S(1)}) custom-call(s32[5]{0:T(128)S(1)} %stack.42.refs_1_.flags, f32[128,2048]{1,0:T(8,128)S(1)} %get-tuple-element.17.partial, f32[128,128]{1,0:T(8,128)S(1)} %add.40.ranked, bf16[64,2048]{1,0:T(8,128)(2,1)S(1)} %copy-done.2, bf16[64,2048]{1,0:T(8,128)(2,1)S(1)} %get-tuple-element.25.other_out), custom_call_target="tpu_custom_call" | custom-call | tf_op jit(solution)/shard_map/add_adapter/pallas_call | solution.py:208
  68.6 0.5 collective-permute-start.20
  69.1 1.5 %collective-permute-done.20 = f32[64,2048]{1,0:T(8,128)S(1)} collective-permute-done((f32[64,2048]{1,0:T(8,128)S(1)}, f32[64,2048]{1,0:T(8,128)S(1)}, u32[]{:S(2)}, u32[]{:S(2)}) %collective-permute-start.20) | collective-permute-done | bytes 524320 | tf_op jit(solution)/shard_map/ppermute | solution.py:321
  70.6 0.6 round_and_split.1
  71.2 2.2 %collective-permute-start.21 = (bf16[4,4,2048]{2,1,0:T(4,128)(2,1)S(1)}, bf16[4,4,2048]{2,1,0:T(4,128)(2,1)S(1)}, u32[]{:S(2)}, u32[]{:S(2)}) collective-permute-start(bf16[4,4,2048]{2,1,0:T(4,128)(2,1)S(1)} %get-tuple-element.21), channel_id=1, source_target_pairs={{0,0},{1,8},{2,2},{3,10},{4,4},{5,12},{6,6},{7,14},{8,9},{9,1},{10... | collective-permute-start | bytes 196616 | tf_op jit(solution)/shard_map/ppermute | solution.py:330
  73.4 0.6 collective-permute-start.22
  74.0 2.2 %collective-permute-start.23 = (bf16[4,4,2048]{2,1,0:T(4,128)(2,1)S(1)}, bf16[4,4,2048]{2,1,0:T(4,128)(2,1)S(1)}, u32[]{:S(2)}, u32[]{:S(2)}) collective-permute-start(bf16[4,4,2048]{2,1,0:T(4,128)(2,1)S(1)} %get-tuple-element.23), channel_id=1, source_target_pairs={{0,4},{1,12},{2,6},{3,14},{4,0},{5,8},{6,2},{7,10},{8,13},{9,5},{1... | collective-permute-start | bytes 196616 | tf_op jit(solution)/shard_map/ppermute | solution.py:330
  76.2 2.0 %collective-permute-start.24 = (bf16[4,4,2048]{2,1,0:T(4,128)(2,1)S(1)}, bf16[4,4,2048]{2,1,0:T(4,128)(2,1)S(1)}, u32[]{:S(2)}, u32[]{:S(2)}) collective-permute-start(bf16[4,4,2048]{2,1,0:T(4,128)(2,1)S(1)} %get-tuple-element.24), channel_id=1, source_target_pairs={{0,6},{1,14},{2,4},{3,12},{4,2},{5,10},{6,0},{7,8},{8,15},{9,7},{1... | collective-permute-start | bytes 196616 | tf_op jit(solution)/shard_map/ppermute | solution.py:330
  78.2 0.6 collective-permute-done.22.refs_1_
  78.8 2.6 %collective-permute-done.23.refs_2_ = bf16[4,4,2048]{2,1,0:T(4,128)(2,1)S(1)} collective-permute-done((bf16[4,4,2048]{2,1,0:T(4,128)(2,1)S(1)}, bf16[4,4,2048]{2,1,0:T(4,128)(2,1)S(1)}, u32[]{:S(2)}, u32[]{:S(2)}) %collective-permute-start.23) | collective-permute-done | bytes 65568 | tf_op jit(solution)/shard_map/ppermute | solution.py:330
  81.3 1.4 %collective-permute-done.24.refs_3_ = bf16[4,4,2048]{2,1,0:T(4,128)(2,1)S(1)} collective-permute-done((bf16[4,4,2048]{2,1,0:T(4,128)(2,1)S(1)}, bf16[4,4,2048]{2,1,0:T(4,128)(2,1)S(1)}, u32[]{:S(2)}, u32[]{:S(2)}) %collective-permute-start.24) | collective-permute-done | bytes 65568 | tf_op jit(solution)/shard_map/ppermute | solution.py:330
  82.7 0.6 copy-done.9
  83.4 1.7 %place.1 = bf16[4,4,8192]{2,1,0:T(4,128)(2,1)} custom-call(s32[5]{0:T(128)} %copy-done.5, bf16[4,4,2048]{2,1,0:T(4,128)(2,1)} %copy-done.6, bf16[4,4,2048]{2,1,0:T(4,128)(2,1)} %copy-done.7, bf16[4,4,2048]{2,1,0:T(4,128)(2,1)} %copy-done.8, bf16[4,4,2048]{2,1,0:T(4,128)(2,1)} %copy-done.9), custom_call_target="tpu_custom_call" | custom-call | tf_op jit(solution)/shard_map/place/pallas_call | solution.py:252
  (40 shorter events, 0.2 us)
Async XLA Ops:
  0.0 4.5 %copy-start = (bf16[4,512,4,128]{3,2,1,0:T(4,128)(2,1)S(1)}, bf16[4,512,4,128]{3,2,1,0:T(4,128)(2,1)}, u32[]{:S(2)}) copy-start(bf16[4,512,4,128]{3,2,1,0:T(4,128)(2,1)} %param.11) | copy-start | bytes 6291460
  2.0 28.6 %collective-permute-start.8 = (bf16[128,2048]{1,0:T(8,128)(2,1)}, bf16[128,2048]{1,0:T(8,128)(2,1)}, u32[]{:S(2)}, u32[]{:S(2)}) collective-permute-start(bf16[128,2048]{1,0:T(8,128)(2,1)} %pad_maximum_fusion), channel_id=1, source_target_pairs={{0,1},{1,0},{2,3},{3,2},{4,5},{5,4},{6,7},{7,6},{8,9},{9,8},{10,11... | collective-permute-start | bytes 1572872 | tf_op jit(solution)/shard_map/ppermute | solution.py:290
  6.4 0.8 copy-start.10
  6.4 1.6 %copy-start.11 = (bf16[4,512,4,128]{3,2,1,0:T(4,128)(2,1)S(1)}, bf16[4,512,4,128]{3,2,1,0:T(4,128)(2,1)}, u32[]{:S(2)}) copy-start(bf16[4,512,4,128]{3,2,1,0:T(4,128)(2,1)} %param.12) | copy-start | bytes 6291460
  9.0 22.7 %copy-start.1 = (bf16[2048,64]{0,1:T(8,128)(2,1)S(1)}, bf16[2048,64]{0,1:T(8,128)(2,1)}, u32[]{:S(2)}) copy-start(bf16[2048,64]{0,1:T(8,128)(2,1)} %param.17) | copy-start | bytes 786436
  9.2 6.6 %collective-permute-start.12 = (bf16[16,4096]{1,0:T(8,128)(2,1)S(1)}, bf16[16,4096]{1,0:T(8,128)(2,1)S(1)}, u32[]{:S(2)}, u32[]{:S(2)}) collective-permute-start(bf16[16,4096]{1,0:T(8,128)(2,1)S(1)} %get-tuple-element.27.refs_2_), channel_id=1, source_target_pairs={{0,4},{4,8},{8,12},{12,14},{14,10},{10,6},{6,2},{2,0},{1,5},{5,9},... | collective-permute-start | bytes 393224 | tf_op jit(solution)/shard_map/ppermute | solution.py:77
  12.0 5.1 %collective-permute-start.9 = (bf16[16,4096]{1,0:T(8,128)(2,1)S(1)}, bf16[16,4096]{1,0:T(8,128)(2,1)S(1)}, u32[]{:S(2)}, u32[]{:S(2)}) collective-permute-start(bf16[16,4096]{1,0:T(8,128)(2,1)S(1)} %get-tuple-element.27.refs_2_), channel_id=1, source_target_pairs={{4,0},{8,4},{12,8},{14,12},{10,14},{6,10},{2,6},{0,2},{5,1},{9,5},... | collective-permute-start | bytes 393224 | tf_op jit(solution)/shard_map/ppermute | solution.py:78
  12.0 6.6 %collective-permute-start.3 = (bf16[16,4096]{1,0:T(8,128)(2,1)S(1)}, bf16[16,4096]{1,0:T(8,128)(2,1)S(1)}, u32[]{:S(2)}, u32[]{:S(2)}) collective-permute-start(bf16[16,4096]{1,0:T(8,128)(2,1)S(1)} %get-tuple-element.28.refs_2_), channel_id=1, source_target_pairs={{0,4},{4,8},{8,12},{12,14},{14,10},{10,6},{6,2},{2,0},{1,5},{5,9},... | collective-permute-start | bytes 393224 | tf_op jit(solution)/shard_map/ppermute | solution.py:77
  13.5 6.5 %collective-permute-start = (bf16[16,4096]{1,0:T(8,128)(2,1)S(1)}, bf16[16,4096]{1,0:T(8,128)(2,1)S(1)}, u32[]{:S(2)}, u32[]{:S(2)}) collective-permute-start(bf16[16,4096]{1,0:T(8,128)(2,1)S(1)} %get-tuple-element.28.refs_2_), channel_id=1, source_target_pairs={{4,0},{8,4},{12,8},{14,12},{10,14},{6,10},{2,6},{0,2},{5,1},{9,5},... | collective-permute-start | bytes 393224 | tf_op jit(solution)/shard_map/ppermute | solution.py:78
  15.8 4.9 %collective-permute-start.13 = (bf16[16,4096]{1,0:T(8,128)(2,1)S(1)}, bf16[16,4096]{1,0:T(8,128)(2,1)}, u32[]{:S(2)}, u32[]{:S(2)}) collective-permute-start(bf16[16,4096]{1,0:T(8,128)(2,1)S(1)} %collective-permute-done.12.refs_8_), channel_id=1, source_target_pairs={{0,4},{4,8},{8,12},{12,14},{14,10},{10,6},{6,2},{2,0},{1,5},{5,9},... | collective-permute-start | bytes 393224 | tf_op jit(solution)/shard_map/ppermute | solution.py:77
  17.1 4.9 %collective-permute-start.10 = (bf16[16,4096]{1,0:T(8,128)(2,1)S(1)}, bf16[16,4096]{1,0:T(8,128)(2,1)}, u32[]{:S(2)}, u32[]{:S(2)}) collective-permute-start(bf16[16,4096]{1,0:T(8,128)(2,1)S(1)} %collective-permute-done.9.refs_3_), channel_id=1, source_target_pairs={{4,0},{8,4},{12,8},{14,12},{10,14},{6,10},{2,6},{0,2},{5,1},{9,5},... | collective-permute-start | bytes 393224 | tf_op jit(solution)/shard_map/ppermute | solution.py:78
  17.3 0.7 copy-start.3
  18.6 4.9 %collective-permute-start.4 = (bf16[16,4096]{1,0:T(8,128)(2,1)S(1)}, bf16[16,4096]{1,0:T(8,128)(2,1)}, u32[]{:S(2)}, u32[]{:S(2)}) collective-permute-start(bf16[16,4096]{1,0:T(8,128)(2,1)S(1)} %collective-permute-done.3.refs_8_), channel_id=1, source_target_pairs={{0,4},{4,8},{8,12},{12,14},{14,10},{10,6},{6,2},{2,0},{1,5},{5,9},... | collective-permute-start | bytes 393224 | tf_op jit(solution)/shard_map/ppermute | solution.py:77
  19.9 4.9 %collective-permute-start.1 = (bf16[16,4096]{1,0:T(8,128)(2,1)S(1)}, bf16[16,4096]{1,0:T(8,128)(2,1)}, u32[]{:S(2)}, u32[]{:S(2)}) collective-permute-start(bf16[16,4096]{1,0:T(8,128)(2,1)S(1)} %collective-permute-done.refs_3_), channel_id=1, source_target_pairs={{4,0},{8,4},{12,8},{14,12},{10,14},{6,10},{2,6},{0,2},{5,1},{9,5},... | collective-permute-start | bytes 393224 | tf_op jit(solution)/shard_map/ppermute | solution.py:78
  20.7 5.3 %collective-permute-start.14 = (bf16[16,4096]{1,0:T(8,128)(2,1)}, bf16[16,4096]{1,0:T(8,128)(2,1)S(1)}, u32[]{:S(2)}, u32[]{:S(2)}) collective-permute-start(bf16[16,4096]{1,0:T(8,128)(2,1)} %collective-permute-done.13.refs_7_), channel_id=1, source_target_pairs={{0,4},{4,8},{8,12},{12,14},{14,10},{10,6},{6,2},{2,0},{1,5},{5,9},... | collective-permute-start | bytes 393224 | tf_op jit(solution)/shard_map/ppermute | solution.py:77
  22.0 5.4 %collective-permute-start.11 = (bf16[16,4096]{1,0:T(8,128)(2,1)}, bf16[16,4096]{1,0:T(8,128)(2,1)S(1)}, u32[]{:S(2)}, u32[]{:S(2)}) collective-permute-start(bf16[16,4096]{1,0:T(8,128)(2,1)} %collective-permute-done.10.refs_4_), channel_id=1, source_target_pairs={{4,0},{8,4},{12,8},{14,12},{10,14},{6,10},{2,6},{0,2},{5,1},{9,5},... | collective-permute-start | bytes 393224 | tf_op jit(solution)/shard_map/ppermute | solution.py:78
  23.6 5.1 %collective-permute-start.5 = (bf16[16,4096]{1,0:T(8,128)(2,1)}, bf16[16,4096]{1,0:T(8,128)(2,1)S(1)}, u32[]{:S(2)}, u32[]{:S(2)}) collective-permute-start(bf16[16,4096]{1,0:T(8,128)(2,1)} %collective-permute-done.4.refs_7_), channel_id=1, source_target_pairs={{0,4},{4,8},{8,12},{12,14},{14,10},{10,6},{6,2},{2,0},{1,5},{5,9},... | collective-permute-start | bytes 393224 | tf_op jit(solution)/shard_map/ppermute | solution.py:77
  24.8 5.7 %collective-permute-start.2 = (bf16[16,4096]{1,0:T(8,128)(2,1)}, bf16[16,4096]{1,0:T(8,128)(2,1)S(1)}, u32[]{:S(2)}, u32[]{:S(2)}) collective-permute-start(bf16[16,4096]{1,0:T(8,128)(2,1)} %collective-permute-done.1.refs_4_), channel_id=1, source_target_pairs={{4,0},{8,4},{12,8},{14,12},{10,14},{6,10},{2,6},{0,2},{5,1},{9,5},... | collective-permute-start | bytes 393224 | tf_op jit(solution)/shard_map/ppermute | solution.py:78
  25.1 45.5 %copy-start.5 = (s32[5]{0:T(128)}, s32[5]{0:T(128)S(1)}, u32[]{:S(2)}) copy-start(s32[5]{0:T(128)S(1)} %stack.42.refs_1_.flags) | copy-start | bytes 64
  26.0 5.7 %collective-permute-start.15 = (bf16[16,2048]{1,0:T(8,128)(2,1)S(1)}, bf16[16,2048]{1,0:T(8,128)(2,1)S(1)}, u32[]{:S(2)}, u32[]{:S(2)}) collective-permute-start(bf16[16,2048]{1,0:T(8,128)(2,1)S(1)} %slice.37), channel_id=1, source_target_pairs={{0,4},{4,8},{8,12},{12,14},{14,10},{10,6},{6,2},{2,0},{1,5},{5,9},... | collective-permute-start | bytes 196616 | tf_op jit(solution)/shard_map/ppermute | solution.py:82
  27.5 4.2 %collective-permute-start.16 = (bf16[16,2048]{1,0:T(8,128)(2,1)S(1)}, bf16[16,2048]{1,0:T(8,128)(2,1)S(1)}, u32[]{:S(2)}, u32[]{:S(2)}) collective-permute-start(bf16[16,2048]{1,0:T(8,128)(2,1)S(1)} %slice.38), channel_id=1, source_target_pairs={{4,0},{8,4},{12,8},{14,12},{10,14},{6,10},{2,6},{0,2},{5,1},{9,5},... | collective-permute-start | bytes 196616 | tf_op jit(solution)/shard_map/ppermute | solution.py:83
  28.6 12.0 %collective-permute-start.6 = (bf16[16,2048]{1,0:T(8,128)(2,1)S(1)}, bf16[16,2048]{1,0:T(8,128)(2,1)S(1)}, u32[]{:S(2)}, u32[]{:S(2)}) collective-permute-start(bf16[16,2048]{1,0:T(8,128)(2,1)S(1)} %slice.33), channel_id=1, source_target_pairs={{0,4},{4,8},{8,12},{12,14},{14,10},{10,6},{6,2},{2,0},{1,5},{5,9},... | collective-permute-start | bytes 196616 | tf_op jit(solution)/shard_map/ppermute | solution.py:82
  30.6 10.1 %collective-permute-start.7 = (bf16[16,2048]{1,0:T(8,128)(2,1)S(1)}, bf16[16,2048]{1,0:T(8,128)(2,1)S(1)}, u32[]{:S(2)}, u32[]{:S(2)}) collective-permute-start(bf16[16,2048]{1,0:T(8,128)(2,1)S(1)} %slice.34), channel_id=1, source_target_pairs={{4,0},{8,4},{12,8},{14,12},{10,14},{6,10},{2,6},{0,2},{5,1},{9,5},... | collective-permute-start | bytes 196616 | tf_op jit(solution)/shard_map/ppermute | solution.py:83
  31.7 0.9 %copy-start.4 = (bf16[16,4096]{1,0:T(8,128)(2,1)S(1)}, bf16[16,4096]{1,0:T(8,128)(2,1)}, u32[]{:S(2)}) copy-start(bf16[16,4096]{1,0:T(8,128)(2,1)} %copy-done.3) | copy-start | bytes 393220
  40.7 26.9 %copy-start.2 = (bf16[64,2048]{1,0:T(8,128)(2,1)S(1)}, bf16[64,2048]{1,0:T(8,128)(2,1)}, u32[]{:S(2)}) copy-start(bf16[64,2048]{1,0:T(8,128)(2,1)} %own_out.1) | copy-start | bytes 786436
  48.8 3.2 %collective-permute-start.17 = (f32[128,128]{1,0:T(8,128)S(1)}, f32[128,128]{1,0:T(8,128)S(1)}, u32[]{:S(2)}, u32[]{:S(2)}) collective-permute-start(f32[128,128]{1,0:T(8,128)S(1)} %get-tuple-element.18), channel_id=1, source_target_pairs={{0,2},{1,3},{2,0},{3,1},{4,6},{5,7},{6,4},{7,5},{8,10},{9,11},{10,... | collective-permute-start | bytes 196616 | tf_op jit(solution)/shard_map/ppermute | solution.py:317
  52.0 3.2 %collective-permute-start.18 = (f32[128,128]{1,0:T(8,128)S(1)}, f32[128,128]{1,0:T(8,128)S(1)}, u32[]{:S(2)}, u32[]{:S(2)}) collective-permute-start(f32[128,128]{1,0:T(8,128)S(1)} %add.38), channel_id=1, source_target_pairs={{0,4},{1,5},{2,6},{3,7},{4,0},{5,1},{6,2},{7,3},{8,12},{9,13},{10,... | collective-permute-start | bytes 196616 | tf_op jit(solution)/shard_map/ppermute | solution.py:317
  55.2 12.4 %collective-permute-start.19 = (f32[128,128]{1,0:T(8,128)S(1)}, f32[128,128]{1,0:T(8,128)S(1)}, u32[]{:S(2)}, u32[]{:S(2)}) collective-permute-start(f32[128,128]{1,0:T(8,128)S(1)} %add.39), channel_id=1, source_target_pairs={{0,9},{1,8},{2,11},{3,10},{4,13},{5,12},{6,15},{7,14},{8,1},{9,0},... | collective-permute-start | bytes 196616 | tf_op jit(solution)/shard_map/ppermute | solution.py:317
  68.6 2.0 %collective-permute-start.20 = (f32[64,2048]{1,0:T(8,128)S(1)}, f32[64,2048]{1,0:T(8,128)S(1)}, u32[]{:S(2)}, u32[]{:S(2)}) collective-permute-start(f32[64,2048]{1,0:T(8,128)S(1)} %get-tuple-element.20), channel_id=1, source_target_pairs={{0,1},{1,0},{2,3},{3,2},{4,5},{5,4},{6,7},{7,6},{8,9},{9,8},{10,11... | collective-permute-start | bytes 1572872 | tf_op jit(solution)/shard_map/ppermute | solution.py:321
  71.2 7.0 %collective-permute-start.21 = (bf16[4,4,2048]{2,1,0:T(4,128)(2,1)S(1)}, bf16[4,4,2048]{2,1,0:T(4,128)(2,1)S(1)}, u32[]{:S(2)}, u32[]{:S(2)}) collective-permute-start(bf16[4,4,2048]{2,1,0:T(4,128)(2,1)S(1)} %get-tuple-element.21), channel_id=1, source_target_pairs={{0,0},{1,8},{2,2},{3,10},{4,4},{5,12},{6,6},{7,14},{8,9},{9,1},{10... | collective-permute-start | bytes 196616 | tf_op jit(solution)/shard_map/ppermute | solution.py:330
  73.4 5.3 %collective-permute-start.22 = (bf16[4,4,2048]{2,1,0:T(4,128)(2,1)S(1)}, bf16[4,4,2048]{2,1,0:T(4,128)(2,1)S(1)}, u32[]{:S(2)}, u32[]{:S(2)}) collective-permute-start(bf16[4,4,2048]{2,1,0:T(4,128)(2,1)S(1)} %get-tuple-element.22), channel_id=1, source_target_pairs={{0,2},{1,10},{2,0},{3,8},{4,6},{5,14},{6,4},{7,12},{8,11},{9,3},{1... | collective-permute-start | bytes 196616 | tf_op jit(solution)/shard_map/ppermute | solution.py:330
  74.0 7.3 %collective-permute-start.23 = (bf16[4,4,2048]{2,1,0:T(4,128)(2,1)S(1)}, bf16[4,4,2048]{2,1,0:T(4,128)(2,1)S(1)}, u32[]{:S(2)}, u32[]{:S(2)}) collective-permute-start(bf16[4,4,2048]{2,1,0:T(4,128)(2,1)S(1)} %get-tuple-element.23), channel_id=1, source_target_pairs={{0,4},{1,12},{2,6},{3,14},{4,0},{5,8},{6,2},{7,10},{8,13},{9,5},{1... | collective-permute-start | bytes 196616 | tf_op jit(solution)/shard_map/ppermute | solution.py:330
  76.2 6.5 %collective-permute-start.24 = (bf16[4,4,2048]{2,1,0:T(4,128)(2,1)S(1)}, bf16[4,4,2048]{2,1,0:T(4,128)(2,1)S(1)}, u32[]{:S(2)}, u32[]{:S(2)}) collective-permute-start(bf16[4,4,2048]{2,1,0:T(4,128)(2,1)S(1)} %get-tuple-element.24), channel_id=1, source_target_pairs={{0,6},{1,14},{2,4},{3,12},{4,2},{5,10},{6,0},{7,8},{8,15},{9,7},{1... | collective-permute-start | bytes 196616 | tf_op jit(solution)/shard_map/ppermute | solution.py:330
  78.2 4.5 %copy-start.6 = (bf16[4,4,2048]{2,1,0:T(4,128)(2,1)}, bf16[4,4,2048]{2,1,0:T(4,128)(2,1)S(1)}, u32[]{:S(2)}) copy-start(bf16[4,4,2048]{2,1,0:T(4,128)(2,1)S(1)} %collective-permute-done.21.refs_0_) | copy-start | bytes 196612
  78.8 4.0 %copy-start.7 = (bf16[4,4,2048]{2,1,0:T(4,128)(2,1)}, bf16[4,4,2048]{2,1,0:T(4,128)(2,1)S(1)}, u32[]{:S(2)}) copy-start(bf16[4,4,2048]{2,1,0:T(4,128)(2,1)S(1)} %collective-permute-done.22.refs_1_) | copy-start | bytes 196612
  81.3 1.4 %copy-start.8 = (bf16[4,4,2048]{2,1,0:T(4,128)(2,1)}, bf16[4,4,2048]{2,1,0:T(4,128)(2,1)S(1)}, u32[]{:S(2)}) copy-start(bf16[4,4,2048]{2,1,0:T(4,128)(2,1)S(1)} %collective-permute-done.23.refs_2_) | copy-start | bytes 196612
  82.7 0.6 copy-start.9

commit v2 on v0

v2 whole, which is shorter than its diff:
```python
import functools
import math

import jax
import jax.numpy as jnp
import numpy as np
from jax import lax
from jax.experimental import pallas as pl
from jax.experimental.pallas import tpu as pltpu
from jax.sharding import PartitionSpec as P

adapter_scale = 2.0
chunk_count = 2
weight_edges = (0, 2, 5, 8, 12, 15, 16)
mebibyte = 1024 * 1024


def attend_kernel(
    lengths, queries, keys, values, fresh_keys, fresh_values, *refs
):
    outs, refs = refs[:chunk_count], refs[chunk_count:]
    query_held, key_held, value_held, fresh_key_held, fresh_value_held, key_wide, value_wide, gathered, sems = refs
    row_count, step_count, heads, head_width = query_held.shape
    old_rows, new_rows = key_held.shape[1], fresh_key_held.shape[1]
    groups = new_rows // step_count
    per_group = heads // groups
    slots = old_rows // groups
    columns = key_wide.shape[1] // groups
    rows = step_count * per_group
    exponent_scale = math.log2(math.e) / math.sqrt(head_width)

    fresh = [
        pltpu.make_async_copy(fresh_keys, fresh_key_held, sems.at[0]),
        pltpu.make_async_copy(queries, query_held, sems.at[1]),
        pltpu.make_async_copy(fresh_values, fresh_value_held, sems.at[2]),
    ]
    old_keys = [
        pltpu.make_async_copy(keys.at[row], key_held.at[row], sems.at[3 + row])
        for row in range(row_count)
    ]
    old_values = [
        pltpu.make_async_copy(values.at[row], value_held.at[row], sems.at[3 + row_count + row])
        for row in range(row_count)
    ]
    for copy in fresh:
        copy.start()
    for row in range(row_count):
        old_keys[row].start()
        old_values[row].start()
    for copy in fresh:
        copy.wait()

    column = lax.broadcasted_iota(jnp.int32, (step_count, 1, columns), 2)
    step = lax.broadcasted_iota(jnp.int32, (step_count, 1, columns), 0)
    fresh_seen = (column >= slots) & (column - slots <= step)

    def widen(old, new, wide):
        wide[:old_rows] = old.astype(jnp.float32)
        wide[old_rows : old_rows + new_rows] = new.astype(jnp.float32)
        wide[old_rows + new_rows :] = jnp.zeros_like(wide[old_rows + new_rows :])

    def picked(group):
        return pl.ds(group, columns, stride=groups)

    for row in range(row_count):
        old_keys[row].wait()
        widen(key_held[row], fresh_key_held[row], key_wide.at[row])
        bias = jnp.where((column < jnp.minimum(lengths[row], slots)) | fresh_seen, 0.0, -jnp.inf)
        scores = [
            lax.dot_general(
                query_held[row, :, group * per_group : (group + 1) * per_group, :].reshape(
                    rows, head_width
                ),
                key_wide[row, picked(group), :].astype(jnp.bfloat16),
                (((1,), (1,)), ((), ())),
                preferred_element_type=jnp.float32,
            ).reshape(step_count, per_group, columns)
            + bias
            for group in range(groups)
        ]
        old_values[row].wait()
        widen(value_held[row], fresh_value_held[row], value_wide.at[row])
        tops = [score.max(-1, keepdims=True) for score in scores]
        scores = [
            jnp.exp2((score - top) * exponent_scale) for score, top in zip(scores, tops)
        ]
        totals = [score.sum(-1, keepdims=True) for score in scores]
        weighted = [
            jnp.dot(
                score.astype(jnp.bfloat16).reshape(rows, columns),
                value_wide[row, picked(group), :].astype(jnp.bfloat16),
                preferred_element_type=jnp.float32,
            ).reshape(step_count, per_group, head_width)
            for group, score in enumerate(scores)
        ]
        for group in range(groups):
            result = weighted[group] / totals[group]
            for s in range(step_count):
                place = (row * step_count + s) * heads + group * per_group
                gathered[place : place + per_group, :] = result[s]
    each = heads // chunk_count
    for head in range(heads):
        place = head % each * head_width
        outs[head // each][:, place : place + head_width] = gathered[
            pl.ds(head, row_count * step_count, stride=heads), :
        ].astype(jnp.bfloat16)


def attend(lengths, queries, keys, values, fresh_keys, fresh_values):
    row_count, step_count, heads, head_width = queries.shape
    smem = pl.BlockSpec(memory_space=pltpu.SMEM)
    vmem = pl.BlockSpec(memory_space=pltpu.VMEM)
    anywhere = pl.BlockSpec(memory_space=pl.ANY)
    kind = jnp.bfloat16
    shape = (row_count * step_count, heads * head_width // chunk_count)
    groups = fresh_keys.shape[1] // step_count
    columns = -(-(keys.shape[1] + fresh_keys.shape[1]) // (16 * groups)) * 16
    wide = pltpu.VMEM((row_count, columns * groups, head_width), jnp.float32)
    return pl.pallas_call(
        attend_kernel,
        in_specs=[smem] + [anywhere] * 5,
        out_specs=[vmem] * chunk_count,
        out_shape=[jax.ShapeDtypeStruct(shape, kind)] * chunk_count,
        scratch_shapes=[
            pltpu.VMEM(queries.shape, kind),
            pltpu.VMEM(keys.shape, kind),
            pltpu.VMEM(values.shape, kind),
            pltpu.VMEM(fresh_keys.shape, kind),
            pltpu.VMEM(fresh_values.shape, kind),
            wide,
            wide,
            pltpu.VMEM((row_count * step_count * heads, head_width), jnp.float32),
            pltpu.SemaphoreType.DMA((3 + 2 * row_count,)),
        ],
        compiler_params=pltpu.CompilerParams(vmem_limit_bytes=58 * mebibyte),
        cost_estimate=pl.CostEstimate(
            flops=4 * row_count * step_count * heads * keys.shape[1] * head_width,
            bytes_accessed=4 * keys.size,
            transcendentals=row_count * step_count * heads * keys.shape[1],
        ),
        name="attend",
    )(lengths, queries, keys, values, fresh_keys, fresh_values)


def ring_order(count):
    inner = max(d for d in range(1, count + 1) if count % d == 0 and d * d <= count)
    outer = count // inner
    if inner == 1:
        return list(range(count))
    order = [z * inner for z in range(outer)]
    for turn, z in enumerate(reversed(range(outer))):
        columns = list(range(1, inner))
        if turn % 2:
            columns.reverse()
        order += [z * inner + c for c in columns]
    return order


def ring_step(blocks, step, order, chunk):
    count = len(order)
    up = [(order[i], order[(i + 1) % count]) for i in range(count)]
    down = [(b, a) for a, b in up]
    if step < count // 2 or chunk % 2 == 0:
        blocks[count - step] = lax.ppermute(blocks[(1 - step) % count], "fsdp", up)
    if step < count // 2 or chunk % 2 == 1:
        blocks[step] = lax.ppermute(blocks[step - 1], "fsdp", down)


def facts_table(count, own_width, width):
    order = ring_order(count)
    position = {f: i for i, f in enumerate(order)}
    half = count // 2
    rows = []
    for chip in range(count):
        for core in range(2):
            side, mine = chip // half, chip % half
            start = mine // 2 * 2 * own_width
            owner = start // width if core == side else -1
            places = [order[(position[chip] + i) % count] for i in range(count)]
            rows.append([core, core ^ side, mine, owner, start % width, chip % 2] + places)
    return np.array(rows, np.int32)


fact_core, fact_kept, fact_mine, fact_owner, fact_start, fact_odd, fact_places = range(7)


def collect(facts, blocks, held, columns):
    for offset, ref in enumerate(blocks):
        held[facts[fact_places + offset]] = ref[:, columns]


def rank_kernel(count, facts, *refs):
    chunks, refs = refs[: chunk_count * count], refs[chunk_count * count :]
    factors, (ranked, held, factor) = refs[:4], refs[4:]
    width = held.shape[2]
    half, each = factors[0].shape
    ranked[...] = jnp.zeros_like(ranked)
    for chunk in range(chunk_count):
        blocks = chunks[chunk * count : (chunk + 1) * count]

        @pl.when(facts[fact_owner] == chunk)
        def _():
            start = pl.multiple_of(facts[fact_start], 128)
            collect(facts, blocks, held, pl.ds(start, width))
            core, odd = facts[fact_core], facts[fact_odd]
            for index, ref in enumerate(factors):
                row = core ^ (index // 2)
                column = odd ^ (index % 2)
                factor[
                    pl.ds(pl.multiple_of(row * half, half), half),
                    pl.ds(pl.multiple_of(column * each, each), each),
                ] = ref[...]
            ranked[...] = lax.dot_general(
                held[...].reshape(-1, width),
                factor[...],
                (((1,), (1,)), ((), ())),
                preferred_element_type=jnp.float32,
            )


def rank_part(facts, gathered, factors):
    blocks = [x for chunk in gathered for x in chunk]
    count = len(gathered[0])
    block_rows = blocks[0].shape[0]
    half, each = factors[0].shape
    vmem = pl.BlockSpec(memory_space=pltpu.VMEM)
    return pl.pallas_call(
        functools.partial(rank_kernel, count),
        in_specs=[pl.BlockSpec(memory_space=pltpu.SMEM)] + [vmem] * (len(blocks) + 4),
        out_specs=vmem,
        out_shape=jax.ShapeDtypeStruct((count * block_rows, 2 * half), jnp.float32),
        scratch_shapes=[
            pltpu.VMEM((count, block_rows, 2 * each), jnp.bfloat16),
            pltpu.VMEM((2 * half, 2 * each), jnp.bfloat16),
        ],
        compiler_params=pltpu.CompilerParams(vmem_limit_bytes=8 * mebibyte),
        cost_estimate=pl.CostEstimate(
            flops=8 * count * block_rows * half * each, bytes_accessed=mebibyte, transcendentals=0
        ),
        name="rank_part",
    )(facts, *blocks, *factors)


def project_kernel(count, facts, *refs):
    chunks, refs = refs[: chunk_count * count], refs[chunk_count * count :]
    weight, keep, send, held, streamed, sems = refs
    width = held.shape[2]
    rows = held.shape[0] * held.shape[1]
    edges = [weight.shape[0] * i // 16 for i in weight_edges]
    copies = [
        pltpu.make_async_copy(
            weight.at[pl.ds(first, last - first), :],
            streamed.at[pl.ds(first, last - first), :],
            sems.at[i],
        )
        for i, (first, last) in enumerate(zip(edges, edges[1:]))
    ]
    for copy in copies:
        copy.start()
    total = None
    chunk = None
    for copy, first, last in zip(copies, edges, edges[1:]):
        if first // width != chunk:
            chunk = first // width
            collect(facts, chunks[chunk * count : (chunk + 1) * count], held, slice(None))
        copy.wait()
        start = first - chunk * width
        part = jnp.dot(
            held[:, :, start : start + last - first].reshape(rows, last - first),
            streamed[first:last, :],
            preferred_element_type=jnp.float32,
        )
        total = part if total is None else total + part
    kept = facts[fact_kept]
    top, bottom = total[: rows // 2], total[rows // 2 :]
    keep[...] = jnp.where(kept == 0, top, bottom)
    send[...] = jnp.where(kept == 0, bottom, top)


def project(facts, gathered, base_weight):
    blocks = [x for chunk in gathered for x in chunk]
    count = len(gathered[0])
    block_rows, width = blocks[0].shape
    columns = base_weight.shape[1]
    rows = count * block_rows
    vmem = pl.BlockSpec(memory_space=pltpu.VMEM)
    return pl.pallas_call(
        functools.partial(project_kernel, count),
        in_specs=[pl.BlockSpec(memory_space=pltpu.SMEM)] + [vmem] * len(blocks) + [pl.BlockSpec(memory_space=pl.ANY)],
        out_specs=[vmem] * 2,
        out_shape=[jax.ShapeDtypeStruct((rows // 2, columns), jnp.float32)] * 2,
        scratch_shapes=[
            pltpu.VMEM((count, block_rows, width), jnp.bfloat16),
            pltpu.VMEM(base_weight.shape, jnp.bfloat16),
            pltpu.SemaphoreType.DMA((len(weight_edges) - 1,)),
        ],
        compiler_params=pltpu.CompilerParams(vmem_limit_bytes=48 * mebibyte),
        cost_estimate=pl.CostEstimate(
            flops=2 * rows * chunk_count * width * columns,
            bytes_accessed=2 * chunk_count * width * columns,
            transcendentals=0,
        ),
        name="project",
    )(facts, *blocks, base_weight)


def add_kernel(a, b, out):
    out[...] = a[...] + b[...]


def add(a, b):
    vmem = pl.BlockSpec(memory_space=pltpu.VMEM)
    return pl.pallas_call(
        add_kernel,
        in_specs=[vmem] * 2,
        out_specs=vmem,
        out_shape=jax.ShapeDtypeStruct(a.shape, a.dtype),
        compiler_params=pltpu.CompilerParams(vmem_limit_bytes=4 * mebibyte),
        name="add",
    )(a, b)


def split_kernel(facts, a, b, keep, send):
    rows = keep.shape[0]
    total = a[...] + b[...]
    kept = facts[fact_kept]
    keep[...] = jnp.where(kept == 0, total[:rows], total[rows:])
    send[...] = jnp.where(kept == 0, total[rows:], total[:rows])


def split(facts, a, b):
    vmem = pl.BlockSpec(memory_space=pltpu.VMEM)
    return pl.pallas_call(
        split_kernel,
        in_specs=[pl.BlockSpec(memory_space=pltpu.SMEM)] + [vmem] * 2,
        out_specs=[vmem] * 2,
        out_shape=[jax.ShapeDtypeStruct((a.shape[0] // 2, a.shape[1]), a.dtype)] * 2,
        compiler_params=pltpu.CompilerParams(vmem_limit_bytes=4 * mebibyte),
        name="split",
    )(facts, a, b)


def finish_kernel(facts, keep, received, ranked, ranked_received, own, other, *refs):
    *outs, factor = refs
    half = own.shape[0]
    core = facts[fact_core]
    for part in range(2):
        base = 2 * half * part
        factor[pl.ds(pl.multiple_of(base + core * half, half), half), :] = own[...]
        factor[pl.ds(pl.multiple_of(base + (1 - core) * half, half), half), :] = other[...]
    scaled = adapter_scale * (ranked[...] + ranked_received[...])
    high = scaled.astype(jnp.bfloat16)
    low = (scaled - high.astype(jnp.float32)).astype(jnp.bfloat16)
    pair = jnp.concatenate([high, low], axis=1)
    added = jnp.dot(pair, factor[...], preferred_element_type=jnp.float32)
    total = (keep[...] + received[...] + added).astype(jnp.bfloat16)
    block = keep.shape[0] // len(outs)
    mine = facts[fact_mine]
    for index in range(len(outs)):
        for offset, out in enumerate(outs):

            @pl.when(mine ^ offset == index)
            def _():
                out[...] = total[index * block : (index + 1) * block].reshape(out.shape)


def finish(facts, keep, received, ranked, ranked_received, own, other, row_count, step_count):
    rows, columns = keep.shape
    pieces = rows // (row_count * step_count)
    vmem = pl.BlockSpec(memory_space=pltpu.VMEM)
    return pl.pallas_call(
        finish_kernel,
        in_specs=[pl.BlockSpec(memory_space=pltpu.SMEM)] + [vmem] * 6,
        out_specs=[vmem] * pieces,
        out_shape=[jax.ShapeDtypeStruct((row_count, step_count, columns), jnp.bfloat16)] * pieces,
        scratch_shapes=[pltpu.VMEM((4 * own.shape[0], columns), jnp.bfloat16)],
        compiler_params=pltpu.CompilerParams(vmem_limit_bytes=16 * mebibyte),
        name="finish",
    )(facts, keep, received, ranked, ranked_received, own, other)


def place_kernel(facts, *refs):
    *pieces, out, sems = refs
    mine = facts[fact_mine]
    copies = []
    for offset, ref in enumerate(pieces):
        width = ref.shape[2]
        columns = pl.ds(pl.multiple_of((mine ^ offset) * width, width), width)
        copies.append(pltpu.make_async_copy(ref, out.at[:, :, columns], sems.at[offset]))
    for copy in copies:
        copy.start()
    for copy in copies:
        copy.wait()


def place(facts, pieces):
    row_count, step_count, width = pieces[0].shape
    anywhere = pl.BlockSpec(memory_space=pl.ANY)
    return pl.pallas_call(
        place_kernel,
        in_specs=[pl.BlockSpec(memory_space=pltpu.SMEM)] + [anywhere] * len(pieces),
        out_specs=anywhere,
        out_shape=jax.ShapeDtypeStruct((row_count, step_count, width * len(pieces)), jnp.bfloat16),
        scratch_shapes=[pltpu.SemaphoreType.DMA((len(pieces),))],
        compiler_params=pltpu.CompilerParams(vmem_limit_bytes=4 * mebibyte),
        name="place",
    )(facts, *pieces)


def shards(
    count,
    queries,
    cache_keys,
    cache_values,
    new_keys,
    new_values,
    cache_lengths,
    base_weight,
    factor_in,
    adapter_output_factor,
):
    order = ring_order(count)
    half = count // 2
    both = ("fsdp", "tp")
    swap = [(0, 1), (1, 0)]
    after = lax.optimization_barrier
    row_count, step_count, head_count, head_width = queries.shape
    slots, key_heads = cache_keys.shape[1:3]
    own_width = factor_in.shape[0]
    width = head_count * head_width // chunk_count
    facts = lax.dynamic_index_in_dim(
        jnp.asarray(facts_table(count, own_width, width)),
        lax.axis_index(both).astype(jnp.int32),
        0,
        keepdims=False,
    )

    own_in, own_out = factor_in.T, adapter_output_factor
    near_in = lax.ppermute(own_in, "fsdp", [(f, f ^ 1) for f in range(count)])
    attended = attend(
        cache_lengths,
        queries,
        cache_keys.reshape(row_count, slots * key_heads, head_width),
        cache_values.reshape(row_count, slots * key_heads, head_width),
        new_keys.reshape(row_count, step_count * key_heads, head_width),
        new_values.reshape(row_count, step_count * key_heads, head_width),
    )
    attended, near_in, facts = after((attended, near_in, facts))
    gathered = [[x] * count for x in attended]
    for step in range(1, half + 1):
        for c, blocks in enumerate(gathered):
            ring_step(blocks, step, order, c)
        if step == 2:
            others = [lax.ppermute(x, "tp", swap) for x in (own_in, near_in, own_out)]
            gathered[0][count - 2], others = after((gathered[0][count - 2], others))
    other_in, other_near_in, other_out = others

    ranked = rank_part(facts, gathered, (own_in, near_in, other_in, other_near_in))
    bit, keep = 2, None
    while True:
        if bit < half:
            pairs = [(2 * f + f // half, 2 * (f ^ bit) + f // half) for f in range(count)]
        else:
            pairs = [(2 * f + f // half, 2 * (f ^ half) + f // half) for f in range(count)]
        received = lax.ppermute(ranked, both, pairs)
        if keep is None:
            keep, send = project(facts, gathered, base_weight)
            received, keep, send = after((received, keep, send))
        if bit >= half:
            break
        ranked = add(ranked, received)
        bit *= 2
    ranked_keep, ranked_send = split(facts, ranked, received)
    ranked_received = lax.ppermute(ranked_send, "tp", swap)
    received = lax.ppermute(send, "tp", swap)
    pieces = finish(
        facts, keep, received, ranked_keep, ranked_received, own_out, other_out, row_count, step_count
    )
    landed = []
    for offset, piece in enumerate(pieces):
        pairs = [
            (2 * f + t, 2 * (f ^ (t * half + offset)) + f // half)
            for f in range(count)
            for t in range(2)
        ]
        landed.append(lax.ppermute(piece, both, pairs))
    return place(facts, landed)


def solution(mesh):
    return jax.shard_map(
        functools.partial(shards, mesh.shape["fsdp"]),
        mesh=mesh,
        in_specs=(
            P(("groups", "fsdp"), None, "tp", None),
            P(("groups", "fsdp"), None, "tp", None),
            P(("groups", "fsdp"), None, "tp", None),
            P(("groups", "fsdp"), None, "tp", None),
            P(("groups", "fsdp"), None, "tp", None),
            P(("groups", "fsdp")),
            P("tp", "fsdp"),
            P(("groups", "fsdp"), "tp"),
            P(("groups", "tp"), "fsdp"),
        ),
        out_specs=P(("groups", "fsdp"), None, "tp"),
        check_vma=False,
    )
```

time: 205 us -> 76.5 us (0.37)
  waiting for transfers between devices: 129 us -> 22.3 us
  blocking collectives: 33.1 us -> 0 us
  starting transfers between devices: 0.09 us -> 29.7 us
  matrix products: 23.5 us -> 0 us
  Pallas kernels: 0 us -> 21.5 us
  between operations: 13.2 us -> 0.15 us
  other arithmetic: 2.76 us -> 0 us
    all_gather x2 -> x0, waiting for transfers between devices: 120 us -> none  [the longest x1 74 us: shards(): every_row = lax.all_gather(rank_all, 'fsdp', axis=0, tiled=True)]
    ppermute x0 -> x26, starting transfers between devices: none -> 29.7 us  [the longest x7 8.65 us: ring_step(): blocks[count - step] = lax.ppermute(blocks[(1 - step) % count], 'fsdp', up)]
    all_to_all x1 -> x0, blocking collectives: 28.5 us -> none  [shards(): lax.all_to_all(partial_value, 'fsdp', split_axis=0, concat_axis=1, tiled=...]
    dot_general x5 -> x0, matrix products: 23.5 us -> none  [the longest x1 18.6 us: shards(): jnp.dot(lax.all_gather(local_rows, 'fsdp', axis=0, tiled=True), combined_...]
    ppermute x0 -> x26, waiting for transfers between devices: none -> 22.3 us  [the longest x7 10.4 us: ring_step(): blocks[step] = lax.ppermute(blocks[step - 1], 'fsdp', down)]
    pallas_call x0 -> x7, Pallas kernels: none -> 21.5 us  [the longest x1 12 us: project(): pl.pallas_call(functools.partial(project_kernel, count), in_specs=[pl.Blo...]
    reduce_scatter x1 -> x0, waiting for transfers between devices: 9.3 us -> none  [shards(): summed = lax.psum_scatter(spread, 'tp', scatter_dimension=1, tiled=True)]
    all_gather x2 -> x0, blocking collectives: 4.63 us -> none  [the longest x1 2.31 us: shards(): lax.all_gather(adapter_output_factor, 'tp', axis=0, tiled=True)]
  transfers between devices with their start and end apart: 3 -> 26, of which waited for: 3 -> 14; matrix products, arithmetic and copies ran while one was open for 0% -> 1% of each run, Pallas kernels for 0% -> 25%
where the time goes in v2:
time: 76.5 us; the launch traced here: 76.2 us
  starting transfers between devices  29.7 us (39%)
  waiting for transfers between devices  22.3 us (29%)
  Pallas kernels  21.5 us (28%)
  local copies, waits for them, and re-layouts  2.52 us (3%)
    pallas_call x1, Pallas kernels, project(): pl.pallas_call(functools.partial(project_kernel, count), in_specs=[pl.Blo...  12 us
    ppermute x7, waiting for transfers between devices, ring_step(): blocks[step] = lax.ppermute(blocks[step - 1], 'fsdp', down)  10.4 us
    ppermute x7, starting transfers between devices, ring_step(): blocks[count - step] = lax.ppermute(blocks[(1 - step) % count], 'fsdp', up)  8.65 us
    ppermute x1, starting transfers between devices, shards(): received = lax.ppermute(send, 'tp', swap)  6.74 us
    ppermute x4, starting transfers between devices, shards(): landed.append(lax.ppermute(piece, both, pairs))  6.7 us
    pallas_call x1, Pallas kernels, attend(): pl.pallas_call(attend_kernel, in_specs=[smem] + [anywhere] * 5, out_specs...  6.15 us
    ppermute x2, waiting for transfers between devices, shards(): received = lax.ppermute(ranked, both, pairs)  5.19 us
    ppermute x4, waiting for transfers between devices, shards(): landed.append(lax.ppermute(piece, both, pairs))  4.11 us
  transfers between devices with their start and end apart: 26, of which 14 were waited for; matrix products, arithmetic and copies ran while one was open for 1% of the time, Pallas kernels for 25%

profile of v2, /device:TPU:1, one launch (start us, length us, event | category | flops | bytes accessed | tf_op | source)
XLA Modules:
  0.0 76.2 jit_solution(789354021461183210)
XLA Ops:
  0.0 2.1 %collective-permute-start = (bf16[64,2048]{1,0:T(8,128)(2,1)}, bf16[64,2048]{1,0:T(8,128)(2,1)S(1)}, u32[]{:S(2)}, u32[]{:S(2)}) collective-permute-start(bf16[64,2048]{1,0:T(8,128)(2,1)} %bitcast.7), channel_id=1, source_target_pairs={{0,2},{2,0},{4,6},{6,4},{8,10},{10,8},{12,14},{14,12},{1,3},{3,1},... | collective-permute-start | bytes 786440 | tf_op jit(solution)/shard_map/ppermute | solution.py:439
  2.1 1.0 %collective-permute-start.6 = (bf16[64,2048]{1,0:T(8,128)(2,1)}, bf16[64,2048]{1,0:T(8,128)(2,1)S(1)}, u32[]{:S(2)}, u32[]{:S(2)}) collective-permute-start(bf16[64,2048]{1,0:T(8,128)(2,1)} %bitcast.8), channel_id=1, source_target_pairs={{0,1},{1,0},{2,3},{3,2},{4,5},{5,4},{6,7},{7,6},{8,9},{9,8},{10,11... | collective-permute-start | bytes 786440 | tf_op jit(solution)/shard_map/ppermute | solution.py:454
  3.0 0.0 collective-permute-start.8
  3.0 6.2 %attend.1 = (bf16[16,4096]{1,0:T(8,128)(2,1)}, bf16[16,4096]{1,0:T(8,128)(2,1)}) custom-call(s32[4]{0:T(128)} %lengths.1, bf16[4,4,64,128]{3,2,1,0:T(8,128)(2,1)} %queries.1, bf16[4,2048,128]{2,1,0:T(8,128)(2,1)} %bitcast.10, bf16[4,2048,128]{2,1,0:T(8,128)(2,1)} %bitcast.11, bf16[4,16,128]{2,1,0:T(8,128)(2,1)} %bitcast.12, bf16[4,16,128]{2,1,0:T(8,128)(2,1)} %bitcast.13), custom_call_target="tpu_custom_call" | custom-call | flops 1073741824 | bytes 4194304 | tf_op jit(solution)/shard_map/attend/pallas_call | solution.py:119
  9.2 0.7 dynamic-slice_bitcast_fusion.facts
  9.9 0.0 collective-permute-done.refs_17_
  9.9 1.3 %collective-permute-start.4 = (bf16[16,4096]{1,0:T(8,128)(2,1)}, bf16[16,4096]{1,0:T(8,128)(2,1)S(1)}, u32[]{:S(2)}, u32[]{:S(2)}) collective-permute-start(bf16[16,4096]{1,0:T(8,128)(2,1)} %get-tuple-element.29.refs_0_), channel_id=1, source_target_pairs={{0,4},{4,8},{8,12},{12,14},{14,10},{10,6},{6,2},{2,0},{1,5},{5,9},... | collective-permute-start | bytes 393224 | tf_op jit(solution)/shard_map/ppermute | solution.py:164
  11.2 0.8 %collective-permute-start.7 = (bf16[64,2048]{1,0:T(8,128)(2,1)S(1)}, bf16[64,2048]{1,0:T(8,128)(2,1)S(1)}, u32[]{:S(2)}, u32[]{:S(2)}) collective-permute-start(bf16[64,2048]{1,0:T(8,128)(2,1)S(1)} %collective-permute-done.refs_17_), channel_id=1, source_target_pairs={{0,1},{1,0},{2,3},{3,2},{4,5},{5,4},{6,7},{7,6},{8,9},{9,8},{10,11... | collective-permute-start | bytes 786440 | tf_op jit(solution)/shard_map/ppermute | solution.py:454
  12.0 0.2 collective-permute-start.11
  12.2 0.0 collective-permute-done.6.refs_18_
  12.2 0.6 collective-permute-start.1
  12.8 0.0 collective-permute-done.8.other
  12.8 0.9 %collective-permute-start.15 = (bf16[16,4096]{1,0:T(8,128)(2,1)}, bf16[16,4096]{1,0:T(8,128)(2,1)S(1)}, u32[]{:S(2)}, u32[]{:S(2)}) collective-permute-start(bf16[16,4096]{1,0:T(8,128)(2,1)} %get-tuple-element.32.refs_8_), channel_id=1, source_target_pairs={{0,4},{4,8},{8,12},{12,14},{14,10},{10,6},{6,2},{2,0},{1,5},{5,9},... | collective-permute-start | bytes 393224 | tf_op jit(solution)/shard_map/ppermute | solution.py:164
  13.6 1.0 %collective-permute-done.4.refs_7_ = bf16[16,4096]{1,0:T(8,128)(2,1)S(1)} collective-permute-done((bf16[16,4096]{1,0:T(8,128)(2,1)}, bf16[16,4096]{1,0:T(8,128)(2,1)S(1)}, u32[]{:S(2)}, u32[]{:S(2)}) %collective-permute-start.4) | collective-permute-done | bytes 131104 | tf_op jit(solution)/shard_map/ppermute | solution.py:164
  14.7 1.3 %collective-permute-start.5 = (bf16[16,4096]{1,0:T(8,128)(2,1)S(1)}, bf16[16,4096]{1,0:T(8,128)(2,1)S(1)}, u32[]{:S(2)}, u32[]{:S(2)}) collective-permute-start(bf16[16,4096]{1,0:T(8,128)(2,1)S(1)} %collective-permute-done.4.refs_7_), channel_id=1, source_target_pairs={{0,4},{4,8},{8,12},{12,14},{14,10},{10,6},{6,2},{2,0},{1,5},{5,9},... | collective-permute-start | bytes 393224 | tf_op jit(solution)/shard_map/ppermute | solution.py:164
  16.0 1.4 %collective-permute-done.11.refs_9_ = bf16[16,4096]{1,0:T(8,128)(2,1)S(1)} collective-permute-done((bf16[16,4096]{1,0:T(8,128)(2,1)}, bf16[16,4096]{1,0:T(8,128)(2,1)S(1)}, u32[]{:S(2)}, u32[]{:S(2)}) %collective-permute-start.11) | collective-permute-done | bytes 131104 | tf_op jit(solution)/shard_map/ppermute | solution.py:166
  17.3 0.2 collective-permute-start.12
  17.5 2.6 %collective-permute-done.1.refs_1_ = bf16[16,4096]{1,0:T(8,128)(2,1)S(1)} collective-permute-done((bf16[16,4096]{1,0:T(8,128)(2,1)}, bf16[16,4096]{1,0:T(8,128)(2,1)S(1)}, u32[]{:S(2)}, u32[]{:S(2)}) %collective-permute-start.1) | collective-permute-done | bytes 131104 | tf_op jit(solution)/shard_map/ppermute | solution.py:166
  20.1 0.2 collective-permute-start.2
  20.3 0.0 collective-permute-done.15.refs_15_
  20.3 1.3 %collective-permute-start.16 = (bf16[16,4096]{1,0:T(8,128)(2,1)S(1)}, bf16[16,4096]{1,0:T(8,128)(2,1)S(1)}, u32[]{:S(2)}, u32[]{:S(2)}) collective-permute-start(bf16[16,4096]{1,0:T(8,128)(2,1)S(1)} %collective-permute-done.15.refs_15_), channel_id=1, source_target_pairs={{0,4},{4,8},{8,12},{12,14},{14,10},{10,6},{6,2},{2,0},{1,5},{5,9},... | collective-permute-start | bytes 393224 | tf_op jit(solution)/shard_map/ppermute | solution.py:164
  21.6 0.0 collective-permute-done.5.refs_6_
  21.6 0.0 collective-permute-done.7.refs_19_
  21.6 0.5 collective-permute-done.12.refs_10_
  22.1 0.2 collective-permute-start.13
  22.3 1.3 %collective-permute-start.9 = (bf16[16,4096]{1,0:T(8,128)(2,1)S(1)}, bf16[16,4096]{1,0:T(8,128)(2,1)S(1)}, u32[]{:S(2)}, u32[]{:S(2)}) collective-permute-start(bf16[16,4096]{1,0:T(8,128)(2,1)S(1)} %collective-permute-done.5.refs_6_), channel_id=1, source_target_pairs={{0,4},{4,8},{8,12},{12,14},{14,10},{10,6},{6,2},{2,0},{1,5},{5,9},... | collective-permute-start | bytes 393224 | tf_op jit(solution)/shard_map/ppermute | solution.py:164
  23.6 1.3 %collective-permute-done.2.refs_2_ = bf16[16,4096]{1,0:T(8,128)(2,1)S(1)} collective-permute-done((bf16[16,4096]{1,0:T(8,128)(2,1)S(1)}, bf16[16,4096]{1,0:T(8,128)(2,1)S(1)}, u32[]{:S(2)}, u32[]{:S(2)}) %collective-permute-start.2) | collective-permute-done | bytes 131104 | tf_op jit(solution)/shard_map/ppermute | solution.py:166
  24.9 0.2 collective-permute-start.3
  25.1 0.0 collective-permute-done.16.refs_14_
  25.1 1.3 %collective-permute-start.17 = (bf16[16,4096]{1,0:T(8,128)(2,1)S(1)}, bf16[16,4096]{1,0:T(8,128)(2,1)S(1)}, u32[]{:S(2)}, u32[]{:S(2)}) collective-permute-start(bf16[16,4096]{1,0:T(8,128)(2,1)S(1)} %collective-permute-done.16.refs_14_), channel_id=1, source_target_pairs={{0,4},{4,8},{8,12},{12,14},{14,10},{10,6},{6,2},{2,0},{1,5},{5,9},... | collective-permute-start | bytes 393224 | tf_op jit(solution)/shard_map/ppermute | solution.py:164
  26.4 1.3 %collective-permute-done.13.refs_11_ = bf16[16,4096]{1,0:T(8,128)(2,1)S(1)} collective-permute-done((bf16[16,4096]{1,0:T(8,128)(2,1)S(1)}, bf16[16,4096]{1,0:T(8,128)(2,1)S(1)}, u32[]{:S(2)}, u32[]{:S(2)}) %collective-permute-start.13) | collective-permute-done | bytes 131104 | tf_op jit(solution)/shard_map/ppermute | solution.py:166
  27.7 0.2 collective-permute-start.14
  27.8 0.0 collective-permute-done.9.refs_5_
  27.8 1.3 %collective-permute-start.10 = (bf16[16,4096]{1,0:T(8,128)(2,1)S(1)}, bf16[16,4096]{1,0:T(8,128)(2,1)S(1)}, u32[]{:S(2)}, u32[]{:S(2)}) collective-permute-start(bf16[16,4096]{1,0:T(8,128)(2,1)S(1)} %collective-permute-done.9.refs_5_), channel_id=1, source_target_pairs={{0,4},{4,8},{8,12},{12,14},{14,10},{10,6},{6,2},{2,0},{1,5},{5,9},... | collective-permute-start | bytes 393224 | tf_op jit(solution)/shard_map/ppermute | solution.py:164
  29.1 1.2 %collective-permute-done.3.refs_3_ = bf16[16,4096]{1,0:T(8,128)(2,1)S(1)} collective-permute-done((bf16[16,4096]{1,0:T(8,128)(2,1)S(1)}, bf16[16,4096]{1,0:T(8,128)(2,1)S(1)}, u32[]{:S(2)}, u32[]{:S(2)}) %collective-permute-start.3) | collective-permute-done | bytes 131104 | tf_op jit(solution)/shard_map/ppermute | solution.py:166
  30.4 0.3 collective-permute-done.17.refs_13_
  30.6 2.1 %collective-permute-done.14.refs_12_ = bf16[16,4096]{1,0:T(8,128)(2,1)S(1)} collective-permute-done((bf16[16,4096]{1,0:T(8,128)(2,1)S(1)}, bf16[16,4096]{1,0:T(8,128)(2,1)S(1)}, u32[]{:S(2)}, u32[]{:S(2)}) %collective-permute-start.14) | collective-permute-done | bytes 131104 | tf_op jit(solution)/shard_map/ppermute | solution.py:166
  32.7 0.0 collective-permute-done.10.refs_4_
  32.7 0.0 copy-done.5
  32.7 0.9 %copy-done = bf16[16,4096]{1,0:T(8,128)(2,1)S(1)} copy-done((bf16[16,4096]{1,0:T(8,128)(2,1)S(1)}, bf16[16,4096]{1,0:T(8,128)(2,1)}, u32[]{:S(2)}) %copy-start) | copy-done | bytes 131096
  33.6 0.9 %copy-done.2 = bf16[16,4096]{1,0:T(8,128)(2,1)S(1)} copy-done((bf16[16,4096]{1,0:T(8,128)(2,1)S(1)}, bf16[16,4096]{1,0:T(8,128)(2,1)}, u32[]{:S(2)}) %copy-start.2) | copy-done | bytes 131096
  34.6 0.6 rank_part.1.a
  35.1 0.0 copy-start.4
  35.1 0.8 %collective-permute-start.18 = (f32[128,128]{1,0:T(8,128)S(1)}, f32[128,128]{1,0:T(8,128)S(1)}, u32[]{:S(2)}, u32[]{:S(2)}) collective-permute-start(f32[128,128]{1,0:T(8,128)S(1)} %rank_part.1.a), channel_id=1, source_target_pairs={{0,4},{2,6},{4,0},{6,2},{9,13},{11,15},{13,9},{15,11},{16,20},{18,... | collective-permute-start | bytes 196616 | tf_op jit(solution)/shard_map/ppermute | solution.py:465
  36.0 12.0 %project.1 = (f32[64,2048]{1,0:T(8,128)S(1)}, f32[64,2048]{1,0:T(8,128)S(1)}) custom-call(s32[14]{0:T(128)S(1)} %dynamic-slice_bitcast_fusion.facts, bf16[16,4096]{1,0:T(8,128)(2,1)S(1)} %copy-done.1, bf16[16,4096]{1,0:T(8,128)(2,1)S(1)} %collective-permute-done.1.refs_1_, bf16[16,4096]{1,0:T(8,128)(2,1)S(1)} %collective-permute-done.2.refs_2_, ...), custom_call_target="tpu_custom_call" | custom-call | flops 4294967296 | bytes 33554432 | tf_op jit(solution)/shard_map/project/pallas_call | solution.py:287
  47.9 0.0 collective-permute-done.18.b
  47.9 6.7 %collective-permute-start.19 = (f32[64,2048]{1,0:T(8,128)S(1)}, f32[64,2048]{1,0:T(8,128)S(1)}, u32[]{:S(2)}, u32[]{:S(2)}) collective-permute-start(f32[64,2048]{1,0:T(8,128)S(1)} %get-tuple-element.38), channel_id=1, source_target_pairs={{0,1},{1,0},{2,3},{3,2},{4,5},{5,4},{6,7},{7,6},{8,9},{9,8},{10,11... | collective-permute-start | bytes 1572872 | tf_op jit(solution)/shard_map/ppermute | solution.py:475
  54.7 1.3 %collective-permute-start.20 = (f32[128,128]{1,0:T(8,128)S(1)}, f32[128,128]{1,0:T(8,128)S(1)}, u32[]{:S(2)}, u32[]{:S(2)}) collective-permute-start(f32[128,128]{1,0:T(8,128)S(1)} %add.10.a), channel_id=1, source_target_pairs={{0,8},{2,10},{4,12},{6,14},{9,1},{11,3},{13,5},{15,7},{16,24},{18,... | collective-permute-start | bytes 196616 | tf_op jit(solution)/shard_map/ppermute | solution.py:465
  56.0 5.2 %collective-permute-done.20.b = f32[128,128]{1,0:T(8,128)S(1)} collective-permute-done((f32[128,128]{1,0:T(8,128)S(1)}, f32[128,128]{1,0:T(8,128)S(1)}, u32[]{:S(2)}, u32[]{:S(2)}) %collective-permute-start.20) | collective-permute-done | bytes 65568 | tf_op jit(solution)/shard_map/ppermute | solution.py:465
  61.2 0.6 split.1
  61.8 0.1 collective-permute-start.21
  61.8 1.2 %collective-permute-done.21.ranked_received = f32[64,128]{1,0:T(8,128)S(1)} collective-permute-done((f32[64,128]{1,0:T(8,128)S(1)}, f32[64,128]{1,0:T(8,128)S(1)}, u32[]{:S(2)}, u32[]{:S(2)}) %collective-permute-start.21) | collective-permute-done | bytes 32800 | tf_op jit(solution)/shard_map/ppermute | solution.py:474
  63.0 0.0 collective-permute-done.19.received
  63.0 0.0 copy-done.4
  63.0 1.0 %finish.1 = (bf16[4,4,2048]{2,1,0:T(4,128)(2,1)S(1)}, bf16[4,4,2048]{2,1,0:T(4,128)(2,1)S(1)}, bf16[4,4,2048]{2,1,0:T(4,128)(2,1)S(1)}, bf16[4,4,2048]{2,1,0:T(4,128)(2,1)S(1)}) custom-call(s32[14]{0:T(128)S(1)} %dynamic-slice_bitcast_fusion.facts, f32[64,2048]{1,0:T(8,128)S(1)} %get-tuple-element.37.keep, f32[64,2048]{1,0:T(8,128)S(1)} %collective-permute-done.19.received, ...), custom_call_target="tpu_custom_call" | custom-call | tf_op jit(solution)/shard_map/finish/pallas_call | solution.py:371
  64.1 1.9 %collective-permute-start.22 = (bf16[4,4,2048]{2,1,0:T(4,128)(2,1)S(1)}, bf16[4,4,2048]{2,1,0:T(4,128)(2,1)S(1)}, u32[]{:S(2)}, u32[]{:S(2)}) collective-permute-start(bf16[4,4,2048]{2,1,0:T(4,128)(2,1)S(1)} %get-tuple-element.43), channel_id=1, source_target_pairs={{0,0},{1,8},{2,2},{3,10},{4,4},{5,12},{6,6},{7,14},{8,9},{9,1},{10... | collective-permute-start | bytes 196616 | tf_op jit(solution)/shard_map/ppermute | solution.py:486
  66.0 0.3 collective-permute-start.23
  66.3 2.3 %collective-permute-start.24 = (bf16[4,4,2048]{2,1,0:T(4,128)(2,1)S(1)}, bf16[4,4,2048]{2,1,0:T(4,128)(2,1)S(1)}, u32[]{:S(2)}, u32[]{:S(2)}) collective-permute-start(bf16[4,4,2048]{2,1,0:T(4,128)(2,1)S(1)} %get-tuple-element.45), channel_id=1, source_target_pairs={{0,4},{1,12},{2,6},{3,14},{4,0},{5,8},{6,2},{7,10},{8,13},{9,5},{1... | collective-permute-start | bytes 196616 | tf_op jit(solution)/shard_map/ppermute | solution.py:486
  68.7 2.1 %collective-permute-start.25 = (bf16[4,4,2048]{2,1,0:T(4,128)(2,1)S(1)}, bf16[4,4,2048]{2,1,0:T(4,128)(2,1)S(1)}, u32[]{:S(2)}, u32[]{:S(2)}) collective-permute-start(bf16[4,4,2048]{2,1,0:T(4,128)(2,1)S(1)} %get-tuple-element.46), channel_id=1, source_target_pairs={{0,6},{1,14},{2,4},{3,12},{4,2},{5,10},{6,0},{7,8},{8,15},{9,7},{1... | collective-permute-start | bytes 196616 | tf_op jit(solution)/shard_map/ppermute | solution.py:486
  70.8 0.0 collective-permute-done.22.refs_0_
  70.8 0.4 collective-permute-done.23.refs_1_
  71.2 1.9 %collective-permute-done.24.refs_2_ = bf16[4,4,2048]{2,1,0:T(4,128)(2,1)S(1)} collective-permute-done((bf16[4,4,2048]{2,1,0:T(4,128)(2,1)S(1)}, bf16[4,4,2048]{2,1,0:T(4,128)(2,1)S(1)}, u32[]{:S(2)}, u32[]{:S(2)}) %collective-permute-start.24) | collective-permute-done | bytes 65568 | tf_op jit(solution)/shard_map/ppermute | solution.py:486
  73.0 1.9 %collective-permute-done.25.refs_3_ = bf16[4,4,2048]{2,1,0:T(4,128)(2,1)S(1)} collective-permute-done((bf16[4,4,2048]{2,1,0:T(4,128)(2,1)S(1)}, bf16[4,4,2048]{2,1,0:T(4,128)(2,1)S(1)}, u32[]{:S(2)}, u32[]{:S(2)}) %collective-permute-start.25) | collective-permute-done | bytes 65568 | tf_op jit(solution)/shard_map/ppermute | solution.py:486
  74.9 1.3 %place.1 = bf16[4,4,8192]{2,1,0:T(4,128)(2,1)} custom-call(s32[14]{0:T(128)S(1)} %dynamic-slice_bitcast_fusion.facts, bf16[4,4,2048]{2,1,0:T(4,128)(2,1)S(1)} %collective-permute-done.22.refs_0_, bf16[4,4,2048]{2,1,0:T(4,128)(2,1)S(1)} %collective-permute-done.23.refs_1_, bf16[4,4,2048]{2,1,0:T(4,128)(2,1)S(1)} %collective-permute-done.24.refs_2_, ...), custom_call_target="tpu_custom_call" | custom-call | tf_op jit(solution)/shard_map/place/pallas_call | solution.py:399
  (8 shorter events, 0.0 us)
Async XLA Ops:
  0.0 9.9 %collective-permute-start = (bf16[64,2048]{1,0:T(8,128)(2,1)}, bf16[64,2048]{1,0:T(8,128)(2,1)S(1)}, u32[]{:S(2)}, u32[]{:S(2)}) collective-permute-start(bf16[64,2048]{1,0:T(8,128)(2,1)} %bitcast.7), channel_id=1, source_target_pairs={{0,2},{2,0},{4,6},{6,4},{8,10},{10,8},{12,14},{14,12},{1,3},{3,1},... | collective-permute-start | bytes 786440 | tf_op jit(solution)/shard_map/ppermute | solution.py:439
  2.1 10.1 %collective-permute-start.6 = (bf16[64,2048]{1,0:T(8,128)(2,1)}, bf16[64,2048]{1,0:T(8,128)(2,1)S(1)}, u32[]{:S(2)}, u32[]{:S(2)}) collective-permute-start(bf16[64,2048]{1,0:T(8,128)(2,1)} %bitcast.8), channel_id=1, source_target_pairs={{0,1},{1,0},{2,3},{3,2},{4,5},{5,4},{6,7},{7,6},{8,9},{9,8},{10,11... | collective-permute-start | bytes 786440 | tf_op jit(solution)/shard_map/ppermute | solution.py:454
  3.0 9.7 %collective-permute-start.8 = (bf16[64,2048]{1,0:T(8,128)(2,1)}, bf16[64,2048]{1,0:T(8,128)(2,1)S(1)}, u32[]{:S(2)}, u32[]{:S(2)}) collective-permute-start(bf16[64,2048]{1,0:T(8,128)(2,1)} %own.1), channel_id=1, source_target_pairs={{0,1},{1,0},{2,3},{3,2},{4,5},{5,4},{6,7},{7,6},{8,9},{9,8},{10,11... | collective-permute-start | bytes 786440 | tf_op jit(solution)/shard_map/ppermute | solution.py:454
  3.0 29.7 %copy-start.5 = (bf16[2048,64]{0,1:T(8,128)(2,1)S(1)}, bf16[2048,64]{0,1:T(8,128)(2,1)}, u32[]{:S(2)}) copy-start(bf16[2048,64]{0,1:T(8,128)(2,1)} %param.17) | copy-start | bytes 786436
  9.9 4.8 %collective-permute-start.4 = (bf16[16,4096]{1,0:T(8,128)(2,1)}, bf16[16,4096]{1,0:T(8,128)(2,1)S(1)}, u32[]{:S(2)}, u32[]{:S(2)}) collective-permute-start(bf16[16,4096]{1,0:T(8,128)(2,1)} %get-tuple-element.29.refs_0_), channel_id=1, source_target_pairs={{0,4},{4,8},{8,12},{12,14},{14,10},{10,6},{6,2},{2,0},{1,5},{5,9},... | collective-permute-start | bytes 393224 | tf_op jit(solution)/shard_map/ppermute | solution.py:164
  11.2 10.4 %collective-permute-start.7 = (bf16[64,2048]{1,0:T(8,128)(2,1)S(1)}, bf16[64,2048]{1,0:T(8,128)(2,1)S(1)}, u32[]{:S(2)}, u32[]{:S(2)}) collective-permute-start(bf16[64,2048]{1,0:T(8,128)(2,1)S(1)} %collective-permute-done.refs_17_), channel_id=1, source_target_pairs={{0,1},{1,0},{2,3},{3,2},{4,5},{5,4},{6,7},{7,6},{8,9},{9,8},{10,11... | collective-permute-start | bytes 786440 | tf_op jit(solution)/shard_map/ppermute | solution.py:454
  12.0 5.3 %collective-permute-start.11 = (bf16[16,4096]{1,0:T(8,128)(2,1)}, bf16[16,4096]{1,0:T(8,128)(2,1)S(1)}, u32[]{:S(2)}, u32[]{:S(2)}) collective-permute-start(bf16[16,4096]{1,0:T(8,128)(2,1)} %get-tuple-element.32.refs_8_), channel_id=1, source_target_pairs={{4,0},{8,4},{12,8},{14,12},{10,14},{6,10},{2,6},{0,2},{5,1},{9,5},... | collective-permute-start | bytes 393224 | tf_op jit(solution)/shard_map/ppermute | solution.py:166
  12.2 8.0 %collective-permute-start.1 = (bf16[16,4096]{1,0:T(8,128)(2,1)}, bf16[16,4096]{1,0:T(8,128)(2,1)S(1)}, u32[]{:S(2)}, u32[]{:S(2)}) collective-permute-start(bf16[16,4096]{1,0:T(8,128)(2,1)} %get-tuple-element.29.refs_0_), channel_id=1, source_target_pairs={{4,0},{8,4},{12,8},{14,12},{10,14},{6,10},{2,6},{0,2},{5,1},{9,5},... | collective-permute-start | bytes 393224 | tf_op jit(solution)/shard_map/ppermute | solution.py:166
  12.8 7.5 %collective-permute-start.15 = (bf16[16,4096]{1,0:T(8,128)(2,1)}, bf16[16,4096]{1,0:T(8,128)(2,1)S(1)}, u32[]{:S(2)}, u32[]{:S(2)}) collective-permute-start(bf16[16,4096]{1,0:T(8,128)(2,1)} %get-tuple-element.32.refs_8_), channel_id=1, source_target_pairs={{0,4},{4,8},{8,12},{12,14},{14,10},{10,6},{6,2},{2,0},{1,5},{5,9},... | collective-permute-start | bytes 393224 | tf_op jit(solution)/shard_map/ppermute | solution.py:164
  14.7 6.9 %collective-permute-start.5 = (bf16[16,4096]{1,0:T(8,128)(2,1)S(1)}, bf16[16,4096]{1,0:T(8,128)(2,1)S(1)}, u32[]{:S(2)}, u32[]{:S(2)}) collective-permute-start(bf16[16,4096]{1,0:T(8,128)(2,1)S(1)} %collective-permute-done.4.refs_7_), channel_id=1, source_target_pairs={{0,4},{4,8},{8,12},{12,14},{14,10},{10,6},{6,2},{2,0},{1,5},{5,9},... | collective-permute-start | bytes 393224 | tf_op jit(solution)/shard_map/ppermute | solution.py:164
  17.3 4.8 %collective-permute-start.12 = (bf16[16,4096]{1,0:T(8,128)(2,1)S(1)}, bf16[16,4096]{1,0:T(8,128)(2,1)S(1)}, u32[]{:S(2)}, u32[]{:S(2)}) collective-permute-start(bf16[16,4096]{1,0:T(8,128)(2,1)S(1)} %collective-permute-done.11.refs_9_), channel_id=1, source_target_pairs={{4,0},{8,4},{12,8},{14,12},{10,14},{6,10},{2,6},{0,2},{5,1},{9,5},... | collective-permute-start | bytes 393224 | tf_op jit(solution)/shard_map/ppermute | solution.py:166
  20.1 4.8 %collective-permute-start.2 = (bf16[16,4096]{1,0:T(8,128)(2,1)S(1)}, bf16[16,4096]{1,0:T(8,128)(2,1)S(1)}, u32[]{:S(2)}, u32[]{:S(2)}) collective-permute-start(bf16[16,4096]{1,0:T(8,128)(2,1)S(1)} %collective-permute-done.1.refs_1_), channel_id=1, source_target_pairs={{4,0},{8,4},{12,8},{14,12},{10,14},{6,10},{2,6},{0,2},{5,1},{9,5},... | collective-permute-start | bytes 393224 | tf_op jit(solution)/shard_map/ppermute | solution.py:166
  20.3 4.8 %collective-permute-start.16 = (bf16[16,4096]{1,0:T(8,128)(2,1)S(1)}, bf16[16,4096]{1,0:T(8,128)(2,1)S(1)}, u32[]{:S(2)}, u32[]{:S(2)}) collective-permute-start(bf16[16,4096]{1,0:T(8,128)(2,1)S(1)} %collective-permute-done.15.refs_15_), channel_id=1, source_target_pairs={{0,4},{4,8},{8,12},{12,14},{14,10},{10,6},{6,2},{2,0},{1,5},{5,9},... | collective-permute-start | bytes 393224 | tf_op jit(solution)/shard_map/ppermute | solution.py:164
  22.1 5.5 %collective-permute-start.13 = (bf16[16,4096]{1,0:T(8,128)(2,1)S(1)}, bf16[16,4096]{1,0:T(8,128)(2,1)S(1)}, u32[]{:S(2)}, u32[]{:S(2)}) collective-permute-start(bf16[16,4096]{1,0:T(8,128)(2,1)S(1)} %collective-permute-done.12.refs_10_), channel_id=1, source_target_pairs={{4,0},{8,4},{12,8},{14,12},{10,14},{6,10},{2,6},{0,2},{5,1},{9,5},... | collective-permute-start | bytes 393224 | tf_op jit(solution)/shard_map/ppermute | solution.py:166
  22.3 5.6 %collective-permute-start.9 = (bf16[16,4096]{1,0:T(8,128)(2,1)S(1)}, bf16[16,4096]{1,0:T(8,128)(2,1)S(1)}, u32[]{:S(2)}, u32[]{:S(2)}) collective-permute-start(bf16[16,4096]{1,0:T(8,128)(2,1)S(1)} %collective-permute-done.5.refs_6_), channel_id=1, source_target_pairs={{0,4},{4,8},{8,12},{12,14},{14,10},{10,6},{6,2},{2,0},{1,5},{5,9},... | collective-permute-start | bytes 393224 | tf_op jit(solution)/shard_map/ppermute | solution.py:164
  24.9 5.4 %collective-permute-start.3 = (bf16[16,4096]{1,0:T(8,128)(2,1)S(1)}, bf16[16,4096]{1,0:T(8,128)(2,1)S(1)}, u32[]{:S(2)}, u32[]{:S(2)}) collective-permute-start(bf16[16,4096]{1,0:T(8,128)(2,1)S(1)} %collective-permute-done.2.refs_2_), channel_id=1, source_target_pairs={{4,0},{8,4},{12,8},{14,12},{10,14},{6,10},{2,6},{0,2},{5,1},{9,5},... | collective-permute-start | bytes 393224 | tf_op jit(solution)/shard_map/ppermute | solution.py:166
  25.1 5.5 %collective-permute-start.17 = (bf16[16,4096]{1,0:T(8,128)(2,1)S(1)}, bf16[16,4096]{1,0:T(8,128)(2,1)S(1)}, u32[]{:S(2)}, u32[]{:S(2)}) collective-permute-start(bf16[16,4096]{1,0:T(8,128)(2,1)S(1)} %collective-permute-done.16.refs_14_), channel_id=1, source_target_pairs={{0,4},{4,8},{8,12},{12,14},{14,10},{10,6},{6,2},{2,0},{1,5},{5,9},... | collective-permute-start | bytes 393224 | tf_op jit(solution)/shard_map/ppermute | solution.py:164
  27.7 5.1 %collective-permute-start.14 = (bf16[16,4096]{1,0:T(8,128)(2,1)S(1)}, bf16[16,4096]{1,0:T(8,128)(2,1)S(1)}, u32[]{:S(2)}, u32[]{:S(2)}) collective-permute-start(bf16[16,4096]{1,0:T(8,128)(2,1)S(1)} %collective-permute-done.13.refs_11_), channel_id=1, source_target_pairs={{4,0},{8,4},{12,8},{14,12},{10,14},{6,10},{2,6},{0,2},{5,1},{9,5},... | collective-permute-start | bytes 393224 | tf_op jit(solution)/shard_map/ppermute | solution.py:166
  27.8 4.9 %collective-permute-start.10 = (bf16[16,4096]{1,0:T(8,128)(2,1)S(1)}, bf16[16,4096]{1,0:T(8,128)(2,1)S(1)}, u32[]{:S(2)}, u32[]{:S(2)}) collective-permute-start(bf16[16,4096]{1,0:T(8,128)(2,1)S(1)} %collective-permute-done.9.refs_5_), channel_id=1, source_target_pairs={{0,4},{4,8},{8,12},{12,14},{14,10},{10,6},{6,2},{2,0},{1,5},{5,9},... | collective-permute-start | bytes 393224 | tf_op jit(solution)/shard_map/ppermute | solution.py:164
  32.7 0.9 %copy-start = (bf16[16,4096]{1,0:T(8,128)(2,1)S(1)}, bf16[16,4096]{1,0:T(8,128)(2,1)}, u32[]{:S(2)}) copy-start(bf16[16,4096]{1,0:T(8,128)(2,1)} %get-tuple-element.29.refs_0_) | copy-start | bytes 393220
  33.6 0.9 %copy-start.2 = (bf16[16,4096]{1,0:T(8,128)(2,1)S(1)}, bf16[16,4096]{1,0:T(8,128)(2,1)}, u32[]{:S(2)}) copy-start(bf16[16,4096]{1,0:T(8,128)(2,1)} %get-tuple-element.32.refs_8_) | copy-start | bytes 393220
  34.6 1.4 %copy-start.1 = (bf16[16,4096]{1,0:T(8,128)(2,1)S(1)}, bf16[16,4096]{1,0:T(8,128)(2,1)}, u32[]{:S(2)}) copy-start(bf16[16,4096]{1,0:T(8,128)(2,1)} %get-tuple-element.29.refs_0_) | copy-start | bytes 393220
  34.6 1.4 %copy-start.3 = (bf16[16,4096]{1,0:T(8,128)(2,1)S(1)}, bf16[16,4096]{1,0:T(8,128)(2,1)}, u32[]{:S(2)}) copy-start(bf16[16,4096]{1,0:T(8,128)(2,1)} %get-tuple-element.32.refs_8_) | copy-start | bytes 393220
  35.1 27.9 %copy-start.4 = (bf16[64,2048]{1,0:T(8,128)(2,1)S(1)}, bf16[64,2048]{1,0:T(8,128)(2,1)}, u32[]{:S(2)}) copy-start(bf16[64,2048]{1,0:T(8,128)(2,1)} %own.1) | copy-start | bytes 786436
  35.1 12.8 %collective-permute-start.18 = (f32[128,128]{1,0:T(8,128)S(1)}, f32[128,128]{1,0:T(8,128)S(1)}, u32[]{:S(2)}, u32[]{:S(2)}) collective-permute-start(f32[128,128]{1,0:T(8,128)S(1)} %rank_part.1.a), channel_id=1, source_target_pairs={{0,4},{2,6},{4,0},{6,2},{9,13},{11,15},{13,9},{15,11},{16,20},{18,... | collective-permute-start | bytes 196616 | tf_op jit(solution)/shard_map/ppermute | solution.py:465
  47.9 15.1 %collective-permute-start.19 = (f32[64,2048]{1,0:T(8,128)S(1)}, f32[64,2048]{1,0:T(8,128)S(1)}, u32[]{:S(2)}, u32[]{:S(2)}) collective-permute-start(f32[64,2048]{1,0:T(8,128)S(1)} %get-tuple-element.38), channel_id=1, source_target_pairs={{0,1},{1,0},{2,3},{3,2},{4,5},{5,4},{6,7},{7,6},{8,9},{9,8},{10,11... | collective-permute-start | bytes 1572872 | tf_op jit(solution)/shard_map/ppermute | solution.py:475
  54.7 6.5 %collective-permute-start.20 = (f32[128,128]{1,0:T(8,128)S(1)}, f32[128,128]{1,0:T(8,128)S(1)}, u32[]{:S(2)}, u32[]{:S(2)}) collective-permute-start(f32[128,128]{1,0:T(8,128)S(1)} %add.10.a), channel_id=1, source_target_pairs={{0,8},{2,10},{4,12},{6,14},{9,1},{11,3},{13,5},{15,7},{16,24},{18,... | collective-permute-start | bytes 196616 | tf_op jit(solution)/shard_map/ppermute | solution.py:465
  61.8 1.3 %collective-permute-start.21 = (f32[64,128]{1,0:T(8,128)S(1)}, f32[64,128]{1,0:T(8,128)S(1)}, u32[]{:S(2)}, u32[]{:S(2)}) collective-permute-start(f32[64,128]{1,0:T(8,128)S(1)} %get-tuple-element.41), channel_id=1, source_target_pairs={{0,1},{1,0},{2,3},{3,2},{4,5},{5,4},{6,7},{7,6},{8,9},{9,8},{10,11... | collective-permute-start | bytes 98312 | tf_op jit(solution)/shard_map/ppermute | solution.py:474
  64.1 6.7 %collective-permute-start.22 = (bf16[4,4,2048]{2,1,0:T(4,128)(2,1)S(1)}, bf16[4,4,2048]{2,1,0:T(4,128)(2,1)S(1)}, u32[]{:S(2)}, u32[]{:S(2)}) collective-permute-start(bf16[4,4,2048]{2,1,0:T(4,128)(2,1)S(1)} %get-tuple-element.43), channel_id=1, source_target_pairs={{0,0},{1,8},{2,2},{3,10},{4,4},{5,12},{6,6},{7,14},{8,9},{9,1},{10... | collective-permute-start | bytes 196616 | tf_op jit(solution)/shard_map/ppermute | solution.py:486
  66.0 5.2 %collective-permute-start.23 = (bf16[4,4,2048]{2,1,0:T(4,128)(2,1)S(1)}, bf16[4,4,2048]{2,1,0:T(4,128)(2,1)S(1)}, u32[]{:S(2)}, u32[]{:S(2)}) collective-permute-start(bf16[4,4,2048]{2,1,0:T(4,128)(2,1)S(1)} %get-tuple-element.44), channel_id=1, source_target_pairs={{0,2},{1,10},{2,0},{3,8},{4,6},{5,14},{6,4},{7,12},{8,11},{9,3},{1... | collective-permute-start | bytes 196616 | tf_op jit(solution)/shard_map/ppermute | solution.py:486
  66.3 6.7 %collective-permute-start.24 = (bf16[4,4,2048]{2,1,0:T(4,128)(2,1)S(1)}, bf16[4,4,2048]{2,1,0:T(4,128)(2,1)S(1)}, u32[]{:S(2)}, u32[]{:S(2)}) collective-permute-start(bf16[4,4,2048]{2,1,0:T(4,128)(2,1)S(1)} %get-tuple-element.45), channel_id=1, source_target_pairs={{0,4},{1,12},{2,6},{3,14},{4,0},{5,8},{6,2},{7,10},{8,13},{9,5},{1... | collective-permute-start | bytes 196616 | tf_op jit(solution)/shard_map/ppermute | solution.py:486
  68.7 6.2 %collective-permute-start.25 = (bf16[4,4,2048]{2,1,0:T(4,128)(2,1)S(1)}, bf16[4,4,2048]{2,1,0:T(4,128)(2,1)S(1)}, u32[]{:S(2)}, u32[]{:S(2)}) collective-permute-start(bf16[4,4,2048]{2,1,0:T(4,128)(2,1)S(1)} %get-tuple-element.46), channel_id=1, source_target_pairs={{0,6},{1,14},{2,4},{3,12},{4,2},{5,10},{6,0},{7,8},{8,15},{9,7},{1... | collective-permute-start | bytes 196616 | tf_op jit(solution)/shard_map/ppermute | solution.py:486

commit v3 on v2

--- a/solution.py
+++ b/solution.py
@@ -11,7 +11,9 @@
 
 adapter_scale = 2.0
 chunk_count = 2
-weight_edges = (0, 2, 5, 8, 12, 15, 16)
+fetched = 64
+staged_rows = 2
+weight_edges = (0, 3, 8, 13, 16)
 mebibyte = 1024 * 1024
 
 
@@ -44,7 +46,7 @@
     ]
     for copy in fresh:
         copy.start()
-    for row in range(row_count):
+    for row in range(min(staged_rows, row_count)):
         old_keys[row].start()
         old_values[row].start()
     for copy in fresh:
@@ -79,6 +81,9 @@
             for group in range(groups)
         ]
         old_values[row].wait()
+        if row + staged_rows < row_count:
+            old_keys[row + staged_rows].start()
+            old_values[row + staged_rows].start()
         widen(value_held[row], fresh_value_held[row], value_wide.at[row])
         tops = [score.max(-1, keepdims=True) for score in scores]
         scores = [
@@ -184,14 +189,49 @@
 fact_core, fact_kept, fact_mine, fact_owner, fact_start, fact_odd, fact_places = range(7)
 
 
-def collect(facts, blocks, held, columns):
-    for offset, ref in enumerate(blocks):
-        held[facts[fact_places + offset]] = ref[:, columns]
-
-
-def rank_kernel(count, facts, *refs):
+def collect(facts, blocks, held, columns, sem):
+    own = pltpu.make_async_copy(blocks[0].at[:, columns], held.at[facts[fact_places]], sem)
+    own.start()
+    for offset, ref in enumerate(blocks[1:]):
+        held[facts[fact_places + 1 + offset]] = ref[:, columns]
+    own.wait()
+
+
+def block_specs(count):
+    vmem = pl.BlockSpec(memory_space=pltpu.VMEM)
+    return [pl.BlockSpec(memory_space=pl.ANY)] + [vmem] * (count - 1)
+
+
+def fetch_kernel(weight, *refs):
+    out, token, sem = refs[-3:]
+    copy = pltpu.make_async_copy(weight.at[pl.ds(0, out.shape[0]), :], out, sem)
+    copy.start()
+    token[...] = jnp.zeros_like(token)
+    copy.wait()
+
+
+def fetch(base_weight, after):
+    rows, columns = base_weight.shape
+    vmem = pl.BlockSpec(memory_space=pltpu.VMEM)
+    rows = rows * fetched // 256
+    return pl.pallas_call(
+        fetch_kernel,
+        in_specs=[pl.BlockSpec(memory_space=pl.ANY)] * (1 + len(after)),
+        out_specs=[vmem] * 2,
+        out_shape=[
+            jax.ShapeDtypeStruct((rows, columns), base_weight.dtype),
+            jax.ShapeDtypeStruct((8, 128), jnp.float32),
+        ],
+        scratch_shapes=[pltpu.SemaphoreType.DMA(())],
+        compiler_params=pltpu.CompilerParams(vmem_limit_bytes=24 * mebibyte),
+        cost_estimate=pl.CostEstimate(flops=0, bytes_accessed=4 * rows * columns, transcendentals=0),
+        name="fetch",
+    )(base_weight, *after)
+
+
+def rank_kernel(count, facts, _, *refs):
     chunks, refs = refs[: chunk_count * count], refs[chunk_count * count :]
-    factors, (ranked, held, factor) = refs[:4], refs[4:]
+    factors, (ranked, held, factor, sem) = refs[:4], refs[4:]
     width = held.shape[2]
     half, each = factors[0].shape
     ranked[...] = jnp.zeros_like(ranked)
@@ -201,7 +241,7 @@
         @pl.when(facts[fact_owner] == chunk)
         def _():
             start = pl.multiple_of(facts[fact_start], 128)
-            collect(facts, blocks, held, pl.ds(start, width))
+            collect(facts, blocks, held, pl.ds(start, width), sem)
             core, odd = facts[fact_core], facts[fact_odd]
             for index, ref in enumerate(factors):
                 row = core ^ (index // 2)
@@ -218,7 +258,7 @@
             )
 
 
-def rank_part(facts, gathered, factors):
+def rank_part(facts, token, gathered, factors):
     blocks = [x for chunk in gathered for x in chunk]
     count = len(gathered[0])
     block_rows = blocks[0].shape[0]
@@ -226,82 +266,100 @@
     vmem = pl.BlockSpec(memory_space=pltpu.VMEM)
     return pl.pallas_call(
         functools.partial(rank_kernel, count),
-        in_specs=[pl.BlockSpec(memory_space=pltpu.SMEM)] + [vmem] * (len(blocks) + 4),
+        in_specs=[pl.BlockSpec(memory_space=pltpu.SMEM), pl.BlockSpec(memory_space=pl.ANY)]
+        + block_specs(count) * chunk_count
+        + [vmem] * 4,
         out_specs=vmem,
         out_shape=jax.ShapeDtypeStruct((count * block_rows, 2 * half), jnp.float32),
         scratch_shapes=[
             pltpu.VMEM((count, block_rows, 2 * each), jnp.bfloat16),
             pltpu.VMEM((2 * half, 2 * each), jnp.bfloat16),
+            pltpu.SemaphoreType.DMA(()),
         ],
-        compiler_params=pltpu.CompilerParams(vmem_limit_bytes=8 * mebibyte),
+        compiler_params=pltpu.CompilerParams(vmem_limit_bytes=47 * mebibyte),
         cost_estimate=pl.CostEstimate(
             flops=8 * count * block_rows * half * each, bytes_accessed=mebibyte, transcendentals=0
         ),
         name="rank_part",
-    )(facts, *blocks, *factors)
-
-
-def project_kernel(count, facts, *refs):
-    chunks, refs = refs[: chunk_count * count], refs[chunk_count * count :]
-    weight, keep, send, held, streamed, sems = refs
+    )(facts, token, *blocks, *factors)
+
+
+def project_kernel(chunk, facts, *refs):
+    refs = list(refs)
+    held, streamed, sem, sems = refs[-4:]
+    last = chunk == chunk_count - 1
+    outs = refs[-5 - last : -4]
+    refs = refs[: -5 - last]
+    previous = refs.pop() if chunk else None
+    weight = refs.pop()
+    ready = None if chunk else refs.pop()
     width = held.shape[2]
     rows = held.shape[0] * held.shape[1]
-    edges = [weight.shape[0] * i // 16 for i in weight_edges]
+    skipped = 0 if chunk else ready.shape[0]
+    edges = [skipped + (width - skipped) * i // 16 for i in weight_edges]
     copies = [
         pltpu.make_async_copy(
-            weight.at[pl.ds(first, last - first), :],
-            streamed.at[pl.ds(first, last - first), :],
+            weight.at[pl.ds(chunk * width + start, stop - start), :],
+            streamed.at[pl.ds(start - skipped, stop - start), :],
             sems.at[i],
         )
-        for i, (first, last) in enumerate(zip(edges, edges[1:]))
+        for i, (start, stop) in enumerate(zip(edges, edges[1:]))
     ]
     for copy in copies:
         copy.start()
-    total = None
-    chunk = None
-    for copy, first, last in zip(copies, edges, edges[1:]):
-        if first // width != chunk:
-            chunk = first // width
-            collect(facts, chunks[chunk * count : (chunk + 1) * count], held, slice(None))
-        copy.wait()
-        start = first - chunk * width
-        part = jnp.dot(
-            held[:, :, start : start + last - first].reshape(rows, last - first),
-            streamed[first:last, :],
+    collect(facts, refs, held, slice(None), sem)
+
+    def product(start, stop, factor):
+        return jnp.dot(
+            held[:, :, start:stop].reshape(rows, stop - start),
+            factor,
             preferred_element_type=jnp.float32,
         )
-        total = part if total is None else total + part
+
+    total = previous[...] if chunk else product(0, skipped, ready[...])
+    for copy, start, stop in zip(copies, edges, edges[1:]):
+        copy.wait()
+        total += product(start, stop, streamed[start - skipped : stop - skipped, :])
+    if not last:
+        outs[0][...] = total
+        return
+    keep, send = outs
     kept = facts[fact_kept]
     top, bottom = total[: rows // 2], total[rows // 2 :]
     keep[...] = jnp.where(kept == 0, top, bottom)
     send[...] = jnp.where(kept == 0, bottom, top)
 
 
-def project(facts, gathered, base_weight):
-    blocks = [x for chunk in gathered for x in chunk]
-    count = len(gathered[0])
+def project(chunk, facts, blocks, ready, base_weight, previous):
+    count = len(blocks)
     block_rows, width = blocks[0].shape
     columns = base_weight.shape[1]
     rows = count * block_rows
-    vmem = pl.BlockSpec(memory_space=pltpu.VMEM)
-    return pl.pallas_call(
-        functools.partial(project_kernel, count),
-        in_specs=[pl.BlockSpec(memory_space=pltpu.SMEM)] + [vmem] * len(blocks) + [pl.BlockSpec(memory_space=pl.ANY)],
-        out_specs=[vmem] * 2,
-        out_shape=[jax.ShapeDtypeStruct((rows // 2, columns), jnp.float32)] * 2,
+    last = chunk == chunk_count - 1
+    vmem = pl.BlockSpec(memory_space=pltpu.VMEM)
+    anywhere = pl.BlockSpec(memory_space=pl.ANY)
+    result = pl.pallas_call(
+        functools.partial(project_kernel, chunk),
+        in_specs=[pl.BlockSpec(memory_space=pltpu.SMEM)]
+        + block_specs(count)
+        + [vmem] * (chunk == 0)
+        + [anywhere]
+        + [vmem] * (chunk > 0),
+        out_specs=[vmem] * (1 + last),
+        out_shape=[jax.ShapeDtypeStruct((rows // (1 + last), columns), jnp.float32)] * (1 + last),
         scratch_shapes=[
             pltpu.VMEM((count, block_rows, width), jnp.bfloat16),
-            pltpu.VMEM(base_weight.shape, jnp.bfloat16),
+            pltpu.VMEM((width if chunk else width - ready.shape[0], columns), jnp.bfloat16),
+            pltpu.SemaphoreType.DMA(()),
             pltpu.SemaphoreType.DMA((len(weight_edges) - 1,)),
         ],
-        compiler_params=pltpu.CompilerParams(vmem_limit_bytes=48 * mebibyte),
+        compiler_params=pltpu.CompilerParams(vmem_limit_bytes=(32 if chunk else 26) * mebibyte),
         cost_estimate=pl.CostEstimate(
-            flops=2 * rows * chunk_count * width * columns,
-            bytes_accessed=2 * chunk_count * width * columns,
-            transcendentals=0,
+            flops=2 * rows * width * columns, bytes_accessed=2 * width * columns, transcendentals=0
         ),
-        name="project",
-    )(facts, *blocks, base_weight)
+        name=f"project_{chunk}",
+    )(facts, *blocks, *([] if chunk else [ready]), base_weight, *([previous] if chunk else []))
+    return result if last else result[0]
 
 
 def add_kernel(a, b, out):
@@ -445,7 +503,7 @@
         new_keys.reshape(row_count, step_count * key_heads, head_width),
         new_values.reshape(row_count, step_count * key_heads, head_width),
     )
-    attended, near_in, facts = after((attended, near_in, facts))
+    attended, near_in = after((attended, near_in))
     gathered = [[x] * count for x in attended]
     for step in range(1, half + 1):
         for c, blocks in enumerate(gathered):
@@ -454,22 +512,26 @@
             others = [lax.ppermute(x, "tp", swap) for x in (own_in, near_in, own_out)]
             gathered[0][count - 2], others = after((gathered[0][count - 2], others))
     other_in, other_near_in, other_out = others
-
-    ranked = rank_part(facts, gathered, (own_in, near_in, other_in, other_near_in))
-    bit, keep = 2, None
+    sent = [blocks[i] for blocks in gathered for i in (half - 1, half + 1)]
+    ready, token = fetch(base_weight, sent)
+    gathered[-1][half], token = after((gathered[-1][half], token))
+
+    ranked = rank_part(facts, token, gathered, (own_in, near_in, other_in, other_near_in))
+    bit, done, state = 2, 0, None
     while True:
-        if bit < half:
-            pairs = [(2 * f + f // half, 2 * (f ^ bit) + f // half) for f in range(count)]
-        else:
-            pairs = [(2 * f + f // half, 2 * (f ^ half) + f // half) for f in range(count)]
+        last = bit >= half
+        turn = half if last else bit
+        pairs = [(2 * f + f // half, 2 * (f ^ turn) + f // half) for f in range(count)]
         received = lax.ppermute(ranked, both, pairs)
-        if keep is None:
-            keep, send = project(facts, gathered, base_weight)
-            received, keep, send = after((received, keep, send))
-        if bit >= half:
+        while done < (chunk_count if last else 1):
+            state = project(done, facts, gathered[done], ready, base_weight, state)
+            done += 1
+        received, state = after((received, state))
+        if last:
             break
         ranked = add(ranked, received)
         bit *= 2
+    keep, send = state
     ranked_keep, ranked_send = split(facts, ranked, received)
     ranked_received = lax.ppermute(ranked_send, "tp", swap)
     received = lax.ppermute(send, "tp", swap)

time: 76.5 us -> 70.9 us (0.927)
  waiting for transfers between devices: 22.3 us -> 15.1 us
  Pallas kernels: 21.5 us -> 24.7 us
  local copies, waits for them, and re-layouts: 2.52 us -> 0.71 us
    ppermute x2, waiting for transfers between devices: 5.19 us -> 0.41 us  [shards(): received = lax.ppermute(ranked, both, pairs)]
    ppermute x7, waiting for transfers between devices: 10.4 us -> 6.02 us  [ring_step(): blocks[step] = lax.ppermute(blocks[step - 1], 'fsdp', down)]
    pallas_call x1 -> x3, Pallas kernels: 12 us -> 15.2 us  [the longest x2 11.8 us: project(): pl.pallas_call(functools.partial(project_kernel, chunk), in_specs=[pl.Blo...]
    unnamed x12 -> x8, local copies, waits for them, and re-layouts: 1.82 us -> 0.02 us
    ppermute x4, waiting for transfers between devices: 4.11 us -> 5.36 us  [shards(): landed.append(lax.ppermute(piece, both, pairs))]
    ppermute x7, waiting for transfers between devices: 1.31 us -> 2.11 us  [ring_step(): blocks[count - step] = lax.ppermute(blocks[(1 - step) % count], 'fsdp', up)]
  transfers between devices with their start and end apart: 26 -> 26, of which waited for: 14 -> 10; matrix products, arithmetic and copies ran while one was open for 1% -> 1% of each run, Pallas kernels for 25% -> 31%
where the time goes in v3:
time: 70.9 us; the launch traced here: 70.6 us
  starting transfers between devices  30 us (42%)
  Pallas kernels  24.7 us (35%)
  waiting for transfers between devices  15.1 us (21%)
  local copies, waits for them, and re-layouts  0.71 us (1%)
    pallas_call x2, Pallas kernels, project(): pl.pallas_call(functools.partial(project_kernel, chunk), in_specs=[pl.Blo...  11.8 us
    ppermute x7, starting transfers between devices, ring_step(): blocks[count - step] = lax.ppermute(blocks[(1 - step) % count], 'fsdp', up)  8.99 us
    ppermute x4, starting transfers between devices, shards(): landed.append(lax.ppermute(piece, both, pairs))  7.22 us
    ppermute x1, starting transfers between devices, shards(): received = lax.ppermute(send, 'tp', swap)  6.22 us
    pallas_call x1, Pallas kernels, attend(): pl.pallas_call(attend_kernel, in_specs=[smem] + [anywhere] * 5, out_specs...  6.03 us
    ppermute x7, waiting for transfers between devices, ring_step(): blocks[step] = lax.ppermute(blocks[step - 1], 'fsdp', down)  6.02 us
    ppermute x4, waiting for transfers between devices, shards(): landed.append(lax.ppermute(piece, both, pairs))  5.36 us
    pallas_call x1, Pallas kernels, fetch(): pl.pallas_call(fetch_kernel, in_specs=[pl.BlockSpec(memory_space=pl.ANY)]...  3.39 us
  transfers between devices with their start and end apart: 26, of which 10 were waited for; matrix products, arithmetic and copies ran while one was open for 1% of the time, Pallas kernels for 31%

profile of v3, /device:TPU:1, one launch (start us, length us, event | category | flops | bytes accessed | tf_op | source)
XLA Modules:
  0.0 70.6 jit_solution(4388265377392989685)
XLA Ops:
  0.0 2.1 %collective-permute-start = (bf16[64,2048]{1,0:T(8,128)(2,1)}, bf16[64,2048]{1,0:T(8,128)(2,1)S(1)}, u32[]{:S(2)}, u32[]{:S(2)}) collective-permute-start(bf16[64,2048]{1,0:T(8,128)(2,1)} %bitcast.7), channel_id=1, source_target_pairs={{0,2},{2,0},{4,6},{6,4},{8,10},{10,8},{12,14},{14,12},{1,3},{3,1},... | collective-permute-start | bytes 786440 | tf_op jit(solution)/shard_map/ppermute | solution.py:497
  2.1 1.0 %collective-permute-start.10 = (bf16[64,2048]{1,0:T(8,128)(2,1)}, bf16[64,2048]{1,0:T(8,128)(2,1)S(1)}, u32[]{:S(2)}, u32[]{:S(2)}) collective-permute-start(bf16[64,2048]{1,0:T(8,128)(2,1)} %bitcast.8), channel_id=1, source_target_pairs={{0,1},{1,0},{2,3},{3,2},{4,5},{5,4},{6,7},{7,6},{8,9},{9,8},{10,11... | collective-permute-start | bytes 786440 | tf_op jit(solution)/shard_map/ppermute | solution.py:512
  3.0 0.0 collective-permute-start.12
  3.0 6.0 %attend.1 = (bf16[16,4096]{1,0:T(8,128)(2,1)}, bf16[16,4096]{1,0:T(8,128)(2,1)}) custom-call(s32[4]{0:T(128)} %lengths.1, bf16[4,4,64,128]{3,2,1,0:T(8,128)(2,1)} %queries.1, bf16[4,2048,128]{2,1,0:T(8,128)(2,1)} %bitcast.10, bf16[4,2048,128]{2,1,0:T(8,128)(2,1)} %bitcast.11, bf16[4,16,128]{2,1,0:T(8,128)(2,1)} %bitcast.12, bf16[4,16,128]{2,1,0:T(8,128)(2,1)} %bitcast.13), custom_call_target="tpu_custom_call" | custom-call | flops 1073741824 | bytes 4194304 | tf_op jit(solution)/shard_map/attend/pallas_call | solution.py:124
  9.1 0.0 collective-permute-done.refs_17_
  9.1 0.4 collective-permute-start.1
  9.5 1.1 %collective-permute-start.8 = (bf16[16,4096]{1,0:T(8,128)(2,1)}, bf16[16,4096]{1,0:T(8,128)(2,1)S(1)}, u32[]{:S(2)}, u32[]{:S(2)}) collective-permute-start(bf16[16,4096]{1,0:T(8,128)(2,1)} %get-tuple-element.34.refs_0_), channel_id=1, source_target_pairs={{0,4},{4,8},{8,12},{12,14},{14,10},{10,6},{6,2},{2,0},{1,5},{5,9},... | collective-permute-start | bytes 393224 | tf_op jit(solution)/shard_map/ppermute | solution.py:169
  10.6 1.1 %collective-permute-start.11 = (bf16[64,2048]{1,0:T(8,128)(2,1)S(1)}, bf16[64,2048]{1,0:T(8,128)(2,1)S(1)}, u32[]{:S(2)}, u32[]{:S(2)}) collective-permute-start(bf16[64,2048]{1,0:T(8,128)(2,1)S(1)} %collective-permute-done.refs_17_), channel_id=1, source_target_pairs={{0,1},{1,0},{2,3},{3,2},{4,5},{5,4},{6,7},{7,6},{8,9},{9,8},{10,11... | collective-permute-start | bytes 786440 | tf_op jit(solution)/shard_map/ppermute | solution.py:512
  11.7 0.0 collective-permute-done.10.refs_18_
  11.7 1.4 %collective-permute-start.14 = (bf16[16,4096]{1,0:T(8,128)(2,1)}, bf16[16,4096]{1,0:T(8,128)(2,1)S(1)}, u32[]{:S(2)}, u32[]{:S(2)}) collective-permute-start(bf16[16,4096]{1,0:T(8,128)(2,1)} %get-tuple-element.33.refs_8_.refs_0_), channel_id=1, source_target_pairs={{0,4},{4,8},{8,12},{12,14},{14,10},{10,6},{6,2},{2,0},{1,5},{5,9},... | collective-permute-start | bytes 393224 | tf_op jit(solution)/shard_map/ppermute | solution.py:169
  13.1 0.0 collective-permute-done.12.other
  13.1 0.0 collective-permute-start.5
  13.1 0.8 %collective-permute-done.1.refs_9_.refs_1_ = bf16[16,4096]{1,0:T(8,128)(2,1)S(1)} collective-permute-done((bf16[16,4096]{1,0:T(8,128)(2,1)}, bf16[16,4096]{1,0:T(8,128)(2,1)S(1)}, u32[]{:S(2)}, u32[]{:S(2)}) %collective-permute-start.1) | collective-permute-done | bytes 131104 | tf_op jit(solution)/shard_map/ppermute | solution.py:171
  13.9 0.6 collective-permute-start.2
  14.5 0.0 collective-permute-done.8.refs_7_
  14.5 0.8 %collective-permute-start.9 = (bf16[16,4096]{1,0:T(8,128)(2,1)S(1)}, bf16[16,4096]{1,0:T(8,128)(2,1)S(1)}, u32[]{:S(2)}, u32[]{:S(2)}) collective-permute-start(bf16[16,4096]{1,0:T(8,128)(2,1)S(1)} %collective-permute-done.8.refs_7_), channel_id=1, source_target_pairs={{0,4},{4,8},{8,12},{12,14},{14,10},{10,6},{6,2},{2,0},{1,5},{5,9},... | collective-permute-start | bytes 393224 | tf_op jit(solution)/shard_map/ppermute | solution.py:169
  15.4 2.0 %collective-permute-done.14.refs_15_.refs_7_ = bf16[16,4096]{1,0:T(8,128)(2,1)S(1)} collective-permute-done((bf16[16,4096]{1,0:T(8,128)(2,1)}, bf16[16,4096]{1,0:T(8,128)(2,1)S(1)}, u32[]{:S(2)}, u32[]{:S(2)}) %collective-permute-start.14) | collective-permute-done | bytes 131104 | tf_op jit(solution)/shard_map/ppermute | solution.py:169
  17.3 1.5 %collective-permute-start.15 = (bf16[16,4096]{1,0:T(8,128)(2,1)S(1)}, bf16[16,4096]{1,0:T(8,128)(2,1)S(1)}, u32[]{:S(2)}, u32[]{:S(2)}) collective-permute-start(bf16[16,4096]{1,0:T(8,128)(2,1)S(1)} %collective-permute-done.14.refs_15_.refs_7_), channel_id=1, source_target_pairs={{0,4},{4,8},{8,12},{12,14},{14,10},{10,6},{6,2},{2,0},{1,5},{5,9},... | collective-permute-start | bytes 393224 | tf_op jit(solution)/shard_map/ppermute | solution.py:169
  18.8 0.0 collective-permute-done.5.refs_1_
  18.9 0.0 collective-permute-start.6
  18.9 2.1 %collective-permute-done.2.refs_10_.refs_2_ = bf16[16,4096]{1,0:T(8,128)(2,1)S(1)} collective-permute-done((bf16[16,4096]{1,0:T(8,128)(2,1)S(1)}, bf16[16,4096]{1,0:T(8,128)(2,1)S(1)}, u32[]{:S(2)}, u32[]{:S(2)}) %collective-permute-start.2) | collective-permute-done | bytes 131104 | tf_op jit(solution)/shard_map/ppermute | solution.py:171
  20.9 0.0 collective-permute-start.3
  21.0 0.0 collective-permute-done.9.refs_6_
  21.0 0.0 collective-permute-done.11.refs_19_
  21.0 1.4 %collective-permute-start.13 = (bf16[16,4096]{1,0:T(8,128)(2,1)S(1)}, bf16[16,4096]{1,0:T(8,128)(2,1)S(1)}, u32[]{:S(2)}, u32[]{:S(2)}) collective-permute-start(bf16[16,4096]{1,0:T(8,128)(2,1)S(1)} %collective-permute-done.9.refs_6_), channel_id=1, source_target_pairs={{0,4},{4,8},{8,12},{12,14},{14,10},{10,6},{6,2},{2,0},{1,5},{5,9},... | collective-permute-start | bytes 393224 | tf_op jit(solution)/shard_map/ppermute | solution.py:169
  22.4 0.0 collective-permute-done.15.refs_14_.refs_6_
  22.4 1.3 %collective-permute-start.16 = (bf16[16,4096]{1,0:T(8,128)(2,1)S(1)}, bf16[16,4096]{1,0:T(8,128)(2,1)S(1)}, u32[]{:S(2)}, u32[]{:S(2)}) collective-permute-start(bf16[16,4096]{1,0:T(8,128)(2,1)S(1)} %collective-permute-done.15.refs_14_.refs_6_), channel_id=1, source_target_pairs={{0,4},{4,8},{8,12},{12,14},{14,10},{10,6},{6,2},{2,0},{1,5},{5,9},... | collective-permute-start | bytes 393224 | tf_op jit(solution)/shard_map/ppermute | solution.py:169
  23.7 0.0 collective-permute-done.6.refs_2_
  23.7 0.2 collective-permute-start.7
  23.9 2.3 %collective-permute-done.3.refs_2_.refs_11_.refs_3_ = bf16[16,4096]{1,0:T(8,128)(2,1)S(1)} collective-permute-done((bf16[16,4096]{1,0:T(8,128)(2,1)S(1)}, bf16[16,4096]{1,0:T(8,128)(2,1)S(1)}, u32[]{:S(2)}, u32[]{:S(2)}) %collective-permute-start.3) | collective-permute-done | bytes 131104 | tf_op jit(solution)/shard_map/ppermute | solution.py:171
  26.2 0.0 collective-permute-start.4
  26.2 0.1 collective-permute-done.13.refs_1_.refs_5_
  26.4 1.3 %collective-permute-start.17 = (bf16[16,4096]{1,0:T(8,128)(2,1)S(1)}, bf16[16,4096]{1,0:T(8,128)(2,1)S(1)}, u32[]{:S(2)}, u32[]{:S(2)}) collective-permute-start(bf16[16,4096]{1,0:T(8,128)(2,1)S(1)} %collective-permute-done.13.refs_1_.refs_5_), channel_id=1, source_target_pairs={{0,4},{4,8},{8,12},{12,14},{14,10},{10,6},{6,2},{2,0},{1,5},{5,9},... | collective-permute-start | bytes 393224 | tf_op jit(solution)/shard_map/ppermute | solution.py:169
  27.7 0.7 dynamic-slice_bitcast_fusion.facts
  28.4 0.0 collective-permute-done.16.refs_3_.refs_13_.refs_5_
  28.4 0.8 %collective-permute-done.7.refs_0_.refs_3_ = bf16[16,4096]{1,0:T(8,128)(2,1)S(1)} collective-permute-done((bf16[16,4096]{1,0:T(8,128)(2,1)S(1)}, bf16[16,4096]{1,0:T(8,128)(2,1)S(1)}, u32[]{:S(2)}, u32[]{:S(2)}) %collective-permute-start.7) | collective-permute-done | bytes 131104 | tf_op jit(solution)/shard_map/ppermute | solution.py:171
  29.2 3.4 %fetch.1 = (bf16[2048,2048]{1,0:T(8,128)(2,1)S(1)}, f32[8,128]{1,0:T(8,128)S(1)}) custom-call(bf16[8192,2048]{1,0:T(8,128)(2,1)} %refs_8_.1, bf16[16,4096]{1,0:T(8,128)(2,1)S(1)} %collective-permute-done.7.refs_0_.refs_3_, bf16[16,4096]{1,0:T(8,128)(2,1)S(1)} %collective-permute-done.13.refs_1_.refs_5_, ...), custom_call_target="tpu_custom_call" | custom-call | bytes 16777216 | tf_op jit(solution)/shard_map/fetch/pallas_call | solution.py:217
  32.6 0.0 collective-permute-done.4.refs_12_.refs_4_
  32.7 0.0 collective-permute-done.17.refs_4_
  32.7 0.0 copy-done
  32.7 0.0 copy-done.1
  32.7 0.6 rank_part.1.a
  33.3 0.7 collective-permute-start.18
  34.0 4.8 %project_0.1.refs_9_ = f32[128,2048]{1,0:T(8,128)S(1)} custom-call(s32[14]{0:T(128)S(1)} %dynamic-slice_bitcast_fusion.facts, bf16[16,4096]{1,0:T(8,128)(2,1)S(1)} %copy-done.1, bf16[16,4096]{1,0:T(8,128)(2,1)S(1)} %collective-permute-done.5.refs_1_, bf16[16,4096]{1,0:T(8,128)(2,1)S(1)} %collective-permute-done.6.refs_2_, ...), custom_call_target="tpu_custom_call" | custom-call | flops 2147483648 | bytes 16777216 | tf_op jit(solution)/shard_map/project_0/pallas_call | solution.py:341
  38.8 0.0 collective-permute-done.18.b
  38.8 0.0 copy-start.2
  38.8 1.4 %collective-permute-start.19 = (f32[128,128]{1,0:T(8,128)S(1)}, f32[128,128]{1,0:T(8,128)S(1)}, u32[]{:S(2)}, u32[]{:S(2)}) collective-permute-start(f32[128,128]{1,0:T(8,128)S(1)} %add.10.a), channel_id=1, source_target_pairs={{0,8},{2,10},{4,12},{6,14},{9,1},{11,3},{13,5},{15,7},{16,24},{18,... | collective-permute-start | bytes 196616 | tf_op jit(solution)/shard_map/ppermute | solution.py:525
  40.2 7.0 %project_1.1 = (f32[64,2048]{1,0:T(8,128)S(1)}, f32[64,2048]{1,0:T(8,128)S(1)}) custom-call(s32[14]{0:T(128)S(1)} %dynamic-slice_bitcast_fusion.facts, bf16[16,4096]{1,0:T(8,128)(2,1)S(1)} %copy-done, bf16[16,4096]{1,0:T(8,128)(2,1)S(1)} %collective-permute-done.1.refs_9_.refs_1_, bf16[16,4096]{1,0:T(8,128)(2,1)S(1)} %collective-permute-done.2.refs_10_.refs_2_, ...), custom_call_target="tpu_custom_call" | custom-call | flops 2147483648 | bytes 16777216 | tf_op jit(solution)/shard_map/project_1/pallas_call | solution.py:341
  47.3 0.4 collective-permute-done.19.b
  47.7 6.2 %collective-permute-start.20 = (f32[64,2048]{1,0:T(8,128)S(1)}, f32[64,2048]{1,0:T(8,128)S(1)}, u32[]{:S(2)}, u32[]{:S(2)}) collective-permute-start(f32[64,2048]{1,0:T(8,128)S(1)} %get-tuple-element.48), channel_id=1, source_target_pairs={{0,1},{1,0},{2,3},{3,2},{4,5},{5,4},{6,7},{7,6},{8,9},{9,8},{10,11... | collective-permute-start | bytes 1572872 | tf_op jit(solution)/shard_map/ppermute | solution.py:537
  53.9 0.6 split.1
  54.4 0.1 collective-permute-start.21
  54.5 1.2 %collective-permute-done.21.ranked_received = f32[64,128]{1,0:T(8,128)S(1)} collective-permute-done((f32[64,128]{1,0:T(8,128)S(1)}, f32[64,128]{1,0:T(8,128)S(1)}, u32[]{:S(2)}, u32[]{:S(2)}) %collective-permute-start.21) | collective-permute-done | bytes 32800 | tf_op jit(solution)/shard_map/ppermute | solution.py:536
  55.7 0.0 collective-permute-done.20.received
  55.7 1.0 %finish.1 = (bf16[4,4,2048]{2,1,0:T(4,128)(2,1)S(1)}, bf16[4,4,2048]{2,1,0:T(4,128)(2,1)S(1)}, bf16[4,4,2048]{2,1,0:T(4,128)(2,1)S(1)}, bf16[4,4,2048]{2,1,0:T(4,128)(2,1)S(1)}) custom-call(s32[14]{0:T(128)S(1)} %dynamic-slice_bitcast_fusion.facts, f32[64,2048]{1,0:T(8,128)S(1)} %get-tuple-element.47.keep, f32[64,2048]{1,0:T(8,128)S(1)} %collective-permute-done.20.received, ...), custom_call_target="tpu_custom_call" | custom-call | tf_op jit(solution)/shard_map/finish/pallas_call | solution.py:429
  56.8 1.9 %collective-permute-start.22 = (bf16[4,4,2048]{2,1,0:T(4,128)(2,1)S(1)}, bf16[4,4,2048]{2,1,0:T(4,128)(2,1)S(1)}, u32[]{:S(2)}, u32[]{:S(2)}) collective-permute-start(bf16[4,4,2048]{2,1,0:T(4,128)(2,1)S(1)} %get-tuple-element.53), channel_id=1, source_target_pairs={{0,0},{1,8},{2,2},{3,10},{4,4},{5,12},{6,6},{7,14},{8,9},{9,1},{10... | collective-permute-start | bytes 196616 | tf_op jit(solution)/shard_map/ppermute | solution.py:548
  58.7 0.6 collective-permute-start.23
  59.3 4.3 %collective-permute-start.24 = (bf16[4,4,2048]{2,1,0:T(4,128)(2,1)S(1)}, bf16[4,4,2048]{2,1,0:T(4,128)(2,1)S(1)}, u32[]{:S(2)}, u32[]{:S(2)}) collective-permute-start(bf16[4,4,2048]{2,1,0:T(4,128)(2,1)S(1)} %get-tuple-element.55), channel_id=1, source_target_pairs={{0,4},{1,12},{2,6},{3,14},{4,0},{5,8},{6,2},{7,10},{8,13},{9,5},{1... | collective-permute-start | bytes 196616 | tf_op jit(solution)/shard_map/ppermute | solution.py:548
  63.5 0.4 collective-permute-start.25
  64.0 0.0 collective-permute-done.22.refs_0_
  64.0 2.8 %collective-permute-done.23.refs_1_ = bf16[4,4,2048]{2,1,0:T(4,128)(2,1)S(1)} collective-permute-done((bf16[4,4,2048]{2,1,0:T(4,128)(2,1)S(1)}, bf16[4,4,2048]{2,1,0:T(4,128)(2,1)S(1)}, u32[]{:S(2)}, u32[]{:S(2)}) %collective-permute-start.23) | collective-permute-done | bytes 65568 | tf_op jit(solution)/shard_map/ppermute | solution.py:548
  66.8 0.0 collective-permute-done.24.refs_2_
  66.8 2.5 %collective-permute-done.25.refs_3_ = bf16[4,4,2048]{2,1,0:T(4,128)(2,1)S(1)} collective-permute-done((bf16[4,4,2048]{2,1,0:T(4,128)(2,1)S(1)}, bf16[4,4,2048]{2,1,0:T(4,128)(2,1)S(1)}, u32[]{:S(2)}, u32[]{:S(2)}) %collective-permute-start.25) | collective-permute-done | bytes 65568 | tf_op jit(solution)/shard_map/ppermute | solution.py:548
  69.4 1.3 %place.1 = bf16[4,4,8192]{2,1,0:T(4,128)(2,1)} custom-call(s32[14]{0:T(128)S(1)} %dynamic-slice_bitcast_fusion.facts, bf16[4,4,2048]{2,1,0:T(4,128)(2,1)S(1)} %collective-permute-done.22.refs_0_, bf16[4,4,2048]{2,1,0:T(4,128)(2,1)S(1)} %collective-permute-done.23.refs_1_, bf16[4,4,2048]{2,1,0:T(4,128)(2,1)S(1)} %collective-permute-done.24.refs_2_, ...), custom_call_target="tpu_custom_call" | custom-call | tf_op jit(solution)/shard_map/place/pallas_call | solution.py:457
  (6 shorter events, 0.0 us)
Async XLA Ops:
  0.0 9.1 %collective-permute-start = (bf16[64,2048]{1,0:T(8,128)(2,1)}, bf16[64,2048]{1,0:T(8,128)(2,1)S(1)}, u32[]{:S(2)}, u32[]{:S(2)}) collective-permute-start(bf16[64,2048]{1,0:T(8,128)(2,1)} %bitcast.7), channel_id=1, source_target_pairs={{0,2},{2,0},{4,6},{6,4},{8,10},{10,8},{12,14},{14,12},{1,3},{3,1},... | collective-permute-start | bytes 786440 | tf_op jit(solution)/shard_map/ppermute | solution.py:497
  2.1 9.6 %collective-permute-start.10 = (bf16[64,2048]{1,0:T(8,128)(2,1)}, bf16[64,2048]{1,0:T(8,128)(2,1)S(1)}, u32[]{:S(2)}, u32[]{:S(2)}) collective-permute-start(bf16[64,2048]{1,0:T(8,128)(2,1)} %bitcast.8), channel_id=1, source_target_pairs={{0,1},{1,0},{2,3},{3,2},{4,5},{5,4},{6,7},{7,6},{8,9},{9,8},{10,11... | collective-permute-start | bytes 786440 | tf_op jit(solution)/shard_map/ppermute | solution.py:512
  3.0 10.1 %collective-permute-start.12 = (bf16[64,2048]{1,0:T(8,128)(2,1)}, bf16[64,2048]{1,0:T(8,128)(2,1)S(1)}, u32[]{:S(2)}, u32[]{:S(2)}) collective-permute-start(bf16[64,2048]{1,0:T(8,128)(2,1)} %own.1), channel_id=1, source_target_pairs={{0,1},{1,0},{2,3},{3,2},{4,5},{5,4},{6,7},{7,6},{8,9},{9,8},{10,11... | collective-permute-start | bytes 786440 | tf_op jit(solution)/shard_map/ppermute | solution.py:512
  9.1 4.8 %collective-permute-start.1 = (bf16[16,4096]{1,0:T(8,128)(2,1)}, bf16[16,4096]{1,0:T(8,128)(2,1)S(1)}, u32[]{:S(2)}, u32[]{:S(2)}) collective-permute-start(bf16[16,4096]{1,0:T(8,128)(2,1)} %get-tuple-element.33.refs_8_.refs_0_), channel_id=1, source_target_pairs={{4,0},{8,4},{12,8},{14,12},{10,14},{6,10},{2,6},{0,2},{5,1},{9,5},... | collective-permute-start | bytes 393224 | tf_op jit(solution)/shard_map/ppermute | solution.py:171
  9.5 5.1 %collective-permute-start.8 = (bf16[16,4096]{1,0:T(8,128)(2,1)}, bf16[16,4096]{1,0:T(8,128)(2,1)S(1)}, u32[]{:S(2)}, u32[]{:S(2)}) collective-permute-start(bf16[16,4096]{1,0:T(8,128)(2,1)} %get-tuple-element.34.refs_0_), channel_id=1, source_target_pairs={{0,4},{4,8},{8,12},{12,14},{14,10},{10,6},{6,2},{2,0},{1,5},{5,9},... | collective-permute-start | bytes 393224 | tf_op jit(solution)/shard_map/ppermute | solution.py:169
  10.6 10.4 %collective-permute-start.11 = (bf16[64,2048]{1,0:T(8,128)(2,1)S(1)}, bf16[64,2048]{1,0:T(8,128)(2,1)S(1)}, u32[]{:S(2)}, u32[]{:S(2)}) collective-permute-start(bf16[64,2048]{1,0:T(8,128)(2,1)S(1)} %collective-permute-done.refs_17_), channel_id=1, source_target_pairs={{0,1},{1,0},{2,3},{3,2},{4,5},{5,4},{6,7},{7,6},{8,9},{9,8},{10,11... | collective-permute-start | bytes 786440 | tf_op jit(solution)/shard_map/ppermute | solution.py:512
  11.7 5.6 %collective-permute-start.14 = (bf16[16,4096]{1,0:T(8,128)(2,1)}, bf16[16,4096]{1,0:T(8,128)(2,1)S(1)}, u32[]{:S(2)}, u32[]{:S(2)}) collective-permute-start(bf16[16,4096]{1,0:T(8,128)(2,1)} %get-tuple-element.33.refs_8_.refs_0_), channel_id=1, source_target_pairs={{0,4},{4,8},{8,12},{12,14},{14,10},{10,6},{6,2},{2,0},{1,5},{5,9},... | collective-permute-start | bytes 393224 | tf_op jit(solution)/shard_map/ppermute | solution.py:169
  13.1 5.8 %collective-permute-start.5 = (bf16[16,4096]{1,0:T(8,128)(2,1)}, bf16[16,4096]{1,0:T(8,128)(2,1)S(1)}, u32[]{:S(2)}, u32[]{:S(2)}) collective-permute-start(bf16[16,4096]{1,0:T(8,128)(2,1)} %get-tuple-element.34.refs_0_), channel_id=1, source_target_pairs={{4,0},{8,4},{12,8},{14,12},{10,14},{6,10},{2,6},{0,2},{5,1},{9,5},... | collective-permute-start | bytes 393224 | tf_op jit(solution)/shard_map/ppermute | solution.py:171
  13.9 7.0 %collective-permute-start.2 = (bf16[16,4096]{1,0:T(8,128)(2,1)S(1)}, bf16[16,4096]{1,0:T(8,128)(2,1)S(1)}, u32[]{:S(2)}, u32[]{:S(2)}) collective-permute-start(bf16[16,4096]{1,0:T(8,128)(2,1)S(1)} %collective-permute-done.1.refs_9_.refs_1_), channel_id=1, source_target_pairs={{4,0},{8,4},{12,8},{14,12},{10,14},{6,10},{2,6},{0,2},{5,1},{9,5},... | collective-permute-start | bytes 393224 | tf_op jit(solution)/shard_map/ppermute | solution.py:171
  14.5 6.5 %collective-permute-start.9 = (bf16[16,4096]{1,0:T(8,128)(2,1)S(1)}, bf16[16,4096]{1,0:T(8,128)(2,1)S(1)}, u32[]{:S(2)}, u32[]{:S(2)}) collective-permute-start(bf16[16,4096]{1,0:T(8,128)(2,1)S(1)} %collective-permute-done.8.refs_7_), channel_id=1, source_target_pairs={{0,4},{4,8},{8,12},{12,14},{14,10},{10,6},{6,2},{2,0},{1,5},{5,9},... | collective-permute-start | bytes 393224 | tf_op jit(solution)/shard_map/ppermute | solution.py:169
  17.3 5.1 %collective-permute-start.15 = (bf16[16,4096]{1,0:T(8,128)(2,1)S(1)}, bf16[16,4096]{1,0:T(8,128)(2,1)S(1)}, u32[]{:S(2)}, u32[]{:S(2)}) collective-permute-start(bf16[16,4096]{1,0:T(8,128)(2,1)S(1)} %collective-permute-done.14.refs_15_.refs_7_), channel_id=1, source_target_pairs={{0,4},{4,8},{8,12},{12,14},{14,10},{10,6},{6,2},{2,0},{1,5},{5,9},... | collective-permute-start | bytes 393224 | tf_op jit(solution)/shard_map/ppermute | solution.py:169
  18.9 4.8 %collective-permute-start.6 = (bf16[16,4096]{1,0:T(8,128)(2,1)S(1)}, bf16[16,4096]{1,0:T(8,128)(2,1)S(1)}, u32[]{:S(2)}, u32[]{:S(2)}) collective-permute-start(bf16[16,4096]{1,0:T(8,128)(2,1)S(1)} %collective-permute-done.5.refs_1_), channel_id=1, source_target_pairs={{4,0},{8,4},{12,8},{14,12},{10,14},{6,10},{2,6},{0,2},{5,1},{9,5},... | collective-permute-start | bytes 393224 | tf_op jit(solution)/shard_map/ppermute | solution.py:171
  20.9 5.3 %collective-permute-start.3 = (bf16[16,4096]{1,0:T(8,128)(2,1)S(1)}, bf16[16,4096]{1,0:T(8,128)(2,1)S(1)}, u32[]{:S(2)}, u32[]{:S(2)}) collective-permute-start(bf16[16,4096]{1,0:T(8,128)(2,1)S(1)} %collective-permute-done.2.refs_10_.refs_2_), channel_id=1, source_target_pairs={{4,0},{8,4},{12,8},{14,12},{10,14},{6,10},{2,6},{0,2},{5,1},{9,5},... | collective-permute-start | bytes 393224 | tf_op jit(solution)/shard_map/ppermute | solution.py:171
  21.0 5.4 %collective-permute-start.13 = (bf16[16,4096]{1,0:T(8,128)(2,1)S(1)}, bf16[16,4096]{1,0:T(8,128)(2,1)S(1)}, u32[]{:S(2)}, u32[]{:S(2)}) collective-permute-start(bf16[16,4096]{1,0:T(8,128)(2,1)S(1)} %collective-permute-done.9.refs_6_), channel_id=1, source_target_pairs={{0,4},{4,8},{8,12},{12,14},{14,10},{10,6},{6,2},{2,0},{1,5},{5,9},... | collective-permute-start | bytes 393224 | tf_op jit(solution)/shard_map/ppermute | solution.py:169
  22.4 6.0 %collective-permute-start.16 = (bf16[16,4096]{1,0:T(8,128)(2,1)S(1)}, bf16[16,4096]{1,0:T(8,128)(2,1)S(1)}, u32[]{:S(2)}, u32[]{:S(2)}) collective-permute-start(bf16[16,4096]{1,0:T(8,128)(2,1)S(1)} %collective-permute-done.15.refs_14_.refs_6_), channel_id=1, source_target_pairs={{0,4},{4,8},{8,12},{12,14},{14,10},{10,6},{6,2},{2,0},{1,5},{5,9},... | collective-permute-start | bytes 393224 | tf_op jit(solution)/shard_map/ppermute | solution.py:169
  23.7 5.5 %collective-permute-start.7 = (bf16[16,4096]{1,0:T(8,128)(2,1)S(1)}, bf16[16,4096]{1,0:T(8,128)(2,1)S(1)}, u32[]{:S(2)}, u32[]{:S(2)}) collective-permute-start(bf16[16,4096]{1,0:T(8,128)(2,1)S(1)} %collective-permute-done.6.refs_2_), channel_id=1, source_target_pairs={{4,0},{8,4},{12,8},{14,12},{10,14},{6,10},{2,6},{0,2},{5,1},{9,5},... | collective-permute-start | bytes 393224 | tf_op jit(solution)/shard_map/ppermute | solution.py:171
  26.2 6.4 %collective-permute-start.4 = (bf16[16,4096]{1,0:T(8,128)(2,1)S(1)}, bf16[16,4096]{1,0:T(8,128)(2,1)S(1)}, u32[]{:S(2)}, u32[]{:S(2)}) collective-permute-start(bf16[16,4096]{1,0:T(8,128)(2,1)S(1)} %collective-permute-done.3.refs_2_.refs_11_.refs_3_), channel_id=1, source_target_pairs={{4,0},{8,4},{12,8},{14,12},{10,14},{6,10},{2,6},{0,2},{5,1},{9,5},... | collective-permute-start | bytes 393224 | tf_op jit(solution)/shard_map/ppermute | solution.py:171
  26.4 6.3 %collective-permute-start.17 = (bf16[16,4096]{1,0:T(8,128)(2,1)S(1)}, bf16[16,4096]{1,0:T(8,128)(2,1)S(1)}, u32[]{:S(2)}, u32[]{:S(2)}) collective-permute-start(bf16[16,4096]{1,0:T(8,128)(2,1)S(1)} %collective-permute-done.13.refs_1_.refs_5_), channel_id=1, source_target_pairs={{0,4},{4,8},{8,12},{12,14},{14,10},{10,6},{6,2},{2,0},{1,5},{5,9},... | collective-permute-start | bytes 393224 | tf_op jit(solution)/shard_map/ppermute | solution.py:169
  28.4 4.3 %copy-start = (bf16[16,4096]{1,0:T(8,128)(2,1)S(1)}, bf16[16,4096]{1,0:T(8,128)(2,1)}, u32[]{:S(2)}) copy-start(bf16[16,4096]{1,0:T(8,128)(2,1)} %get-tuple-element.33.refs_8_.refs_0_) | copy-start | bytes 393220
  28.4 4.3 %copy-start.1 = (bf16[16,4096]{1,0:T(8,128)(2,1)S(1)}, bf16[16,4096]{1,0:T(8,128)(2,1)}, u32[]{:S(2)}) copy-start(bf16[16,4096]{1,0:T(8,128)(2,1)} %get-tuple-element.34.refs_0_) | copy-start | bytes 393220
  28.4 4.3 %copy-start.3 = (bf16[2048,64]{0,1:T(8,128)(2,1)S(1)}, bf16[2048,64]{0,1:T(8,128)(2,1)}, u32[]{:S(2)}) copy-start(bf16[2048,64]{0,1:T(8,128)(2,1)} %param.17) | copy-start | bytes 786436
  33.3 5.5 %collective-permute-start.18 = (f32[128,128]{1,0:T(8,128)S(1)}, f32[128,128]{1,0:T(8,128)S(1)}, u32[]{:S(2)}, u32[]{:S(2)}) collective-permute-start(f32[128,128]{1,0:T(8,128)S(1)} %rank_part.1.a), channel_id=1, source_target_pairs={{0,4},{2,6},{4,0},{6,2},{9,13},{11,15},{13,9},{15,11},{16,20},{18,... | collective-permute-start | bytes 196616 | tf_op jit(solution)/shard_map/ppermute | solution.py:525
  38.8 16.9 %copy-start.2 = (bf16[64,2048]{1,0:T(8,128)(2,1)S(1)}, bf16[64,2048]{1,0:T(8,128)(2,1)}, u32[]{:S(2)}) copy-start(bf16[64,2048]{1,0:T(8,128)(2,1)} %own.1) | copy-start | bytes 786436
  38.8 8.9 %collective-permute-start.19 = (f32[128,128]{1,0:T(8,128)S(1)}, f32[128,128]{1,0:T(8,128)S(1)}, u32[]{:S(2)}, u32[]{:S(2)}) collective-permute-start(f32[128,128]{1,0:T(8,128)S(1)} %add.10.a), channel_id=1, source_target_pairs={{0,8},{2,10},{4,12},{6,14},{9,1},{11,3},{13,5},{15,7},{16,24},{18,... | collective-permute-start | bytes 196616 | tf_op jit(solution)/shard_map/ppermute | solution.py:525
  47.7 8.1 %collective-permute-start.20 = (f32[64,2048]{1,0:T(8,128)S(1)}, f32[64,2048]{1,0:T(8,128)S(1)}, u32[]{:S(2)}, u32[]{:S(2)}) collective-permute-start(f32[64,2048]{1,0:T(8,128)S(1)} %get-tuple-element.48), channel_id=1, source_target_pairs={{0,1},{1,0},{2,3},{3,2},{4,5},{5,4},{6,7},{7,6},{8,9},{9,8},{10,11... | collective-permute-start | bytes 1572872 | tf_op jit(solution)/shard_map/ppermute | solution.py:537
  54.4 1.3 %collective-permute-start.21 = (f32[64,128]{1,0:T(8,128)S(1)}, f32[64,128]{1,0:T(8,128)S(1)}, u32[]{:S(2)}, u32[]{:S(2)}) collective-permute-start(f32[64,128]{1,0:T(8,128)S(1)} %get-tuple-element.51), channel_id=1, source_target_pairs={{0,1},{1,0},{2,3},{3,2},{4,5},{5,4},{6,7},{7,6},{8,9},{9,8},{10,11... | collective-permute-start | bytes 98312 | tf_op jit(solution)/shard_map/ppermute | solution.py:536
  56.8 7.2 %collective-permute-start.22 = (bf16[4,4,2048]{2,1,0:T(4,128)(2,1)S(1)}, bf16[4,4,2048]{2,1,0:T(4,128)(2,1)S(1)}, u32[]{:S(2)}, u32[]{:S(2)}) collective-permute-start(bf16[4,4,2048]{2,1,0:T(4,128)(2,1)S(1)} %get-tuple-element.53), channel_id=1, source_target_pairs={{0,0},{1,8},{2,2},{3,10},{4,4},{5,12},{6,6},{7,14},{8,9},{9,1},{10... | collective-permute-start | bytes 196616 | tf_op jit(solution)/shard_map/ppermute | solution.py:548
  58.7 8.1 %collective-permute-start.23 = (bf16[4,4,2048]{2,1,0:T(4,128)(2,1)S(1)}, bf16[4,4,2048]{2,1,0:T(4,128)(2,1)S(1)}, u32[]{:S(2)}, u32[]{:S(2)}) collective-permute-start(bf16[4,4,2048]{2,1,0:T(4,128)(2,1)S(1)} %get-tuple-element.54), channel_id=1, source_target_pairs={{0,2},{1,10},{2,0},{3,8},{4,6},{5,14},{6,4},{7,12},{8,11},{9,3},{1... | collective-permute-start | bytes 196616 | tf_op jit(solution)/shard_map/ppermute | solution.py:548
  59.3 7.6 %collective-permute-start.24 = (bf16[4,4,2048]{2,1,0:T(4,128)(2,1)S(1)}, bf16[4,4,2048]{2,1,0:T(4,128)(2,1)S(1)}, u32[]{:S(2)}, u32[]{:S(2)}) collective-permute-start(bf16[4,4,2048]{2,1,0:T(4,128)(2,1)S(1)} %get-tuple-element.55), channel_id=1, source_target_pairs={{0,4},{1,12},{2,6},{3,14},{4,0},{5,8},{6,2},{7,10},{8,13},{9,5},{1... | collective-permute-start | bytes 196616 | tf_op jit(solution)/shard_map/ppermute | solution.py:548
  63.5 5.8 %collective-permute-start.25 = (bf16[4,4,2048]{2,1,0:T(4,128)(2,1)S(1)}, bf16[4,4,2048]{2,1,0:T(4,128)(2,1)S(1)}, u32[]{:S(2)}, u32[]{:S(2)}) collective-permute-start(bf16[4,4,2048]{2,1,0:T(4,128)(2,1)S(1)} %get-tuple-element.56), channel_id=1, source_target_pairs={{0,6},{1,14},{2,4},{3,12},{4,2},{5,10},{6,0},{7,8},{8,15},{9,7},{1... | collective-permute-start | bytes 196616 | tf_op jit(solution)/shard_map/ppermute | solution.py:548

commit v4 on v3

--- a/solution.py
+++ b/solution.py
@@ -12,8 +12,9 @@
 adapter_scale = 2.0
 chunk_count = 2
 fetched = 64
+ahead_share = 5
 staged_rows = 2
-weight_edges = (0, 3, 8, 13, 16)
+tile_rows = 512
 mebibyte = 1024 * 1024
 
 
@@ -284,82 +285,93 @@
     )(facts, token, *blocks, *factors)
 
 
-def project_kernel(chunk, facts, *refs):
+def project_kernel(start, stop, first, ahead, last, facts, *refs):
     refs = list(refs)
-    held, streamed, sem, sems = refs[-4:]
-    last = chunk == chunk_count - 1
-    outs = refs[-5 - last : -4]
-    refs = refs[: -5 - last]
-    previous = refs.pop() if chunk else None
-    weight = refs.pop()
-    ready = None if chunk else refs.pop()
-    width = held.shape[2]
-    rows = held.shape[0] * held.shape[1]
-    skipped = 0 if chunk else ready.shape[0]
-    edges = [skipped + (width - skipped) * i // 16 for i in weight_edges]
+    held, streamed, sem, sems, ahead_sem = refs[-5:]
+    count = held.shape[0]
+    blocks, refs = refs[:count], refs[count:-5]
+    ready, weight, refs = refs[0], refs[1], refs[2:]
+    previous = refs.pop(0) if first else None
+    width = stop - start
+    rows = count * held.shape[1]
+    skipped = ready.shape[0]
+    edges = [*range(skipped, width, tile_rows), width]
     copies = [
         pltpu.make_async_copy(
-            weight.at[pl.ds(chunk * width + start, stop - start), :],
-            streamed.at[pl.ds(start - skipped, stop - start), :],
+            weight.at[pl.ds(first + begin, end - begin), :],
+            streamed.at[pl.ds(begin - skipped, end - begin), :],
             sems.at[i],
         )
-        for i, (start, stop) in enumerate(zip(edges, edges[1:]))
+        for i, (begin, end) in enumerate(zip(edges, edges[1:]))
     ]
     for copy in copies:
         copy.start()
-    collect(facts, refs, held, slice(None), sem)
-
-    def product(start, stop, factor):
+    if ahead:
+        later = pltpu.make_async_copy(weight.at[pl.ds(first + width, ahead), :], refs[1], ahead_sem)
+        later.start()
+    collect(facts, blocks, held, slice(start, stop), sem)
+
+    def product(begin, end, factor):
         return jnp.dot(
-            held[:, :, start:stop].reshape(rows, stop - start),
+            held[:, :, begin:end].reshape(rows, end - begin),
             factor,
             preferred_element_type=jnp.float32,
         )
 
-    total = previous[...] if chunk else product(0, skipped, ready[...])
-    for copy, start, stop in zip(copies, edges, edges[1:]):
+    total = product(0, skipped, ready[...])
+    if first:
+        total += previous[...]
+    for copy, begin, end in zip(copies, edges, edges[1:]):
         copy.wait()
-        total += product(start, stop, streamed[start - skipped : stop - skipped, :])
+        total += product(begin, end, streamed[begin - skipped : end - skipped, :])
     if not last:
-        outs[0][...] = total
+        refs[0][...] = total
+        later.wait()
         return
-    keep, send = outs
+    keep, send = refs
     kept = facts[fact_kept]
     top, bottom = total[: rows // 2], total[rows // 2 :]
     keep[...] = jnp.where(kept == 0, top, bottom)
     send[...] = jnp.where(kept == 0, bottom, top)
 
 
-def project(chunk, facts, blocks, ready, base_weight, previous):
+def project(facts, gathered, start, stop, ahead, ready, base_weight, previous):
+    features, columns = base_weight.shape
+    chunk_width = features // chunk_count
+    chunk, start = divmod(start, chunk_width)
+    stop = stop - chunk * chunk_width
+    first = chunk * chunk_width + start
+    blocks = gathered[chunk]
     count = len(blocks)
-    block_rows, width = blocks[0].shape
-    columns = base_weight.shape[1]
+    block_rows = blocks[0].shape[0]
     rows = count * block_rows
-    last = chunk == chunk_count - 1
-    vmem = pl.BlockSpec(memory_space=pltpu.VMEM)
-    anywhere = pl.BlockSpec(memory_space=pl.ANY)
-    result = pl.pallas_call(
-        functools.partial(project_kernel, chunk),
+    last = not ahead
+    vmem = pl.BlockSpec(memory_space=pltpu.VMEM)
+    shape = jax.ShapeDtypeStruct((rows // (1 + last), columns), jnp.float32)
+    shapes = [shape] * 2 if last else [shape, jax.ShapeDtypeStruct((ahead, columns), jnp.bfloat16)]
+    return pl.pallas_call(
+        functools.partial(project_kernel, start, stop, first, ahead, last),
         in_specs=[pl.BlockSpec(memory_space=pltpu.SMEM)]
         + block_specs(count)
-        + [vmem] * (chunk == 0)
-        + [anywhere]
-        + [vmem] * (chunk > 0),
-        out_specs=[vmem] * (1 + last),
-        out_shape=[jax.ShapeDtypeStruct((rows // (1 + last), columns), jnp.float32)] * (1 + last),
+        + [vmem, pl.BlockSpec(memory_space=pl.ANY)]
+        + [vmem] * (first > 0),
+        out_specs=[vmem] * 2,
+        out_shape=shapes,
         scratch_shapes=[
-            pltpu.VMEM((count, block_rows, width), jnp.bfloat16),
-            pltpu.VMEM((width if chunk else width - ready.shape[0], columns), jnp.bfloat16),
+            pltpu.VMEM((count, block_rows, stop - start), jnp.bfloat16),
+            pltpu.VMEM((stop - start - ready.shape[0], columns), jnp.bfloat16),
             pltpu.SemaphoreType.DMA(()),
-            pltpu.SemaphoreType.DMA((len(weight_edges) - 1,)),
+            pltpu.SemaphoreType.DMA((-(-(stop - start - ready.shape[0]) // tile_rows),)),
+            pltpu.SemaphoreType.DMA(()),
         ],
-        compiler_params=pltpu.CompilerParams(vmem_limit_bytes=(32 if chunk else 26) * mebibyte),
+        compiler_params=pltpu.CompilerParams(vmem_limit_bytes=26 * mebibyte),
         cost_estimate=pl.CostEstimate(
-            flops=2 * rows * width * columns, bytes_accessed=2 * width * columns, transcendentals=0
+            flops=2 * rows * (stop - start) * columns,
+            bytes_accessed=2 * (stop - start) * columns,
+            transcendentals=0,
         ),
-        name=f"project_{chunk}",
-    )(facts, *blocks, *([] if chunk else [ready]), base_weight, *([previous] if chunk else []))
-    return result if last else result[0]
+        name=f"project_{first}",
+    )(facts, *blocks, ready, base_weight, *([previous] if first else []))
 
 
 def add_kernel(a, b, out):
@@ -517,21 +529,28 @@
     gathered[-1][half], token = after((gathered[-1][half], token))
 
     ranked = rank_part(facts, token, gathered, (own_in, near_in, other_in, other_near_in))
-    bit, done, state = 2, 0, None
-    while True:
-        last = bit >= half
-        turn = half if last else bit
-        pairs = [(2 * f + f // half, 2 * (f ^ turn) + f // half) for f in range(count)]
+    features = base_weight.shape[0]
+    parts = [(0, features // 2), (features // 2, features)]
+    state = None
+
+    def next_part():
+        start, stop = parts.pop(0)
+        ahead = (parts[0][1] - parts[0][0]) * ahead_share // 16 if parts else 0
+        return project(facts, gathered, start, stop, ahead, ready, base_weight, state)
+
+    bit = 2
+    while bit < half:
+        pairs = [(2 * f + f // half, 2 * (f ^ bit) + f // half) for f in range(count)]
         received = lax.ppermute(ranked, both, pairs)
-        while done < (chunk_count if last else 1):
-            state = project(done, facts, gathered[done], ready, base_weight, state)
-            done += 1
-        received, state = after((received, state))
-        if last:
-            break
+        if bit == 2:
+            received, (state, ready) = after((received, next_part()))
         ranked = add(ranked, received)
         bit *= 2
-    keep, send = state
+    pairs = [(2 * f + f // half, 2 * (f ^ half) + f // half) for f in range(count)]
+    received = lax.ppermute(ranked, both, pairs)
+    if len(parts) > 1:
+        received, (state, ready) = after((received, next_part()))
+    received, (keep, send) = after((received, next_part()))
     ranked_keep, ranked_send = split(facts, ranked, received)
     ranked_received = lax.ppermute(ranked_send, "tp", swap)
     received = lax.ppermute(send, "tp", swap)

time: 70.9 us -> 70 us (0.987)
  waiting for transfers between devices: 15.1 us -> 16.8 us
  starting transfers between devices: 30 us -> 28.3 us
  Pallas kernels: 24.7 us -> 23.7 us
    ppermute x2, waiting for transfers between devices: 0.41 us -> 2.1 us  [shards(): received = lax.ppermute(ranked, both, pairs)]
    ppermute x1, starting transfers between devices: 6.22 us -> 4.55 us  [shards(): received = lax.ppermute(send, 'tp', swap)]
    pallas_call x2, Pallas kernels: 11.8 us -> 10.9 us  [project(): pl.pallas_call(functools.partial(project_kernel, start, stop, first, ahea...]
  transfers between devices with their start and end apart: 26 -> 26, of which waited for: 10 -> 10; matrix products, arithmetic and copies ran while one was open for 1% -> 1% of each run, Pallas kernels for 31% -> 30%
where the time goes in v4:
time: 70 us; the launch traced here: 69.7 us
  starting transfers between devices  28.3 us (40%)
  Pallas kernels  23.7 us (34%)
  waiting for transfers between devices  16.8 us (24%)
  local copies, waits for them, and re-layouts  0.71 us (1%)
    pallas_call x2, Pallas kernels, project(): pl.pallas_call(functools.partial(project_kernel, start, stop, first, ahea...  10.9 us
    ppermute x7, starting transfers between devices, ring_step(): blocks[count - step] = lax.ppermute(blocks[(1 - step) % count], 'fsdp', up)  9.01 us
    ppermute x4, starting transfers between devices, shards(): landed.append(lax.ppermute(piece, both, pairs))  7.22 us
    ppermute x7, waiting for transfers between devices, ring_step(): blocks[step] = lax.ppermute(blocks[step - 1], 'fsdp', down)  6.03 us
    pallas_call x1, Pallas kernels, attend(): pl.pallas_call(attend_kernel, in_specs=[smem] + [anywhere] * 5, out_specs...  6.02 us
    ppermute x4, waiting for transfers between devices, shards(): landed.append(lax.ppermute(piece, both, pairs))  5.36 us
    ppermute x1, starting transfers between devices, shards(): received = lax.ppermute(send, 'tp', swap)  4.55 us
    pallas_call x1, Pallas kernels, fetch(): pl.pallas_call(fetch_kernel, in_specs=[pl.BlockSpec(memory_space=pl.ANY)]...  3.39 us
  transfers between devices with their start and end apart: 26, of which 10 were waited for; matrix products, arithmetic and copies ran while one was open for 1% of the time, Pallas kernels for 30%

profile of v4, /device:TPU:1, one launch (start us, length us, event | category | flops | bytes accessed | tf_op | source)
XLA Modules:
  0.0 69.7 jit_solution(13216584278662671427)
XLA Ops:
  0.0 2.1 %collective-permute-start = (bf16[64,2048]{1,0:T(8,128)(2,1)}, bf16[64,2048]{1,0:T(8,128)(2,1)S(1)}, u32[]{:S(2)}, u32[]{:S(2)}) collective-permute-start(bf16[64,2048]{1,0:T(8,128)(2,1)} %bitcast.7), channel_id=1, source_target_pairs={{0,2},{2,0},{4,6},{6,4},{8,10},{10,8},{12,14},{14,12},{1,3},{3,1},... | collective-permute-start | bytes 786440 | tf_op jit(solution)/shard_map/ppermute | solution.py:509
  2.1 1.0 %collective-permute-start.10 = (bf16[64,2048]{1,0:T(8,128)(2,1)}, bf16[64,2048]{1,0:T(8,128)(2,1)S(1)}, u32[]{:S(2)}, u32[]{:S(2)}) collective-permute-start(bf16[64,2048]{1,0:T(8,128)(2,1)} %bitcast.8), channel_id=1, source_target_pairs={{0,1},{1,0},{2,3},{3,2},{4,5},{5,4},{6,7},{7,6},{8,9},{9,8},{10,11... | collective-permute-start | bytes 786440 | tf_op jit(solution)/shard_map/ppermute | solution.py:524
  3.0 0.0 collective-permute-start.12
  3.0 6.0 %attend.1 = (bf16[16,4096]{1,0:T(8,128)(2,1)}, bf16[16,4096]{1,0:T(8,128)(2,1)}) custom-call(s32[4]{0:T(128)} %lengths.1, bf16[4,4,64,128]{3,2,1,0:T(8,128)(2,1)} %queries.1, bf16[4,2048,128]{2,1,0:T(8,128)(2,1)} %bitcast.10, bf16[4,2048,128]{2,1,0:T(8,128)(2,1)} %bitcast.11, bf16[4,16,128]{2,1,0:T(8,128)(2,1)} %bitcast.12, bf16[4,16,128]{2,1,0:T(8,128)(2,1)} %bitcast.13), custom_call_target="tpu_custom_call" | custom-call | flops 1073741824 | bytes 4194304 | tf_op jit(solution)/shard_map/attend/pallas_call | solution.py:125
  9.1 0.0 collective-permute-done.refs_17_
  9.1 0.4 collective-permute-start.1
  9.5 1.1 %collective-permute-start.8 = (bf16[16,4096]{1,0:T(8,128)(2,1)}, bf16[16,4096]{1,0:T(8,128)(2,1)S(1)}, u32[]{:S(2)}, u32[]{:S(2)}) collective-permute-start(bf16[16,4096]{1,0:T(8,128)(2,1)} %get-tuple-element.37.refs_0_), channel_id=1, source_target_pairs={{0,4},{4,8},{8,12},{12,14},{14,10},{10,6},{6,2},{2,0},{1,5},{5,9},... | collective-permute-start | bytes 393224 | tf_op jit(solution)/shard_map/ppermute | solution.py:170
  10.6 1.1 %collective-permute-start.11 = (bf16[64,2048]{1,0:T(8,128)(2,1)S(1)}, bf16[64,2048]{1,0:T(8,128)(2,1)S(1)}, u32[]{:S(2)}, u32[]{:S(2)}) collective-permute-start(bf16[64,2048]{1,0:T(8,128)(2,1)S(1)} %collective-permute-done.refs_17_), channel_id=1, source_target_pairs={{0,1},{1,0},{2,3},{3,2},{4,5},{5,4},{6,7},{7,6},{8,9},{9,8},{10,11... | collective-permute-start | bytes 786440 | tf_op jit(solution)/shard_map/ppermute | solution.py:524
  11.7 0.0 collective-permute-done.10.refs_18_
  11.7 1.4 %collective-permute-start.14 = (bf16[16,4096]{1,0:T(8,128)(2,1)}, bf16[16,4096]{1,0:T(8,128)(2,1)S(1)}, u32[]{:S(2)}, u32[]{:S(2)}) collective-permute-start(bf16[16,4096]{1,0:T(8,128)(2,1)} %get-tuple-element.36.refs_8_.refs_0_), channel_id=1, source_target_pairs={{0,4},{4,8},{8,12},{12,14},{14,10},{10,6},{6,2},{2,0},{1,5},{5,9},... | collective-permute-start | bytes 393224 | tf_op jit(solution)/shard_map/ppermute | solution.py:170
  13.1 0.0 collective-permute-done.12.other
  13.1 0.0 collective-permute-start.5
  13.1 0.8 %collective-permute-done.1.refs_9_.refs_1_ = bf16[16,4096]{1,0:T(8,128)(2,1)S(1)} collective-permute-done((bf16[16,4096]{1,0:T(8,128)(2,1)}, bf16[16,4096]{1,0:T(8,128)(2,1)S(1)}, u32[]{:S(2)}, u32[]{:S(2)}) %collective-permute-start.1) | collective-permute-done | bytes 131104 | tf_op jit(solution)/shard_map/ppermute | solution.py:172
  13.9 0.6 collective-permute-start.2
  14.5 0.0 collective-permute-done.8.refs_7_
  14.5 0.8 %collective-permute-start.9 = (bf16[16,4096]{1,0:T(8,128)(2,1)S(1)}, bf16[16,4096]{1,0:T(8,128)(2,1)S(1)}, u32[]{:S(2)}, u32[]{:S(2)}) collective-permute-start(bf16[16,4096]{1,0:T(8,128)(2,1)S(1)} %collective-permute-done.8.refs_7_), channel_id=1, source_target_pairs={{0,4},{4,8},{8,12},{12,14},{14,10},{10,6},{6,2},{2,0},{1,5},{5,9},... | collective-permute-start | bytes 393224 | tf_op jit(solution)/shard_map/ppermute | solution.py:170
  15.4 1.9 %collective-permute-done.14.refs_15_.refs_7_ = bf16[16,4096]{1,0:T(8,128)(2,1)S(1)} collective-permute-done((bf16[16,4096]{1,0:T(8,128)(2,1)}, bf16[16,4096]{1,0:T(8,128)(2,1)S(1)}, u32[]{:S(2)}, u32[]{:S(2)}) %collective-permute-start.14) | collective-permute-done | bytes 131104 | tf_op jit(solution)/shard_map/ppermute | solution.py:170
  17.3 1.5 %collective-permute-start.15 = (bf16[16,4096]{1,0:T(8,128)(2,1)S(1)}, bf16[16,4096]{1,0:T(8,128)(2,1)S(1)}, u32[]{:S(2)}, u32[]{:S(2)}) collective-permute-start(bf16[16,4096]{1,0:T(8,128)(2,1)S(1)} %collective-permute-done.14.refs_15_.refs_7_), channel_id=1, source_target_pairs={{0,4},{4,8},{8,12},{12,14},{14,10},{10,6},{6,2},{2,0},{1,5},{5,9},... | collective-permute-start | bytes 393224 | tf_op jit(solution)/shard_map/ppermute | solution.py:170
  18.8 0.0 collective-permute-done.5.refs_1_
  18.9 0.0 collective-permute-start.6
  18.9 2.1 %collective-permute-done.2.refs_10_.refs_2_ = bf16[16,4096]{1,0:T(8,128)(2,1)S(1)} collective-permute-done((bf16[16,4096]{1,0:T(8,128)(2,1)S(1)}, bf16[16,4096]{1,0:T(8,128)(2,1)S(1)}, u32[]{:S(2)}, u32[]{:S(2)}) %collective-permute-start.2) | collective-permute-done | bytes 131104 | tf_op jit(solution)/shard_map/ppermute | solution.py:172
  20.9 0.0 collective-permute-start.3
  21.0 0.0 collective-permute-done.9.refs_6_
  21.0 0.0 collective-permute-done.11.refs_19_
  21.0 1.4 %collective-permute-start.13 = (bf16[16,4096]{1,0:T(8,128)(2,1)S(1)}, bf16[16,4096]{1,0:T(8,128)(2,1)S(1)}, u32[]{:S(2)}, u32[]{:S(2)}) collective-permute-start(bf16[16,4096]{1,0:T(8,128)(2,1)S(1)} %collective-permute-done.9.refs_6_), channel_id=1, source_target_pairs={{0,4},{4,8},{8,12},{12,14},{14,10},{10,6},{6,2},{2,0},{1,5},{5,9},... | collective-permute-start | bytes 393224 | tf_op jit(solution)/shard_map/ppermute | solution.py:170
  22.4 0.0 collective-permute-done.15.refs_14_.refs_6_
  22.4 1.3 %collective-permute-start.16 = (bf16[16,4096]{1,0:T(8,128)(2,1)S(1)}, bf16[16,4096]{1,0:T(8,128)(2,1)S(1)}, u32[]{:S(2)}, u32[]{:S(2)}) collective-permute-start(bf16[16,4096]{1,0:T(8,128)(2,1)S(1)} %collective-permute-done.15.refs_14_.refs_6_), channel_id=1, source_target_pairs={{0,4},{4,8},{8,12},{12,14},{14,10},{10,6},{6,2},{2,0},{1,5},{5,9},... | collective-permute-start | bytes 393224 | tf_op jit(solution)/shard_map/ppermute | solution.py:170
  23.7 0.0 collective-permute-done.6.refs_2_
  23.7 0.2 collective-permute-start.7
  23.9 2.3 %collective-permute-done.3.refs_2_.refs_11_.refs_3_ = bf16[16,4096]{1,0:T(8,128)(2,1)S(1)} collective-permute-done((bf16[16,4096]{1,0:T(8,128)(2,1)S(1)}, bf16[16,4096]{1,0:T(8,128)(2,1)S(1)}, u32[]{:S(2)}, u32[]{:S(2)}) %collective-permute-start.3) | collective-permute-done | bytes 131104 | tf_op jit(solution)/shard_map/ppermute | solution.py:172
  26.2 0.0 collective-permute-start.4
  26.2 0.1 collective-permute-done.13.refs_1_.refs_5_
  26.4 1.3 %collective-permute-start.17 = (bf16[16,4096]{1,0:T(8,128)(2,1)S(1)}, bf16[16,4096]{1,0:T(8,128)(2,1)S(1)}, u32[]{:S(2)}, u32[]{:S(2)}) collective-permute-start(bf16[16,4096]{1,0:T(8,128)(2,1)S(1)} %collective-permute-done.13.refs_1_.refs_5_), channel_id=1, source_target_pairs={{0,4},{4,8},{8,12},{12,14},{14,10},{10,6},{6,2},{2,0},{1,5},{5,9},... | collective-permute-start | bytes 393224 | tf_op jit(solution)/shard_map/ppermute | solution.py:170
  27.7 0.7 dynamic-slice_bitcast_fusion.facts
  28.4 0.0 collective-permute-done.16.refs_3_.refs_13_.refs_5_
  28.4 0.8 %collective-permute-done.7.refs_0_.refs_3_ = bf16[16,4096]{1,0:T(8,128)(2,1)S(1)} collective-permute-done((bf16[16,4096]{1,0:T(8,128)(2,1)S(1)}, bf16[16,4096]{1,0:T(8,128)(2,1)S(1)}, u32[]{:S(2)}, u32[]{:S(2)}) %collective-permute-start.7) | collective-permute-done | bytes 131104 | tf_op jit(solution)/shard_map/ppermute | solution.py:172
  29.2 3.4 %fetch.1 = (bf16[2048,2048]{1,0:T(8,128)(2,1)S(1)}, f32[8,128]{1,0:T(8,128)S(1)}) custom-call(bf16[8192,2048]{1,0:T(8,128)(2,1)} %refs_9_.3, bf16[16,4096]{1,0:T(8,128)(2,1)S(1)} %collective-permute-done.7.refs_0_.refs_3_, bf16[16,4096]{1,0:T(8,128)(2,1)S(1)} %collective-permute-done.13.refs_1_.refs_5_, ...), custom_call_target="tpu_custom_call" | custom-call | bytes 16777216 | tf_op jit(solution)/shard_map/fetch/pallas_call | solution.py:218
  32.6 0.0 collective-permute-done.4.refs_12_.refs_4_
  32.7 0.0 collective-permute-done.17.refs_4_
  32.7 0.0 copy-done
  32.7 0.0 copy-done.1
  32.7 0.6 rank_part.1.a
  33.3 0.7 collective-permute-start.18
  34.0 5.6 %project_0.1 = (f32[128,2048]{1,0:T(8,128)S(1)}, bf16[1280,2048]{1,0:T(8,128)(2,1)S(1)}) custom-call(s32[14]{0:T(128)S(1)} %dynamic-slice_bitcast_fusion.facts, bf16[16,4096]{1,0:T(8,128)(2,1)S(1)} %copy-done.1, bf16[16,4096]{1,0:T(8,128)(2,1)S(1)} %collective-permute-done.5.refs_1_, bf16[16,4096]{1,0:T(8,128)(2,1)S(1)} %collective-permute-done.6.refs_2_, ...), custom_call_target="tpu_custom_call" | custom-call | flops 2147483648 | bytes 16777216 | tf_op jit(solution)/shard_map/project_0/pallas_call | solution.py:352
  39.5 0.0 collective-permute-done.18.b
  39.6 0.0 copy-start.2
  39.6 1.4 %collective-permute-start.19 = (f32[128,128]{1,0:T(8,128)S(1)}, f32[128,128]{1,0:T(8,128)S(1)}, u32[]{:S(2)}, u32[]{:S(2)}) collective-permute-start(f32[128,128]{1,0:T(8,128)S(1)} %add.10.a), channel_id=1, source_target_pairs={{0,8},{2,10},{4,12},{6,14},{9,1},{11,3},{13,5},{15,7},{16,24},{18,... | collective-permute-start | bytes 196616 | tf_op jit(solution)/shard_map/ppermute | solution.py:550
  41.0 5.3 %project_4096.1 = (f32[64,2048]{1,0:T(8,128)S(1)}, f32[64,2048]{1,0:T(8,128)S(1)}) custom-call(s32[14]{0:T(128)S(1)} %dynamic-slice_bitcast_fusion.facts, bf16[16,4096]{1,0:T(8,128)(2,1)S(1)} %copy-done, bf16[16,4096]{1,0:T(8,128)(2,1)S(1)} %collective-permute-done.1.refs_9_.refs_1_, bf16[16,4096]{1,0:T(8,128)(2,1)S(1)} %collective-permute-done.2.refs_10_.refs_2_, ...), custom_call_target="tpu_custom_call" | custom-call | flops 2147483648 | bytes 16777216 | tf_op jit(solution)/shard_map/project_4096/pallas_call | solution.py:352
  46.3 2.1 %collective-permute-done.19.b = f32[128,128]{1,0:T(8,128)S(1)} collective-permute-done((f32[128,128]{1,0:T(8,128)S(1)}, f32[128,128]{1,0:T(8,128)S(1)}, u32[]{:S(2)}, u32[]{:S(2)}) %collective-permute-start.19) | collective-permute-done | bytes 65568 | tf_op jit(solution)/shard_map/ppermute | solution.py:550
  48.4 4.6 %collective-permute-start.20 = (f32[64,2048]{1,0:T(8,128)S(1)}, f32[64,2048]{1,0:T(8,128)S(1)}, u32[]{:S(2)}, u32[]{:S(2)}) collective-permute-start(f32[64,2048]{1,0:T(8,128)S(1)} %get-tuple-element.54), channel_id=1, source_target_pairs={{0,1},{1,0},{2,3},{3,2},{4,5},{5,4},{6,7},{7,6},{8,9},{9,8},{10,11... | collective-permute-start | bytes 1572872 | tf_op jit(solution)/shard_map/ppermute | solution.py:556
  53.0 0.6 split.1
  53.5 0.1 collective-permute-start.21
  53.6 1.2 %collective-permute-done.21.ranked_received = f32[64,128]{1,0:T(8,128)S(1)} collective-permute-done((f32[64,128]{1,0:T(8,128)S(1)}, f32[64,128]{1,0:T(8,128)S(1)}, u32[]{:S(2)}, u32[]{:S(2)}) %collective-permute-start.21) | collective-permute-done | bytes 32800 | tf_op jit(solution)/shard_map/ppermute | solution.py:555
  54.8 0.0 collective-permute-done.20.received
  54.8 1.0 %finish.1 = (bf16[4,4,2048]{2,1,0:T(4,128)(2,1)S(1)}, bf16[4,4,2048]{2,1,0:T(4,128)(2,1)S(1)}, bf16[4,4,2048]{2,1,0:T(4,128)(2,1)S(1)}, bf16[4,4,2048]{2,1,0:T(4,128)(2,1)S(1)}) custom-call(s32[14]{0:T(128)S(1)} %dynamic-slice_bitcast_fusion.facts, f32[64,2048]{1,0:T(8,128)S(1)} %get-tuple-element.53.keep, f32[64,2048]{1,0:T(8,128)S(1)} %collective-permute-done.20.received, ...), custom_call_target="tpu_custom_call" | custom-call | tf_op jit(solution)/shard_map/finish/pallas_call | solution.py:441
  55.9 1.9 %collective-permute-start.22 = (bf16[4,4,2048]{2,1,0:T(4,128)(2,1)S(1)}, bf16[4,4,2048]{2,1,0:T(4,128)(2,1)S(1)}, u32[]{:S(2)}, u32[]{:S(2)}) collective-permute-start(bf16[4,4,2048]{2,1,0:T(4,128)(2,1)S(1)} %get-tuple-element.59), channel_id=1, source_target_pairs={{0,0},{1,8},{2,2},{3,10},{4,4},{5,12},{6,6},{7,14},{8,9},{9,1},{10... | collective-permute-start | bytes 196616 | tf_op jit(solution)/shard_map/ppermute | solution.py:567
  57.8 1.3 %collective-permute-start.23 = (bf16[4,4,2048]{2,1,0:T(4,128)(2,1)S(1)}, bf16[4,4,2048]{2,1,0:T(4,128)(2,1)S(1)}, u32[]{:S(2)}, u32[]{:S(2)}) collective-permute-start(bf16[4,4,2048]{2,1,0:T(4,128)(2,1)S(1)} %get-tuple-element.60), channel_id=1, source_target_pairs={{0,2},{1,10},{2,0},{3,8},{4,6},{5,14},{6,4},{7,12},{8,11},{9,3},{1... | collective-permute-start | bytes 196616 | tf_op jit(solution)/shard_map/ppermute | solution.py:567
  59.1 3.5 %collective-permute-start.24 = (bf16[4,4,2048]{2,1,0:T(4,128)(2,1)S(1)}, bf16[4,4,2048]{2,1,0:T(4,128)(2,1)S(1)}, u32[]{:S(2)}, u32[]{:S(2)}) collective-permute-start(bf16[4,4,2048]{2,1,0:T(4,128)(2,1)S(1)} %get-tuple-element.61), channel_id=1, source_target_pairs={{0,4},{1,12},{2,6},{3,14},{4,0},{5,8},{6,2},{7,10},{8,13},{9,5},{1... | collective-permute-start | bytes 196616 | tf_op jit(solution)/shard_map/ppermute | solution.py:567
  62.6 0.5 collective-permute-start.25
  63.1 0.0 collective-permute-done.22.refs_0_
  63.1 2.8 %collective-permute-done.23.refs_1_ = bf16[4,4,2048]{2,1,0:T(4,128)(2,1)S(1)} collective-permute-done((bf16[4,4,2048]{2,1,0:T(4,128)(2,1)S(1)}, bf16[4,4,2048]{2,1,0:T(4,128)(2,1)S(1)}, u32[]{:S(2)}, u32[]{:S(2)}) %collective-permute-start.23) | collective-permute-done | bytes 65568 | tf_op jit(solution)/shard_map/ppermute | solution.py:567
  65.9 0.0 collective-permute-done.24.refs_2_
  65.9 2.5 %collective-permute-done.25.refs_3_ = bf16[4,4,2048]{2,1,0:T(4,128)(2,1)S(1)} collective-permute-done((bf16[4,4,2048]{2,1,0:T(4,128)(2,1)S(1)}, bf16[4,4,2048]{2,1,0:T(4,128)(2,1)S(1)}, u32[]{:S(2)}, u32[]{:S(2)}) %collective-permute-start.25) | collective-permute-done | bytes 65568 | tf_op jit(solution)/shard_map/ppermute | solution.py:567
  68.5 1.3 %place.1 = bf16[4,4,8192]{2,1,0:T(4,128)(2,1)} custom-call(s32[14]{0:T(128)S(1)} %dynamic-slice_bitcast_fusion.facts, bf16[4,4,2048]{2,1,0:T(4,128)(2,1)S(1)} %collective-permute-done.22.refs_0_, bf16[4,4,2048]{2,1,0:T(4,128)(2,1)S(1)} %collective-permute-done.23.refs_1_, bf16[4,4,2048]{2,1,0:T(4,128)(2,1)S(1)} %collective-permute-done.24.refs_2_, ...), custom_call_target="tpu_custom_call" | custom-call | tf_op jit(solution)/shard_map/place/pallas_call | solution.py:469
  (6 shorter events, 0.0 us)
Async XLA Ops:
  0.0 9.1 %collective-permute-start = (bf16[64,2048]{1,0:T(8,128)(2,1)}, bf16[64,2048]{1,0:T(8,128)(2,1)S(1)}, u32[]{:S(2)}, u32[]{:S(2)}) collective-permute-start(bf16[64,2048]{1,0:T(8,128)(2,1)} %bitcast.7), channel_id=1, source_target_pairs={{0,2},{2,0},{4,6},{6,4},{8,10},{10,8},{12,14},{14,12},{1,3},{3,1},... | collective-permute-start | bytes 786440 | tf_op jit(solution)/shard_map/ppermute | solution.py:509
  2.1 9.6 %collective-permute-start.10 = (bf16[64,2048]{1,0:T(8,128)(2,1)}, bf16[64,2048]{1,0:T(8,128)(2,1)S(1)}, u32[]{:S(2)}, u32[]{:S(2)}) collective-permute-start(bf16[64,2048]{1,0:T(8,128)(2,1)} %bitcast.8), channel_id=1, source_target_pairs={{0,1},{1,0},{2,3},{3,2},{4,5},{5,4},{6,7},{7,6},{8,9},{9,8},{10,11... | collective-permute-start | bytes 786440 | tf_op jit(solution)/shard_map/ppermute | solution.py:524
  3.0 10.1 %collective-permute-start.12 = (bf16[64,2048]{1,0:T(8,128)(2,1)}, bf16[64,2048]{1,0:T(8,128)(2,1)S(1)}, u32[]{:S(2)}, u32[]{:S(2)}) collective-permute-start(bf16[64,2048]{1,0:T(8,128)(2,1)} %own.1), channel_id=1, source_target_pairs={{0,1},{1,0},{2,3},{3,2},{4,5},{5,4},{6,7},{7,6},{8,9},{9,8},{10,11... | collective-permute-start | bytes 786440 | tf_op jit(solution)/shard_map/ppermute | solution.py:524
  9.1 4.8 %collective-permute-start.1 = (bf16[16,4096]{1,0:T(8,128)(2,1)}, bf16[16,4096]{1,0:T(8,128)(2,1)S(1)}, u32[]{:S(2)}, u32[]{:S(2)}) collective-permute-start(bf16[16,4096]{1,0:T(8,128)(2,1)} %get-tuple-element.36.refs_8_.refs_0_), channel_id=1, source_target_pairs={{4,0},{8,4},{12,8},{14,12},{10,14},{6,10},{2,6},{0,2},{5,1},{9,5},... | collective-permute-start | bytes 393224 | tf_op jit(solution)/shard_map/ppermute | solution.py:172
  9.5 5.1 %collective-permute-start.8 = (bf16[16,4096]{1,0:T(8,128)(2,1)}, bf16[16,4096]{1,0:T(8,128)(2,1)S(1)}, u32[]{:S(2)}, u32[]{:S(2)}) collective-permute-start(bf16[16,4096]{1,0:T(8,128)(2,1)} %get-tuple-element.37.refs_0_), channel_id=1, source_target_pairs={{0,4},{4,8},{8,12},{12,14},{14,10},{10,6},{6,2},{2,0},{1,5},{5,9},... | collective-permute-start | bytes 393224 | tf_op jit(solution)/shard_map/ppermute | solution.py:170
  10.6 10.4 %collective-permute-start.11 = (bf16[64,2048]{1,0:T(8,128)(2,1)S(1)}, bf16[64,2048]{1,0:T(8,128)(2,1)S(1)}, u32[]{:S(2)}, u32[]{:S(2)}) collective-permute-start(bf16[64,2048]{1,0:T(8,128)(2,1)S(1)} %collective-permute-done.refs_17_), channel_id=1, source_target_pairs={{0,1},{1,0},{2,3},{3,2},{4,5},{5,4},{6,7},{7,6},{8,9},{9,8},{10,11... | collective-permute-start | bytes 786440 | tf_op jit(solution)/shard_map/ppermute | solution.py:524
  11.7 5.6 %collective-permute-start.14 = (bf16[16,4096]{1,0:T(8,128)(2,1)}, bf16[16,4096]{1,0:T(8,128)(2,1)S(1)}, u32[]{:S(2)}, u32[]{:S(2)}) collective-permute-start(bf16[16,4096]{1,0:T(8,128)(2,1)} %get-tuple-element.36.refs_8_.refs_0_), channel_id=1, source_target_pairs={{0,4},{4,8},{8,12},{12,14},{14,10},{10,6},{6,2},{2,0},{1,5},{5,9},... | collective-permute-start | bytes 393224 | tf_op jit(solution)/shard_map/ppermute | solution.py:170
  13.1 5.8 %collective-permute-start.5 = (bf16[16,4096]{1,0:T(8,128)(2,1)}, bf16[16,4096]{1,0:T(8,128)(2,1)S(1)}, u32[]{:S(2)}, u32[]{:S(2)}) collective-permute-start(bf16[16,4096]{1,0:T(8,128)(2,1)} %get-tuple-element.37.refs_0_), channel_id=1, source_target_pairs={{4,0},{8,4},{12,8},{14,12},{10,14},{6,10},{2,6},{0,2},{5,1},{9,5},... | collective-permute-start | bytes 393224 | tf_op jit(solution)/shard_map/ppermute | solution.py:172
  13.9 7.0 %collective-permute-start.2 = (bf16[16,4096]{1,0:T(8,128)(2,1)S(1)}, bf16[16,4096]{1,0:T(8,128)(2,1)S(1)}, u32[]{:S(2)}, u32[]{:S(2)}) collective-permute-start(bf16[16,4096]{1,0:T(8,128)(2,1)S(1)} %collective-permute-done.1.refs_9_.refs_1_), channel_id=1, source_target_pairs={{4,0},{8,4},{12,8},{14,12},{10,14},{6,10},{2,6},{0,2},{5,1},{9,5},... | collective-permute-start | bytes 393224 | tf_op jit(solution)/shard_map/ppermute | solution.py:172
  14.5 6.4 %collective-permute-start.9 = (bf16[16,4096]{1,0:T(8,128)(2,1)S(1)}, bf16[16,4096]{1,0:T(8,128)(2,1)S(1)}, u32[]{:S(2)}, u32[]{:S(2)}) collective-permute-start(bf16[16,4096]{1,0:T(8,128)(2,1)S(1)} %collective-permute-done.8.refs_7_), channel_id=1, source_target_pairs={{0,4},{4,8},{8,12},{12,14},{14,10},{10,6},{6,2},{2,0},{1,5},{5,9},... | collective-permute-start | bytes 393224 | tf_op jit(solution)/shard_map/ppermute | solution.py:170
  17.3 5.1 %collective-permute-start.15 = (bf16[16,4096]{1,0:T(8,128)(2,1)S(1)}, bf16[16,4096]{1,0:T(8,128)(2,1)S(1)}, u32[]{:S(2)}, u32[]{:S(2)}) collective-permute-start(bf16[16,4096]{1,0:T(8,128)(2,1)S(1)} %collective-permute-done.14.refs_15_.refs_7_), channel_id=1, source_target_pairs={{0,4},{4,8},{8,12},{12,14},{14,10},{10,6},{6,2},{2,0},{1,5},{5,9},... | collective-permute-start | bytes 393224 | tf_op jit(solution)/shard_map/ppermute | solution.py:170
  18.9 4.8 %collective-permute-start.6 = (bf16[16,4096]{1,0:T(8,128)(2,1)S(1)}, bf16[16,4096]{1,0:T(8,128)(2,1)S(1)}, u32[]{:S(2)}, u32[]{:S(2)}) collective-permute-start(bf16[16,4096]{1,0:T(8,128)(2,1)S(1)} %collective-permute-done.5.refs_1_), channel_id=1, source_target_pairs={{4,0},{8,4},{12,8},{14,12},{10,14},{6,10},{2,6},{0,2},{5,1},{9,5},... | collective-permute-start | bytes 393224 | tf_op jit(solution)/shard_map/ppermute | solution.py:172
  20.9 5.3 %collective-permute-start.3 = (bf16[16,4096]{1,0:T(8,128)(2,1)S(1)}, bf16[16,4096]{1,0:T(8,128)(2,1)S(1)}, u32[]{:S(2)}, u32[]{:S(2)}) collective-permute-start(bf16[16,4096]{1,0:T(8,128)(2,1)S(1)} %collective-permute-done.2.refs_10_.refs_2_), channel_id=1, source_target_pairs={{4,0},{8,4},{12,8},{14,12},{10,14},{6,10},{2,6},{0,2},{5,1},{9,5},... | collective-permute-start | bytes 393224 | tf_op jit(solution)/shard_map/ppermute | solution.py:172
  21.0 5.4 %collective-permute-start.13 = (bf16[16,4096]{1,0:T(8,128)(2,1)S(1)}, bf16[16,4096]{1,0:T(8,128)(2,1)S(1)}, u32[]{:S(2)}, u32[]{:S(2)}) collective-permute-start(bf16[16,4096]{1,0:T(8,128)(2,1)S(1)} %collective-permute-done.9.refs_6_), channel_id=1, source_target_pairs={{0,4},{4,8},{8,12},{12,14},{14,10},{10,6},{6,2},{2,0},{1,5},{5,9},... | collective-permute-start | bytes 393224 | tf_op jit(solution)/shard_map/ppermute | solution.py:170
  22.4 6.0 %collective-permute-start.16 = (bf16[16,4096]{1,0:T(8,128)(2,1)S(1)}, bf16[16,4096]{1,0:T(8,128)(2,1)S(1)}, u32[]{:S(2)}, u32[]{:S(2)}) collective-permute-start(bf16[16,4096]{1,0:T(8,128)(2,1)S(1)} %collective-permute-done.15.refs_14_.refs_6_), channel_id=1, source_target_pairs={{0,4},{4,8},{8,12},{12,14},{14,10},{10,6},{6,2},{2,0},{1,5},{5,9},... | collective-permute-start | bytes 393224 | tf_op jit(solution)/shard_map/ppermute | solution.py:170
  23.7 5.5 %collective-permute-start.7 = (bf16[16,4096]{1,0:T(8,128)(2,1)S(1)}, bf16[16,4096]{1,0:T(8,128)(2,1)S(1)}, u32[]{:S(2)}, u32[]{:S(2)}) collective-permute-start(bf16[16,4096]{1,0:T(8,128)(2,1)S(1)} %collective-permute-done.6.refs_2_), channel_id=1, source_target_pairs={{4,0},{8,4},{12,8},{14,12},{10,14},{6,10},{2,6},{0,2},{5,1},{9,5},... | collective-permute-start | bytes 393224 | tf_op jit(solution)/shard_map/ppermute | solution.py:172
  26.2 6.4 %collective-permute-start.4 = (bf16[16,4096]{1,0:T(8,128)(2,1)S(1)}, bf16[16,4096]{1,0:T(8,128)(2,1)S(1)}, u32[]{:S(2)}, u32[]{:S(2)}) collective-permute-start(bf16[16,4096]{1,0:T(8,128)(2,1)S(1)} %collective-permute-done.3.refs_2_.refs_11_.refs_3_), channel_id=1, source_target_pairs={{4,0},{8,4},{12,8},{14,12},{10,14},{6,10},{2,6},{0,2},{5,1},{9,5},... | collective-permute-start | bytes 393224 | tf_op jit(solution)/shard_map/ppermute | solution.py:172
  26.4 6.3 %collective-permute-start.17 = (bf16[16,4096]{1,0:T(8,128)(2,1)S(1)}, bf16[16,4096]{1,0:T(8,128)(2,1)S(1)}, u32[]{:S(2)}, u32[]{:S(2)}) collective-permute-start(bf16[16,4096]{1,0:T(8,128)(2,1)S(1)} %collective-permute-done.13.refs_1_.refs_5_), channel_id=1, source_target_pairs={{0,4},{4,8},{8,12},{12,14},{14,10},{10,6},{6,2},{2,0},{1,5},{5,9},... | collective-permute-start | bytes 393224 | tf_op jit(solution)/shard_map/ppermute | solution.py:170
  28.4 4.3 %copy-start = (bf16[16,4096]{1,0:T(8,128)(2,1)S(1)}, bf16[16,4096]{1,0:T(8,128)(2,1)}, u32[]{:S(2)}) copy-start(bf16[16,4096]{1,0:T(8,128)(2,1)} %get-tuple-element.36.refs_8_.refs_0_) | copy-start | bytes 393220
  28.4 4.3 %copy-start.1 = (bf16[16,4096]{1,0:T(8,128)(2,1)S(1)}, bf16[16,4096]{1,0:T(8,128)(2,1)}, u32[]{:S(2)}) copy-start(bf16[16,4096]{1,0:T(8,128)(2,1)} %get-tuple-element.37.refs_0_) | copy-start | bytes 393220
  28.4 4.3 %copy-start.3 = (bf16[2048,64]{0,1:T(8,128)(2,1)S(1)}, bf16[2048,64]{0,1:T(8,128)(2,1)}, u32[]{:S(2)}) copy-start(bf16[2048,64]{0,1:T(8,128)(2,1)} %param.17) | copy-start | bytes 786436
  33.3 6.2 %collective-permute-start.18 = (f32[128,128]{1,0:T(8,128)S(1)}, f32[128,128]{1,0:T(8,128)S(1)}, u32[]{:S(2)}, u32[]{:S(2)}) collective-permute-start(f32[128,128]{1,0:T(8,128)S(1)} %rank_part.1.a), channel_id=1, source_target_pairs={{0,4},{2,6},{4,0},{6,2},{9,13},{11,15},{13,9},{15,11},{16,20},{18,... | collective-permute-start | bytes 196616 | tf_op jit(solution)/shard_map/ppermute | solution.py:544
  39.6 15.3 %copy-start.2 = (bf16[64,2048]{1,0:T(8,128)(2,1)S(1)}, bf16[64,2048]{1,0:T(8,128)(2,1)}, u32[]{:S(2)}) copy-start(bf16[64,2048]{1,0:T(8,128)(2,1)} %own.1) | copy-start | bytes 786436
  39.6 8.9 %collective-permute-start.19 = (f32[128,128]{1,0:T(8,128)S(1)}, f32[128,128]{1,0:T(8,128)S(1)}, u32[]{:S(2)}, u32[]{:S(2)}) collective-permute-start(f32[128,128]{1,0:T(8,128)S(1)} %add.10.a), channel_id=1, source_target_pairs={{0,8},{2,10},{4,12},{6,14},{9,1},{11,3},{13,5},{15,7},{16,24},{18,... | collective-permute-start | bytes 196616 | tf_op jit(solution)/shard_map/ppermute | solution.py:550
  48.4 6.4 %collective-permute-start.20 = (f32[64,2048]{1,0:T(8,128)S(1)}, f32[64,2048]{1,0:T(8,128)S(1)}, u32[]{:S(2)}, u32[]{:S(2)}) collective-permute-start(f32[64,2048]{1,0:T(8,128)S(1)} %get-tuple-element.54), channel_id=1, source_target_pairs={{0,1},{1,0},{2,3},{3,2},{4,5},{5,4},{6,7},{7,6},{8,9},{9,8},{10,11... | collective-permute-start | bytes 1572872 | tf_op jit(solution)/shard_map/ppermute | solution.py:556
  53.5 1.3 %collective-permute-start.21 = (f32[64,128]{1,0:T(8,128)S(1)}, f32[64,128]{1,0:T(8,128)S(1)}, u32[]{:S(2)}, u32[]{:S(2)}) collective-permute-start(f32[64,128]{1,0:T(8,128)S(1)} %get-tuple-element.57), channel_id=1, source_target_pairs={{0,1},{1,0},{2,3},{3,2},{4,5},{5,4},{6,7},{7,6},{8,9},{9,8},{10,11... | collective-permute-start | bytes 98312 | tf_op jit(solution)/shard_map/ppermute | solution.py:555
  55.9 7.2 %collective-permute-start.22 = (bf16[4,4,2048]{2,1,0:T(4,128)(2,1)S(1)}, bf16[4,4,2048]{2,1,0:T(4,128)(2,1)S(1)}, u32[]{:S(2)}, u32[]{:S(2)}) collective-permute-start(bf16[4,4,2048]{2,1,0:T(4,128)(2,1)S(1)} %get-tuple-element.59), channel_id=1, source_target_pairs={{0,0},{1,8},{2,2},{3,10},{4,4},{5,12},{6,6},{7,14},{8,9},{9,1},{10... | collective-permute-start | bytes 196616 | tf_op jit(solution)/shard_map/ppermute | solution.py:567
  57.8 8.1 %collective-permute-start.23 = (bf16[4,4,2048]{2,1,0:T(4,128)(2,1)S(1)}, bf16[4,4,2048]{2,1,0:T(4,128)(2,1)S(1)}, u32[]{:S(2)}, u32[]{:S(2)}) collective-permute-start(bf16[4,4,2048]{2,1,0:T(4,128)(2,1)S(1)} %get-tuple-element.60), channel_id=1, source_target_pairs={{0,2},{1,10},{2,0},{3,8},{4,6},{5,14},{6,4},{7,12},{8,11},{9,3},{1... | collective-permute-start | bytes 196616 | tf_op jit(solution)/shard_map/ppermute | solution.py:567
  59.1 6.8 %collective-permute-start.24 = (bf16[4,4,2048]{2,1,0:T(4,128)(2,1)S(1)}, bf16[4,4,2048]{2,1,0:T(4,128)(2,1)S(1)}, u32[]{:S(2)}, u32[]{:S(2)}) collective-permute-start(bf16[4,4,2048]{2,1,0:T(4,128)(2,1)S(1)} %get-tuple-element.61), channel_id=1, source_target_pairs={{0,4},{1,12},{2,6},{3,14},{4,0},{5,8},{6,2},{7,10},{8,13},{9,5},{1... | collective-permute-start | bytes 196616 | tf_op jit(solution)/shard_map/ppermute | solution.py:567
  62.6 5.8 %collective-permute-start.25 = (bf16[4,4,2048]{2,1,0:T(4,128)(2,1)S(1)}, bf16[4,4,2048]{2,1,0:T(4,128)(2,1)S(1)}, u32[]{:S(2)}, u32[]{:S(2)}) collective-permute-start(bf16[4,4,2048]{2,1,0:T(4,128)(2,1)S(1)} %get-tuple-element.62), channel_id=1, source_target_pairs={{0,6},{1,14},{2,4},{3,12},{4,2},{5,10},{6,0},{7,8},{8,15},{9,7},{1... | collective-permute-start | bytes 196616 | tf_op jit(solution)/shard_map/ppermute | solution.py:567

commit v5 on v4

--- a/solution.py
+++ b/solution.py
@@ -13,7 +13,7 @@
 chunk_count = 2
 fetched = 64
 ahead_share = 5
-staged_rows = 2
+staged_rows = 4
 tile_rows = 512
 mebibyte = 1024 * 1024
 
@@ -172,6 +172,17 @@
         blocks[step] = lax.ppermute(blocks[step - 1], "fsdp", down)
 
 
+def output_step(count, core, offset):
+    half = count // 2
+    return offset ^ ((core ^ (1 if offset >= max(half // 2, 1) else 0)) * half)
+
+
+def row_slot(count, chip):
+    half = count // 2
+    mine = chip % half
+    return ((chip // half) ^ (1 if mine >= max(half // 2, 1) else 0)) * half + mine
+
+
 def facts_table(count, own_width, width):
     order = ring_order(count)
     position = {f: i for i, f in enumerate(order)}
@@ -182,8 +193,9 @@
             side, mine = chip // half, chip % half
             start = mine // 2 * 2 * own_width
             owner = start // width if core == side else -1
-            places = [order[(position[chip] + i) % count] for i in range(count)]
-            rows.append([core, core ^ side, mine, owner, start % width, chip % 2] + places)
+            places = [row_slot(count, order[(position[chip] + i) % count]) for i in range(count)]
+            kept = core ^ (row_slot(count, chip) // half)
+            rows.append([core, kept, mine, owner, start % width, chip % 2] + places)
     return np.array(rows, np.int32)
 
 
@@ -560,7 +572,7 @@
     landed = []
     for offset, piece in enumerate(pieces):
         pairs = [
-            (2 * f + t, 2 * (f ^ (t * half + offset)) + f // half)
+            (2 * f + t, 2 * (f ^ output_step(count, t, offset)) + f // half)
             for f in range(count)
             for t in range(2)
         ]

time: 70 us -> 69.9 us (level); the launches traced: 69.7 us -> 68.7 us
  starting transfers between devices: 28.3 us -> 27.4 us
    ppermute x4, starting transfers between devices: 7.22 us -> 6.36 us  [shards(): landed.append(lax.ppermute(piece, both, pairs))]
  transfers between devices with their start and end apart: 26 -> 26, of which waited for: 10 -> 9; matrix products, arithmetic and copies ran while one was open for 1% -> 1% of each run, Pallas kernels for 30% -> 30%
where the time goes in v5:
time: 69.9 us; the launch traced here: 68.7 us
  starting transfers between devices  27.4 us (39%)
  Pallas kernels  23.7 us (34%)
  waiting for transfers between devices  16.7 us (24%)
  local copies, waits for them, and re-layouts  0.71 us (1%)
    pallas_call x2, Pallas kernels, project(): pl.pallas_call(functools.partial(project_kernel, start, stop, first, ahea...  10.9 us
    ppermute x7, starting transfers between devices, ring_step(): blocks[count - step] = lax.ppermute(blocks[(1 - step) % count], 'fsdp', up)  9.02 us
    ppermute x4, starting transfers between devices, shards(): landed.append(lax.ppermute(piece, both, pairs))  6.36 us
    ppermute x7, waiting for transfers between devices, ring_step(): blocks[step] = lax.ppermute(blocks[step - 1], 'fsdp', down)  6.03 us
    pallas_call x1, Pallas kernels, attend(): pl.pallas_call(attend_kernel, in_specs=[smem] + [anywhere] * 5, out_specs...  6.02 us
    ppermute x4, waiting for transfers between devices, shards(): landed.append(lax.ppermute(piece, both, pairs))  5.22 us
    ppermute x1, starting transfers between devices, shards(): received = lax.ppermute(send, 'tp', swap)  4.56 us
    pallas_call x1, Pallas kernels, fetch(): pl.pallas_call(fetch_kernel, in_specs=[pl.BlockSpec(memory_space=pl.ANY)]...  3.39 us
  transfers between devices with their start and end apart: 26, of which 9 were waited for; matrix products, arithmetic and copies ran while one was open for 1% of the time, Pallas kernels for 30%

profile of v5, /device:TPU:1, one launch (start us, length us, event | category | flops | bytes accessed | tf_op | source)
XLA Modules:
  0.0 68.7 jit_solution(13655130071899256156)
XLA Ops:
  0.0 2.1 %collective-permute-start = (bf16[64,2048]{1,0:T(8,128)(2,1)}, bf16[64,2048]{1,0:T(8,128)(2,1)S(1)}, u32[]{:S(2)}, u32[]{:S(2)}) collective-permute-start(bf16[64,2048]{1,0:T(8,128)(2,1)} %bitcast.7), channel_id=1, source_target_pairs={{0,2},{2,0},{4,6},{6,4},{8,10},{10,8},{12,14},{14,12},{1,3},{3,1},... | collective-permute-start | bytes 786440 | tf_op jit(solution)/shard_map/ppermute | solution.py:521
  2.1 1.0 %collective-permute-start.10 = (bf16[64,2048]{1,0:T(8,128)(2,1)}, bf16[64,2048]{1,0:T(8,128)(2,1)S(1)}, u32[]{:S(2)}, u32[]{:S(2)}) collective-permute-start(bf16[64,2048]{1,0:T(8,128)(2,1)} %bitcast.8), channel_id=1, source_target_pairs={{0,1},{1,0},{2,3},{3,2},{4,5},{5,4},{6,7},{7,6},{8,9},{9,8},{10,11... | collective-permute-start | bytes 786440 | tf_op jit(solution)/shard_map/ppermute | solution.py:536
  3.0 0.0 collective-permute-start.12
  3.0 6.0 %attend.1 = (bf16[16,4096]{1,0:T(8,128)(2,1)}, bf16[16,4096]{1,0:T(8,128)(2,1)}) custom-call(s32[4]{0:T(128)} %lengths.1, bf16[4,4,64,128]{3,2,1,0:T(8,128)(2,1)} %queries.1, bf16[4,2048,128]{2,1,0:T(8,128)(2,1)} %bitcast.10, bf16[4,2048,128]{2,1,0:T(8,128)(2,1)} %bitcast.11, bf16[4,16,128]{2,1,0:T(8,128)(2,1)} %bitcast.12, bf16[4,16,128]{2,1,0:T(8,128)(2,1)} %bitcast.13), custom_call_target="tpu_custom_call" | custom-call | flops 1073741824 | bytes 4194304 | tf_op jit(solution)/shard_map/attend/pallas_call | solution.py:125
  9.1 0.0 collective-permute-done.refs_17_
  9.1 0.4 collective-permute-start.1
  9.5 1.1 %collective-permute-start.8 = (bf16[16,4096]{1,0:T(8,128)(2,1)}, bf16[16,4096]{1,0:T(8,128)(2,1)S(1)}, u32[]{:S(2)}, u32[]{:S(2)}) collective-permute-start(bf16[16,4096]{1,0:T(8,128)(2,1)} %get-tuple-element.37.refs_0_), channel_id=1, source_target_pairs={{0,4},{4,8},{8,12},{12,14},{14,10},{10,6},{6,2},{2,0},{1,5},{5,9},... | collective-permute-start | bytes 393224 | tf_op jit(solution)/shard_map/ppermute | solution.py:170
  10.6 1.1 %collective-permute-start.11 = (bf16[64,2048]{1,0:T(8,128)(2,1)S(1)}, bf16[64,2048]{1,0:T(8,128)(2,1)S(1)}, u32[]{:S(2)}, u32[]{:S(2)}) collective-permute-start(bf16[64,2048]{1,0:T(8,128)(2,1)S(1)} %collective-permute-done.refs_17_), channel_id=1, source_target_pairs={{0,1},{1,0},{2,3},{3,2},{4,5},{5,4},{6,7},{7,6},{8,9},{9,8},{10,11... | collective-permute-start | bytes 786440 | tf_op jit(solution)/shard_map/ppermute | solution.py:536
  11.7 0.0 collective-permute-done.10.refs_18_
  11.7 1.4 %collective-permute-start.14 = (bf16[16,4096]{1,0:T(8,128)(2,1)}, bf16[16,4096]{1,0:T(8,128)(2,1)S(1)}, u32[]{:S(2)}, u32[]{:S(2)}) collective-permute-start(bf16[16,4096]{1,0:T(8,128)(2,1)} %get-tuple-element.36.refs_8_.refs_0_), channel_id=1, source_target_pairs={{0,4},{4,8},{8,12},{12,14},{14,10},{10,6},{6,2},{2,0},{1,5},{5,9},... | collective-permute-start | bytes 393224 | tf_op jit(solution)/shard_map/ppermute | solution.py:170
  13.1 0.0 collective-permute-done.12.other
  13.1 0.0 collective-permute-start.5
  13.1 0.8 %collective-permute-done.1.refs_9_.refs_1_ = bf16[16,4096]{1,0:T(8,128)(2,1)S(1)} collective-permute-done((bf16[16,4096]{1,0:T(8,128)(2,1)}, bf16[16,4096]{1,0:T(8,128)(2,1)S(1)}, u32[]{:S(2)}, u32[]{:S(2)}) %collective-permute-start.1) | collective-permute-done | bytes 131104 | tf_op jit(solution)/shard_map/ppermute | solution.py:172
  13.9 0.6 collective-permute-start.2
  14.5 0.0 collective-permute-done.8.refs_7_
  14.5 0.8 %collective-permute-start.9 = (bf16[16,4096]{1,0:T(8,128)(2,1)S(1)}, bf16[16,4096]{1,0:T(8,128)(2,1)S(1)}, u32[]{:S(2)}, u32[]{:S(2)}) collective-permute-start(bf16[16,4096]{1,0:T(8,128)(2,1)S(1)} %collective-permute-done.8.refs_7_), channel_id=1, source_target_pairs={{0,4},{4,8},{8,12},{12,14},{14,10},{10,6},{6,2},{2,0},{1,5},{5,9},... | collective-permute-start | bytes 393224 | tf_op jit(solution)/shard_map/ppermute | solution.py:170
  15.4 1.9 %collective-permute-done.14.refs_15_.refs_7_ = bf16[16,4096]{1,0:T(8,128)(2,1)S(1)} collective-permute-done((bf16[16,4096]{1,0:T(8,128)(2,1)}, bf16[16,4096]{1,0:T(8,128)(2,1)S(1)}, u32[]{:S(2)}, u32[]{:S(2)}) %collective-permute-start.14) | collective-permute-done | bytes 131104 | tf_op jit(solution)/shard_map/ppermute | solution.py:170
  17.3 1.6 %collective-permute-start.15 = (bf16[16,4096]{1,0:T(8,128)(2,1)S(1)}, bf16[16,4096]{1,0:T(8,128)(2,1)S(1)}, u32[]{:S(2)}, u32[]{:S(2)}) collective-permute-start(bf16[16,4096]{1,0:T(8,128)(2,1)S(1)} %collective-permute-done.14.refs_15_.refs_7_), channel_id=1, source_target_pairs={{0,4},{4,8},{8,12},{12,14},{14,10},{10,6},{6,2},{2,0},{1,5},{5,9},... | collective-permute-start | bytes 393224 | tf_op jit(solution)/shard_map/ppermute | solution.py:170
  18.8 0.0 collective-permute-done.5.refs_1_
  18.9 0.0 collective-permute-start.6
  18.9 2.1 %collective-permute-done.2.refs_10_.refs_2_ = bf16[16,4096]{1,0:T(8,128)(2,1)S(1)} collective-permute-done((bf16[16,4096]{1,0:T(8,128)(2,1)S(1)}, bf16[16,4096]{1,0:T(8,128)(2,1)S(1)}, u32[]{:S(2)}, u32[]{:S(2)}) %collective-permute-start.2) | collective-permute-done | bytes 131104 | tf_op jit(solution)/shard_map/ppermute | solution.py:172
  20.9 0.0 collective-permute-start.3
  21.0 0.0 collective-permute-done.9.refs_6_
  21.0 0.0 collective-permute-done.11.refs_19_
  21.0 1.4 %collective-permute-start.13 = (bf16[16,4096]{1,0:T(8,128)(2,1)S(1)}, bf16[16,4096]{1,0:T(8,128)(2,1)S(1)}, u32[]{:S(2)}, u32[]{:S(2)}) collective-permute-start(bf16[16,4096]{1,0:T(8,128)(2,1)S(1)} %collective-permute-done.9.refs_6_), channel_id=1, source_target_pairs={{0,4},{4,8},{8,12},{12,14},{14,10},{10,6},{6,2},{2,0},{1,5},{5,9},... | collective-permute-start | bytes 393224 | tf_op jit(solution)/shard_map/ppermute | solution.py:170
  22.4 0.0 collective-permute-done.15.refs_14_.refs_6_
  22.4 1.3 %collective-permute-start.16 = (bf16[16,4096]{1,0:T(8,128)(2,1)S(1)}, bf16[16,4096]{1,0:T(8,128)(2,1)S(1)}, u32[]{:S(2)}, u32[]{:S(2)}) collective-permute-start(bf16[16,4096]{1,0:T(8,128)(2,1)S(1)} %collective-permute-done.15.refs_14_.refs_6_), channel_id=1, source_target_pairs={{0,4},{4,8},{8,12},{12,14},{14,10},{10,6},{6,2},{2,0},{1,5},{5,9},... | collective-permute-start | bytes 393224 | tf_op jit(solution)/shard_map/ppermute | solution.py:170
  23.7 0.0 collective-permute-done.6.refs_2_
  23.7 0.2 collective-permute-start.7
  23.9 2.4 %collective-permute-done.3.refs_2_.refs_11_.refs_3_ = bf16[16,4096]{1,0:T(8,128)(2,1)S(1)} collective-permute-done((bf16[16,4096]{1,0:T(8,128)(2,1)S(1)}, bf16[16,4096]{1,0:T(8,128)(2,1)S(1)}, u32[]{:S(2)}, u32[]{:S(2)}) %collective-permute-start.3) | collective-permute-done | bytes 131104 | tf_op jit(solution)/shard_map/ppermute | solution.py:172
  26.2 0.0 collective-permute-start.4
  26.2 0.1 collective-permute-done.13.refs_1_.refs_5_
  26.4 1.3 %collective-permute-start.17 = (bf16[16,4096]{1,0:T(8,128)(2,1)S(1)}, bf16[16,4096]{1,0:T(8,128)(2,1)S(1)}, u32[]{:S(2)}, u32[]{:S(2)}) collective-permute-start(bf16[16,4096]{1,0:T(8,128)(2,1)S(1)} %collective-permute-done.13.refs_1_.refs_5_), channel_id=1, source_target_pairs={{0,4},{4,8},{8,12},{12,14},{14,10},{10,6},{6,2},{2,0},{1,5},{5,9},... | collective-permute-start | bytes 393224 | tf_op jit(solution)/shard_map/ppermute | solution.py:170
  27.7 0.7 %dynamic-slice_bitcast_fusion.facts = s32[14]{0:T(128)S(1)} fusion(s32[16,14]{1,0:T(8,128)} %constant.18.clone, s32[]{:T(128)S(6)} %select_n.4), kind=kLoop, calls=%fused_computation | loop fusion | bytes 116 | tf_op jit(solution)/shard_map/jit(dynamic_index_in_dim)/squeeze | solution.py:513
  28.4 0.0 collective-permute-done.16.refs_3_.refs_13_.refs_5_
  28.4 0.8 %collective-permute-done.7.refs_0_.refs_3_ = bf16[16,4096]{1,0:T(8,128)(2,1)S(1)} collective-permute-done((bf16[16,4096]{1,0:T(8,128)(2,1)S(1)}, bf16[16,4096]{1,0:T(8,128)(2,1)S(1)}, u32[]{:S(2)}, u32[]{:S(2)}) %collective-permute-start.7) | collective-permute-done | bytes 131104 | tf_op jit(solution)/shard_map/ppermute | solution.py:172
  29.2 3.4 %fetch.1 = (bf16[2048,2048]{1,0:T(8,128)(2,1)S(1)}, f32[8,128]{1,0:T(8,128)S(1)}) custom-call(bf16[8192,2048]{1,0:T(8,128)(2,1)} %refs_9_.3, bf16[16,4096]{1,0:T(8,128)(2,1)S(1)} %collective-permute-done.7.refs_0_.refs_3_, bf16[16,4096]{1,0:T(8,128)(2,1)S(1)} %collective-permute-done.13.refs_1_.refs_5_, ...), custom_call_target="tpu_custom_call" | custom-call | bytes 16777216 | tf_op jit(solution)/shard_map/fetch/pallas_call | solution.py:230
  32.6 0.0 collective-permute-done.4.refs_12_.refs_4_
  32.7 0.0 collective-permute-done.17.refs_4_
  32.7 0.0 copy-done
  32.7 0.0 copy-done.1
  32.7 0.6 rank_part.1.a
  33.3 0.7 collective-permute-start.18
  34.0 5.6 %project_0.1 = (f32[128,2048]{1,0:T(8,128)S(1)}, bf16[1280,2048]{1,0:T(8,128)(2,1)S(1)}) custom-call(s32[14]{0:T(128)S(1)} %dynamic-slice_bitcast_fusion.facts, bf16[16,4096]{1,0:T(8,128)(2,1)S(1)} %copy-done.1, bf16[16,4096]{1,0:T(8,128)(2,1)S(1)} %collective-permute-done.5.refs_1_, bf16[16,4096]{1,0:T(8,128)(2,1)S(1)} %collective-permute-done.6.refs_2_, ...), custom_call_target="tpu_custom_call" | custom-call | flops 2147483648 | bytes 16777216 | tf_op jit(solution)/shard_map/project_0/pallas_call | solution.py:364
  39.5 0.0 collective-permute-done.18.b
  39.6 0.0 copy-start.2
  39.6 1.4 %collective-permute-start.19 = (f32[128,128]{1,0:T(8,128)S(1)}, f32[128,128]{1,0:T(8,128)S(1)}, u32[]{:S(2)}, u32[]{:S(2)}) collective-permute-start(f32[128,128]{1,0:T(8,128)S(1)} %add.10.a), channel_id=1, source_target_pairs={{0,8},{2,10},{4,12},{6,14},{9,1},{11,3},{13,5},{15,7},{16,24},{18,... | collective-permute-start | bytes 196616 | tf_op jit(solution)/shard_map/ppermute | solution.py:562
  41.0 5.3 %project_4096.1 = (f32[64,2048]{1,0:T(8,128)S(1)}, f32[64,2048]{1,0:T(8,128)S(1)}) custom-call(s32[14]{0:T(128)S(1)} %dynamic-slice_bitcast_fusion.facts, bf16[16,4096]{1,0:T(8,128)(2,1)S(1)} %copy-done, bf16[16,4096]{1,0:T(8,128)(2,1)S(1)} %collective-permute-done.1.refs_9_.refs_1_, bf16[16,4096]{1,0:T(8,128)(2,1)S(1)} %collective-permute-done.2.refs_10_.refs_2_, ...), custom_call_target="tpu_custom_call" | custom-call | flops 2147483648 | bytes 16777216 | tf_op jit(solution)/shard_map/project_4096/pallas_call | solution.py:364
  46.3 2.1 %collective-permute-done.19.b = f32[128,128]{1,0:T(8,128)S(1)} collective-permute-done((f32[128,128]{1,0:T(8,128)S(1)}, f32[128,128]{1,0:T(8,128)S(1)}, u32[]{:S(2)}, u32[]{:S(2)}) %collective-permute-start.19) | collective-permute-done | bytes 65568 | tf_op jit(solution)/shard_map/ppermute | solution.py:562
  48.4 4.6 %collective-permute-start.20 = (f32[64,2048]{1,0:T(8,128)S(1)}, f32[64,2048]{1,0:T(8,128)S(1)}, u32[]{:S(2)}, u32[]{:S(2)}) collective-permute-start(f32[64,2048]{1,0:T(8,128)S(1)} %get-tuple-element.54), channel_id=1, source_target_pairs={{0,1},{1,0},{2,3},{3,2},{4,5},{5,4},{6,7},{7,6},{8,9},{9,8},{10,11... | collective-permute-start | bytes 1572872 | tf_op jit(solution)/shard_map/ppermute | solution.py:568
  53.0 0.6 split.1
  53.5 0.1 collective-permute-start.21
  53.6 1.2 %collective-permute-done.21.ranked_received = f32[64,128]{1,0:T(8,128)S(1)} collective-permute-done((f32[64,128]{1,0:T(8,128)S(1)}, f32[64,128]{1,0:T(8,128)S(1)}, u32[]{:S(2)}, u32[]{:S(2)}) %collective-permute-start.21) | collective-permute-done | bytes 32800 | tf_op jit(solution)/shard_map/ppermute | solution.py:567
  54.8 0.0 collective-permute-done.20.received
  54.8 1.0 %finish.1 = (bf16[4,4,2048]{2,1,0:T(4,128)(2,1)S(1)}, bf16[4,4,2048]{2,1,0:T(4,128)(2,1)S(1)}, bf16[4,4,2048]{2,1,0:T(4,128)(2,1)S(1)}, bf16[4,4,2048]{2,1,0:T(4,128)(2,1)S(1)}) custom-call(s32[14]{0:T(128)S(1)} %dynamic-slice_bitcast_fusion.facts, f32[64,2048]{1,0:T(8,128)S(1)} %get-tuple-element.53.keep, f32[64,2048]{1,0:T(8,128)S(1)} %collective-permute-done.20.received, ...), custom_call_target="tpu_custom_call" | custom-call | tf_op jit(solution)/shard_map/finish/pallas_call | solution.py:453
  55.9 1.9 %collective-permute-start.22 = (bf16[4,4,2048]{2,1,0:T(4,128)(2,1)S(1)}, bf16[4,4,2048]{2,1,0:T(4,128)(2,1)S(1)}, u32[]{:S(2)}, u32[]{:S(2)}) collective-permute-start(bf16[4,4,2048]{2,1,0:T(4,128)(2,1)S(1)} %get-tuple-element.59), channel_id=1, source_target_pairs={{0,0},{1,8},{2,2},{3,10},{4,4},{5,12},{6,6},{7,14},{8,9},{9,1},{10... | collective-permute-start | bytes 196616 | tf_op jit(solution)/shard_map/ppermute | solution.py:579
  57.8 1.3 %collective-permute-start.23 = (bf16[4,4,2048]{2,1,0:T(4,128)(2,1)S(1)}, bf16[4,4,2048]{2,1,0:T(4,128)(2,1)S(1)}, u32[]{:S(2)}, u32[]{:S(2)}) collective-permute-start(bf16[4,4,2048]{2,1,0:T(4,128)(2,1)S(1)} %get-tuple-element.60), channel_id=1, source_target_pairs={{0,2},{1,10},{2,0},{3,8},{4,6},{5,14},{6,4},{7,12},{8,11},{9,3},{1... | collective-permute-start | bytes 196616 | tf_op jit(solution)/shard_map/ppermute | solution.py:579
  59.1 0.2 collective-permute-start.24
  59.4 2.9 %collective-permute-start.25 = (bf16[4,4,2048]{2,1,0:T(4,128)(2,1)S(1)}, bf16[4,4,2048]{2,1,0:T(4,128)(2,1)S(1)}, u32[]{:S(2)}, u32[]{:S(2)}) collective-permute-start(bf16[4,4,2048]{2,1,0:T(4,128)(2,1)S(1)} %get-tuple-element.62), channel_id=1, source_target_pairs={{0,14},{1,6},{2,12},{3,4},{4,10},{5,2},{6,8},{7,0},{8,7},{9,15},{1... | collective-permute-start | bytes 196616 | tf_op jit(solution)/shard_map/ppermute | solution.py:579
  62.2 0.0 collective-permute-done.22.refs_0_
  62.2 5.2 %collective-permute-done.23.refs_1_ = bf16[4,4,2048]{2,1,0:T(4,128)(2,1)S(1)} collective-permute-done((bf16[4,4,2048]{2,1,0:T(4,128)(2,1)S(1)}, bf16[4,4,2048]{2,1,0:T(4,128)(2,1)S(1)}, u32[]{:S(2)}, u32[]{:S(2)}) %collective-permute-start.23) | collective-permute-done | bytes 65568 | tf_op jit(solution)/shard_map/ppermute | solution.py:579
  67.5 0.0 collective-permute-done.24.refs_2_
  67.5 0.0 collective-permute-done.25.refs_3_
  67.5 1.3 %place.1 = bf16[4,4,8192]{2,1,0:T(4,128)(2,1)} custom-call(s32[14]{0:T(128)S(1)} %dynamic-slice_bitcast_fusion.facts, bf16[4,4,2048]{2,1,0:T(4,128)(2,1)S(1)} %collective-permute-done.22.refs_0_, bf16[4,4,2048]{2,1,0:T(4,128)(2,1)S(1)} %collective-permute-done.23.refs_1_, bf16[4,4,2048]{2,1,0:T(4,128)(2,1)S(1)} %collective-permute-done.24.refs_2_, ...), custom_call_target="tpu_custom_call" | custom-call | tf_op jit(solution)/shard_map/place/pallas_call | solution.py:481
  (6 shorter events, 0.0 us)
Async XLA Ops:
  0.0 9.1 %collective-permute-start = (bf16[64,2048]{1,0:T(8,128)(2,1)}, bf16[64,2048]{1,0:T(8,128)(2,1)S(1)}, u32[]{:S(2)}, u32[]{:S(2)}) collective-permute-start(bf16[64,2048]{1,0:T(8,128)(2,1)} %bitcast.7), channel_id=1, source_target_pairs={{0,2},{2,0},{4,6},{6,4},{8,10},{10,8},{12,14},{14,12},{1,3},{3,1},... | collective-permute-start | bytes 786440 | tf_op jit(solution)/shard_map/ppermute | solution.py:521
  2.1 9.6 %collective-permute-start.10 = (bf16[64,2048]{1,0:T(8,128)(2,1)}, bf16[64,2048]{1,0:T(8,128)(2,1)S(1)}, u32[]{:S(2)}, u32[]{:S(2)}) collective-permute-start(bf16[64,2048]{1,0:T(8,128)(2,1)} %bitcast.8), channel_id=1, source_target_pairs={{0,1},{1,0},{2,3},{3,2},{4,5},{5,4},{6,7},{7,6},{8,9},{9,8},{10,11... | collective-permute-start | bytes 786440 | tf_op jit(solution)/shard_map/ppermute | solution.py:536
  3.0 10.1 %collective-permute-start.12 = (bf16[64,2048]{1,0:T(8,128)(2,1)}, bf16[64,2048]{1,0:T(8,128)(2,1)S(1)}, u32[]{:S(2)}, u32[]{:S(2)}) collective-permute-start(bf16[64,2048]{1,0:T(8,128)(2,1)} %own.1), channel_id=1, source_target_pairs={{0,1},{1,0},{2,3},{3,2},{4,5},{5,4},{6,7},{7,6},{8,9},{9,8},{10,11... | collective-permute-start | bytes 786440 | tf_op jit(solution)/shard_map/ppermute | solution.py:536
  9.1 4.8 %collective-permute-start.1 = (bf16[16,4096]{1,0:T(8,128)(2,1)}, bf16[16,4096]{1,0:T(8,128)(2,1)S(1)}, u32[]{:S(2)}, u32[]{:S(2)}) collective-permute-start(bf16[16,4096]{1,0:T(8,128)(2,1)} %get-tuple-element.36.refs_8_.refs_0_), channel_id=1, source_target_pairs={{4,0},{8,4},{12,8},{14,12},{10,14},{6,10},{2,6},{0,2},{5,1},{9,5},... | collective-permute-start | bytes 393224 | tf_op jit(solution)/shard_map/ppermute | solution.py:172
  9.5 5.1 %collective-permute-start.8 = (bf16[16,4096]{1,0:T(8,128)(2,1)}, bf16[16,4096]{1,0:T(8,128)(2,1)S(1)}, u32[]{:S(2)}, u32[]{:S(2)}) collective-permute-start(bf16[16,4096]{1,0:T(8,128)(2,1)} %get-tuple-element.37.refs_0_), channel_id=1, source_target_pairs={{0,4},{4,8},{8,12},{12,14},{14,10},{10,6},{6,2},{2,0},{1,5},{5,9},... | collective-permute-start | bytes 393224 | tf_op jit(solution)/shard_map/ppermute | solution.py:170
  10.6 10.4 %collective-permute-start.11 = (bf16[64,2048]{1,0:T(8,128)(2,1)S(1)}, bf16[64,2048]{1,0:T(8,128)(2,1)S(1)}, u32[]{:S(2)}, u32[]{:S(2)}) collective-permute-start(bf16[64,2048]{1,0:T(8,128)(2,1)S(1)} %collective-permute-done.refs_17_), channel_id=1, source_target_pairs={{0,1},{1,0},{2,3},{3,2},{4,5},{5,4},{6,7},{7,6},{8,9},{9,8},{10,11... | collective-permute-start | bytes 786440 | tf_op jit(solution)/shard_map/ppermute | solution.py:536
  11.7 5.6 %collective-permute-start.14 = (bf16[16,4096]{1,0:T(8,128)(2,1)}, bf16[16,4096]{1,0:T(8,128)(2,1)S(1)}, u32[]{:S(2)}, u32[]{:S(2)}) collective-permute-start(bf16[16,4096]{1,0:T(8,128)(2,1)} %get-tuple-element.36.refs_8_.refs_0_), channel_id=1, source_target_pairs={{0,4},{4,8},{8,12},{12,14},{14,10},{10,6},{6,2},{2,0},{1,5},{5,9},... | collective-permute-start | bytes 393224 | tf_op jit(solution)/shard_map/ppermute | solution.py:170
  13.1 5.8 %collective-permute-start.5 = (bf16[16,4096]{1,0:T(8,128)(2,1)}, bf16[16,4096]{1,0:T(8,128)(2,1)S(1)}, u32[]{:S(2)}, u32[]{:S(2)}) collective-permute-start(bf16[16,4096]{1,0:T(8,128)(2,1)} %get-tuple-element.37.refs_0_), channel_id=1, source_target_pairs={{4,0},{8,4},{12,8},{14,12},{10,14},{6,10},{2,6},{0,2},{5,1},{9,5},... | collective-permute-start | bytes 393224 | tf_op jit(solution)/shard_map/ppermute | solution.py:172
  13.9 7.0 %collective-permute-start.2 = (bf16[16,4096]{1,0:T(8,128)(2,1)S(1)}, bf16[16,4096]{1,0:T(8,128)(2,1)S(1)}, u32[]{:S(2)}, u32[]{:S(2)}) collective-permute-start(bf16[16,4096]{1,0:T(8,128)(2,1)S(1)} %collective-permute-done.1.refs_9_.refs_1_), channel_id=1, source_target_pairs={{4,0},{8,4},{12,8},{14,12},{10,14},{6,10},{2,6},{0,2},{5,1},{9,5},... | collective-permute-start | bytes 393224 | tf_op jit(solution)/shard_map/ppermute | solution.py:172
  14.5 6.4 %collective-permute-start.9 = (bf16[16,4096]{1,0:T(8,128)(2,1)S(1)}, bf16[16,4096]{1,0:T(8,128)(2,1)S(1)}, u32[]{:S(2)}, u32[]{:S(2)}) collective-permute-start(bf16[16,4096]{1,0:T(8,128)(2,1)S(1)} %collective-permute-done.8.refs_7_), channel_id=1, source_target_pairs={{0,4},{4,8},{8,12},{12,14},{14,10},{10,6},{6,2},{2,0},{1,5},{5,9},... | collective-permute-start | bytes 393224 | tf_op jit(solution)/shard_map/ppermute | solution.py:170
  17.3 5.1 %collective-permute-start.15 = (bf16[16,4096]{1,0:T(8,128)(2,1)S(1)}, bf16[16,4096]{1,0:T(8,128)(2,1)S(1)}, u32[]{:S(2)}, u32[]{:S(2)}) collective-permute-start(bf16[16,4096]{1,0:T(8,128)(2,1)S(1)} %collective-permute-done.14.refs_15_.refs_7_), channel_id=1, source_target_pairs={{0,4},{4,8},{8,12},{12,14},{14,10},{10,6},{6,2},{2,0},{1,5},{5,9},... | collective-permute-start | bytes 393224 | tf_op jit(solution)/shard_map/ppermute | solution.py:170
  18.9 4.8 %collective-permute-start.6 = (bf16[16,4096]{1,0:T(8,128)(2,1)S(1)}, bf16[16,4096]{1,0:T(8,128)(2,1)S(1)}, u32[]{:S(2)}, u32[]{:S(2)}) collective-permute-start(bf16[16,4096]{1,0:T(8,128)(2,1)S(1)} %collective-permute-done.5.refs_1_), channel_id=1, source_target_pairs={{4,0},{8,4},{12,8},{14,12},{10,14},{6,10},{2,6},{0,2},{5,1},{9,5},... | collective-permute-start | bytes 393224 | tf_op jit(solution)/shard_map/ppermute | solution.py:172
  20.9 5.3 %collective-permute-start.3 = (bf16[16,4096]{1,0:T(8,128)(2,1)S(1)}, bf16[16,4096]{1,0:T(8,128)(2,1)S(1)}, u32[]{:S(2)}, u32[]{:S(2)}) collective-permute-start(bf16[16,4096]{1,0:T(8,128)(2,1)S(1)} %collective-permute-done.2.refs_10_.refs_2_), channel_id=1, source_target_pairs={{4,0},{8,4},{12,8},{14,12},{10,14},{6,10},{2,6},{0,2},{5,1},{9,5},... | collective-permute-start | bytes 393224 | tf_op jit(solution)/shard_map/ppermute | solution.py:172
  21.0 5.4 %collective-permute-start.13 = (bf16[16,4096]{1,0:T(8,128)(2,1)S(1)}, bf16[16,4096]{1,0:T(8,128)(2,1)S(1)}, u32[]{:S(2)}, u32[]{:S(2)}) collective-permute-start(bf16[16,4096]{1,0:T(8,128)(2,1)S(1)} %collective-permute-done.9.refs_6_), channel_id=1, source_target_pairs={{0,4},{4,8},{8,12},{12,14},{14,10},{10,6},{6,2},{2,0},{1,5},{5,9},... | collective-permute-start | bytes 393224 | tf_op jit(solution)/shard_map/ppermute | solution.py:170
  22.4 6.0 %collective-permute-start.16 = (bf16[16,4096]{1,0:T(8,128)(2,1)S(1)}, bf16[16,4096]{1,0:T(8,128)(2,1)S(1)}, u32[]{:S(2)}, u32[]{:S(2)}) collective-permute-start(bf16[16,4096]{1,0:T(8,128)(2,1)S(1)} %collective-permute-done.15.refs_14_.refs_6_), channel_id=1, source_target_pairs={{0,4},{4,8},{8,12},{12,14},{14,10},{10,6},{6,2},{2,0},{1,5},{5,9},... | collective-permute-start | bytes 393224 | tf_op jit(solution)/shard_map/ppermute | solution.py:170
  23.7 5.5 %collective-permute-start.7 = (bf16[16,4096]{1,0:T(8,128)(2,1)S(1)}, bf16[16,4096]{1,0:T(8,128)(2,1)S(1)}, u32[]{:S(2)}, u32[]{:S(2)}) collective-permute-start(bf16[16,4096]{1,0:T(8,128)(2,1)S(1)} %collective-permute-done.6.refs_2_), channel_id=1, source_target_pairs={{4,0},{8,4},{12,8},{14,12},{10,14},{6,10},{2,6},{0,2},{5,1},{9,5},... | collective-permute-start | bytes 393224 | tf_op jit(solution)/shard_map/ppermute | solution.py:172
  26.2 6.4 %collective-permute-start.4 = (bf16[16,4096]{1,0:T(8,128)(2,1)S(1)}, bf16[16,4096]{1,0:T(8,128)(2,1)S(1)}, u32[]{:S(2)}, u32[]{:S(2)}) collective-permute-start(bf16[16,4096]{1,0:T(8,128)(2,1)S(1)} %collective-permute-done.3.refs_2_.refs_11_.refs_3_), channel_id=1, source_target_pairs={{4,0},{8,4},{12,8},{14,12},{10,14},{6,10},{2,6},{0,2},{5,1},{9,5},... | collective-permute-start | bytes 393224 | tf_op jit(solution)/shard_map/ppermute | solution.py:172
  26.4 6.3 %collective-permute-start.17 = (bf16[16,4096]{1,0:T(8,128)(2,1)S(1)}, bf16[16,4096]{1,0:T(8,128)(2,1)S(1)}, u32[]{:S(2)}, u32[]{:S(2)}) collective-permute-start(bf16[16,4096]{1,0:T(8,128)(2,1)S(1)} %collective-permute-done.13.refs_1_.refs_5_), channel_id=1, source_target_pairs={{0,4},{4,8},{8,12},{12,14},{14,10},{10,6},{6,2},{2,0},{1,5},{5,9},... | collective-permute-start | bytes 393224 | tf_op jit(solution)/shard_map/ppermute | solution.py:170
  28.4 4.3 %copy-start = (bf16[16,4096]{1,0:T(8,128)(2,1)S(1)}, bf16[16,4096]{1,0:T(8,128)(2,1)}, u32[]{:S(2)}) copy-start(bf16[16,4096]{1,0:T(8,128)(2,1)} %get-tuple-element.36.refs_8_.refs_0_) | copy-start | bytes 393220
  28.4 4.3 %copy-start.1 = (bf16[16,4096]{1,0:T(8,128)(2,1)S(1)}, bf16[16,4096]{1,0:T(8,128)(2,1)}, u32[]{:S(2)}) copy-start(bf16[16,4096]{1,0:T(8,128)(2,1)} %get-tuple-element.37.refs_0_) | copy-start | bytes 393220
  28.4 4.3 %copy-start.3 = (bf16[2048,64]{0,1:T(8,128)(2,1)S(1)}, bf16[2048,64]{0,1:T(8,128)(2,1)}, u32[]{:S(2)}) copy-start(bf16[2048,64]{0,1:T(8,128)(2,1)} %param.17) | copy-start | bytes 786436
  33.3 6.2 %collective-permute-start.18 = (f32[128,128]{1,0:T(8,128)S(1)}, f32[128,128]{1,0:T(8,128)S(1)}, u32[]{:S(2)}, u32[]{:S(2)}) collective-permute-start(f32[128,128]{1,0:T(8,128)S(1)} %rank_part.1.a), channel_id=1, source_target_pairs={{0,4},{2,6},{4,0},{6,2},{9,13},{11,15},{13,9},{15,11},{16,20},{18,... | collective-permute-start | bytes 196616 | tf_op jit(solution)/shard_map/ppermute | solution.py:556
  39.6 15.3 %copy-start.2 = (bf16[64,2048]{1,0:T(8,128)(2,1)S(1)}, bf16[64,2048]{1,0:T(8,128)(2,1)}, u32[]{:S(2)}) copy-start(bf16[64,2048]{1,0:T(8,128)(2,1)} %own.1) | copy-start | bytes 786436
  39.6 8.9 %collective-permute-start.19 = (f32[128,128]{1,0:T(8,128)S(1)}, f32[128,128]{1,0:T(8,128)S(1)}, u32[]{:S(2)}, u32[]{:S(2)}) collective-permute-start(f32[128,128]{1,0:T(8,128)S(1)} %add.10.a), channel_id=1, source_target_pairs={{0,8},{2,10},{4,12},{6,14},{9,1},{11,3},{13,5},{15,7},{16,24},{18,... | collective-permute-start | bytes 196616 | tf_op jit(solution)/shard_map/ppermute | solution.py:562
  48.4 6.4 %collective-permute-start.20 = (f32[64,2048]{1,0:T(8,128)S(1)}, f32[64,2048]{1,0:T(8,128)S(1)}, u32[]{:S(2)}, u32[]{:S(2)}) collective-permute-start(f32[64,2048]{1,0:T(8,128)S(1)} %get-tuple-element.54), channel_id=1, source_target_pairs={{0,1},{1,0},{2,3},{3,2},{4,5},{5,4},{6,7},{7,6},{8,9},{9,8},{10,11... | collective-permute-start | bytes 1572872 | tf_op jit(solution)/shard_map/ppermute | solution.py:568
  53.5 1.3 %collective-permute-start.21 = (f32[64,128]{1,0:T(8,128)S(1)}, f32[64,128]{1,0:T(8,128)S(1)}, u32[]{:S(2)}, u32[]{:S(2)}) collective-permute-start(f32[64,128]{1,0:T(8,128)S(1)} %get-tuple-element.57), channel_id=1, source_target_pairs={{0,1},{1,0},{2,3},{3,2},{4,5},{5,4},{6,7},{7,6},{8,9},{9,8},{10,11... | collective-permute-start | bytes 98312 | tf_op jit(solution)/shard_map/ppermute | solution.py:567
  55.9 6.4 %collective-permute-start.22 = (bf16[4,4,2048]{2,1,0:T(4,128)(2,1)S(1)}, bf16[4,4,2048]{2,1,0:T(4,128)(2,1)S(1)}, u32[]{:S(2)}, u32[]{:S(2)}) collective-permute-start(bf16[4,4,2048]{2,1,0:T(4,128)(2,1)S(1)} %get-tuple-element.59), channel_id=1, source_target_pairs={{0,0},{1,8},{2,2},{3,10},{4,4},{5,12},{6,6},{7,14},{8,9},{9,1},{10... | collective-permute-start | bytes 196616 | tf_op jit(solution)/shard_map/ppermute | solution.py:579
  57.8 9.7 %collective-permute-start.23 = (bf16[4,4,2048]{2,1,0:T(4,128)(2,1)S(1)}, bf16[4,4,2048]{2,1,0:T(4,128)(2,1)S(1)}, u32[]{:S(2)}, u32[]{:S(2)}) collective-permute-start(bf16[4,4,2048]{2,1,0:T(4,128)(2,1)S(1)} %get-tuple-element.60), channel_id=1, source_target_pairs={{0,2},{1,10},{2,0},{3,8},{4,6},{5,14},{6,4},{7,12},{8,11},{9,3},{1... | collective-permute-start | bytes 196616 | tf_op jit(solution)/shard_map/ppermute | solution.py:579
  59.1 8.3 %collective-permute-start.24 = (bf16[4,4,2048]{2,1,0:T(4,128)(2,1)S(1)}, bf16[4,4,2048]{2,1,0:T(4,128)(2,1)S(1)}, u32[]{:S(2)}, u32[]{:S(2)}) collective-permute-start(bf16[4,4,2048]{2,1,0:T(4,128)(2,1)S(1)} %get-tuple-element.61), channel_id=1, source_target_pairs={{0,12},{1,4},{2,14},{3,6},{4,8},{5,0},{6,10},{7,2},{8,5},{9,13},{1... | collective-permute-start | bytes 196616 | tf_op jit(solution)/shard_map/ppermute | solution.py:579
  59.4 8.1 %collective-permute-start.25 = (bf16[4,4,2048]{2,1,0:T(4,128)(2,1)S(1)}, bf16[4,4,2048]{2,1,0:T(4,128)(2,1)S(1)}, u32[]{:S(2)}, u32[]{:S(2)}) collective-permute-start(bf16[4,4,2048]{2,1,0:T(4,128)(2,1)S(1)} %get-tuple-element.62), channel_id=1, source_target_pairs={{0,14},{1,6},{2,12},{3,4},{4,10},{5,2},{6,8},{7,0},{8,7},{9,15},{1... | collective-permute-start | bytes 196616 | tf_op jit(solution)/shard_map/ppermute | solution.py:579
